TPU v7x, 256 devices: a whole 4x4x8 slice. The times are simulated.
256 devices in a mesh: frag: 32 (over z, x), band: 8 (over y, core).
Axes of the slice: x: 4, y: 4, z: 8, core: 2. Of those that a mesh axis runs over, the one named last changes fastest.
Arguments:
- wave_init: bfloat16 [32, 8, 64, 64, 128], P('frag', 'band'), may hold values from -6 to 6
- potential: float32 [1024, 256, 128], P('frag', 'band'), may hold values from -4 to 4
- fragment_order: int32 [32, 1], P('frag'), may hold values from 0 to 31, as said below
Outputs:
- density: float32 [1024, 256, 128], P('frag', 'band')
Inputs may be any that keep to these rules, and one draw needn't show every extreme that they name: `fragment_order`: every group holds at least one code q with (q % 4) // 2 == 1; a group may hold the same code in two slots.
All inputs are finite; a program needn't handle non-finite values.
Results may differ from a plain program's by a relative error of at most 0.0003.
Values sent between devices are 32-bit elements; how exact they have to be, the bound alone decides.
No kernel may reach another device: no remote copies, remote signals or barrier semaphores. Data moves between devices by JAX's collectives and lax.ppermute only.
A program may use at most 64 MiB of HBM per device.

v0:
```python
import jax
import jax.numpy as jnp
from jax import lax
from jax.sharding import PartitionSpec as P

STEP_LENGTH = 0.1
EPSILON = 1e-06


def from_behind(block, axis, distance):
    devices = range(lax.axis_size(axis))
    route = [((i - distance) % len(devices), i) for i in devices]
    return lax.ppermute(block, axis, route)


def kinetic(extent, live_length):
    positions = jnp.arange(live_length, dtype=jnp.int32)
    angles = (positions[:, None] * positions[None, :] % live_length).astype(jnp.float32) * (
        2.0 * jnp.pi / live_length
    )
    folded = jnp.minimum(positions, live_length - positions).astype(jnp.float32)
    weight = (2.0 * jnp.pi * folded / live_length) ** 2
    cosine = jnp.cos(angles)
    sine = jnp.sin(angles)
    matrix = jnp.dot(cosine * weight[None, :], cosine.T, precision=lax.Precision.HIGHEST)
    matrix = matrix + jnp.dot(sine * weight[None, :], sine.T, precision=lax.Precision.HIGHEST)
    matrix = matrix / live_length
    return jnp.pad(matrix, ((0, extent - live_length), (0, extent - live_length)))


def geometry(slot_ids, columns, box_depth, box_width, length):
    piece_column = slot_ids // 4
    z_double = slot_ids % 4 // 2
    y_double = slot_ids % 2
    column_ids = jnp.arange(columns, dtype=jnp.int32)
    lower_pick = (piece_column[:, None] == column_ids[None, :]).astype(jnp.float32)
    upper_pick = (((piece_column + 1) % columns)[:, None] == column_ids[None, :]).astype(
        jnp.float32
    )
    z_lines = jnp.arange(box_depth, dtype=jnp.int32)
    y_lines = jnp.arange(box_width, dtype=jnp.int32)
    live_z = z_lines[None, :] < (box_depth // 2 * (1 + z_double))[:, None]
    live_y = y_lines[None, :] < (box_width // 2 * (1 + y_double))[:, None]
    live_mask = (live_z[:, :, None] & live_y[:, None, :]).astype(jnp.float32)[..., None]
    box_cells = (
        box_depth // 2 * (1 + z_double) * (box_width // 2) * (1 + y_double) * length
    ).astype(jnp.float32)
    fragment_sign = jnp.where(z_double == y_double, 1.0, -1.0).astype(jnp.float32)
    z_ops = jnp.where(
        (z_double == 1)[:, None, None],
        kinetic(box_depth, box_depth)[None],
        kinetic(box_depth, box_depth // 2)[None],
    )
    y_ops = jnp.where(
        (y_double == 1)[:, None, None],
        kinetic(box_width, box_width)[None],
        kinetic(box_width, box_width // 2)[None],
    )
    return (lower_pick, upper_pick, live_mask, box_cells, fragment_sign, z_ops, y_ops)


def hamiltonian(states, box_potential, live_mask, x_op, z_ops, y_ops):
    spectral = jnp.einsum("sbzyx,xw->sbzyw", states, x_op, precision=lax.Precision.HIGHEST)
    spectral = spectral + jnp.einsum(
        "sbzyx,szw->sbwyx", states, z_ops, precision=lax.Precision.HIGHEST
    )
    spectral = spectral + jnp.einsum(
        "sbzyx,syw->sbzwx", states, y_ops, precision=lax.Precision.HIGHEST
    )
    applied = 0.5 * spectral + box_potential[:, None] * states
    return applied * live_mask[:, None]


def gradient_step(states, box_potential, live_mask, box_cells, x_op, z_ops, y_ops):
    applied = hamiltonian(states, box_potential, live_mask, x_op, z_ops, y_ops)
    intersection = jnp.sum(states * states, axis=(2, 3, 4)) + EPSILON
    rayleigh = jnp.sum(states * applied, axis=(2, 3, 4)) / intersection
    stepped = states - STEP_LENGTH * (applied - rayleigh[:, :, None, None, None] * states)
    weight = jnp.sum(stepped * stepped, axis=(2, 3, 4)) + EPSILON
    return stepped * jnp.sqrt(box_cells[:, None] / weight)[:, :, None, None, None]


def from_region(region, lower_pick, upper_pick, columns, piece_width, length):
    region_cols = region.reshape(region.shape[0], columns, piece_width, length)
    lower_box = jnp.einsum(
        "sp,zpqx->szqx", lower_pick, region_cols, precision=lax.Precision.HIGHEST
    )
    upper_box = jnp.einsum(
        "sp,zpqx->szqx", upper_pick, region_cols, precision=lax.Precision.HIGHEST
    )
    return jnp.concatenate([lower_box, upper_box], axis=2)


def body(wave_init, potential, fragment_order):
    slot_count, band_local, box_depth, box_width, length = wave_init.shape
    slab_depth = box_depth // 2
    piece_width = box_width // 2
    columns = lax.axis_size("band")
    grid_width = piece_width * columns
    total_bands = band_local * columns
    slot_ids = fragment_order[0]
    lower_pick, upper_pick, live_mask, box_cells, fragment_sign, z_ops, y_ops = geometry(
        slot_ids, columns, box_depth, box_width, length
    )
    x_op = kinetic(length, length)
    following = from_behind(potential, "frag", -1)
    region = lax.all_gather(
        jnp.concatenate([potential, following], axis=0), "band", axis=1, tiled=True
    )
    box_potential = from_region(region, lower_pick, upper_pick, columns, piece_width, length)
    states = wave_init.astype(jnp.float32) * live_mask[:, None]
    for repeat in range(2):
        states = gradient_step(states, box_potential, live_mask, box_cells, x_op, z_ops, y_ops)
    box_density = (
        fragment_sign[:, None, None, None] * jnp.sum(states * states, axis=1) / total_bands
    )
    placed = jnp.einsum(
        "sp,szqx->zpqx",
        lower_pick,
        box_density[:, :, :piece_width],
        precision=lax.Precision.HIGHEST,
    )
    placed = placed + jnp.einsum(
        "sp,szqx->zpqx",
        upper_pick,
        box_density[:, :, piece_width:],
        precision=lax.Precision.HIGHEST,
    )
    placed = placed.reshape(2 * slab_depth, grid_width, length)
    partial_value = lax.psum_scatter(placed, "band", scatter_dimension=1, tiled=True)
    arrived = from_behind(partial_value[slab_depth:], "frag", 1)
    density = partial_value[:slab_depth] + arrived
    return density


def solution(mesh):
    placed = (P("frag", "band", None, None, None), P("frag", "band", None), P("frag", None))
    return jax.shard_map(
        body, mesh=mesh, in_specs=placed, out_specs=P("frag", "band", None), check_vma=False
    )
```

profile of v0, /device:TPU:24, one launch (start us, length us, event | category | flops | bytes accessed | tf_op | source)
XLA Modules:
  0.0 215.1 jit_solution(14401478401092014447)
XLA Ops:
  6.5 0.0 all-gather.2.cloned.1.call-start
  6.5 8.1 %collective-permute-start = (f32[32,32,128]{2,1,0:T(8,128)}, f32[32,32,128]{2,1,0:T(8,128)S(1)}, u32[]{:S(2)}, u32[]{:S(2)}) collective-permute-start(f32[32,32,128]{2,1,0:T(8,128)} %param.4), channel_id=1, source_target_pairs={{8,0},{16,8},{24,16},{32,24},{40,32},{48,40},{56,48},{64,56},{72,6... | collective-permute-start | bytes 1572872 | tf_op jit(solution)/shard_map/ppermute | solution.py:13
  14.6 11.5 %collective-permute-done = f32[32,32,128]{2,1,0:T(8,128)S(1)} collective-permute-done((f32[32,32,128]{2,1,0:T(8,128)}, f32[32,32,128]{2,1,0:T(8,128)S(1)}, u32[]{:S(2)}, u32[]{:S(2)}) %collective-permute-start) | collective-permute-done | bytes 524320 | tf_op jit(solution)/shard_map/ppermute | solution.py:13
  26.1 2.1 pad_maximum_fusion
  28.2 0.0 copy-start.1
  28.2 0.0 all-gather.2.cloned.1.call-update
  28.2 0.0 reduce-scatter.2.cloned.1.call-start
  29.1 0.5 fusion.24
  29.6 0.5 fusion.16
  30.1 0.2 fusion.52
  30.4 0.3 fusion.35
  30.7 0.2 fusion.18
  30.9 0.1 and_convert_fusion
  31.0 0.3 fusion.17
  31.4 0.0 copy-done.1
  31.4 0.6 fusion.14
  32.0 1.8 fusion.20
  33.8 4.4 %fusion.12 = f32[64,64,128]{2,0,1:T(8,128)} fusion(f32[64,64,128]{2,1,0:T(8,128)S(1)} %fusion.14, f32[64,64]{1,0:T(8,128)S(1)} %fusion.17, f32[32,32]{1,0:T(8,128)S(1)} %fusion.18, pred[]{:T(512)} %bitcast.9), kind=kOutput, calls=%fused_computation.18 | convolution fusion | flops 402657280 | bytes 4214785 | tf_op jit(solution)/shard_map/sbzyx,szw->sbwyx/dot_general | solution.py:64
  38.3 39.4 %all-gather.2.cloned.1.call-done = f32[64,256,128]{2,1,0:T(8,128)} async-done(((f32[64,32,128]{2,1,0:T(8,128)}), f32[64,256,128]{2,1,0:T(8,128)}) %all-gather.2.cloned.1.call-update) | async-done | bytes 8388624 | tf_op jit(solution)/shard_map/all_gather | solution.py:107
  77.6 12.2 %fusion = f32[1,64,32,128]{3,0,2,1:T(1,128)S(1)} fusion(f32[64,8,32,128]{3,2,1,0:T(8,128)} %bitcast.111, s32[]{:T(128)} %bitcast.23), kind=kOutput, calls=%fused_computation.1 | convolution fusion | flops 25165832 | bytes 9437188 | tf_op jit(solution)/shard_map/sp,zpqx->szqx/dot_general | solution.py:88
  89.8 0.0 copy-done
  89.8 0.0 copy-start.2
  89.8 0.0 copy-start.6
  89.8 7.4 %fusion.2 = f32[1,64,32,128]{3,0,2,1:T(1,128)S(1)} fusion(f32[64,8,32,128]{3,2,1,0:T(8,128)S(1)} %bitcast.112, s32[]{:T(128)} %bitcast.16), kind=kOutput, calls=%fused_computation.3 | convolution fusion | flops 25165832 | bytes 9437188 | tf_op jit(solution)/shard_map/sp,zpqx->szqx/dot_general | solution.py:85
  97.2 0.0 copy-start.4
  97.2 0.0 copy-done.2
  97.2 0.0 copy-done.6
  97.2 6.8 %multiply_reduce_fusion.4 = (f32[]{:T(128)}, f32[]{:T(128)}, f32[1,1,64,64,128]{4,3,2,1,0:T(8,128)}) fusion(bf16[1,1,64,64,128]{4,3,2,1,0:T(8,128)(2,1)S(1)} %copy-done.1, f32[64,64]{1,0:T(8,128)S(1)} %and_convert_fusion, f32[1,64,32,128]{3,2,1,0:T(8,128)S(1)} %bitcast.114, f32[1,64,32,128]{3,2,1,0:T(8,128)S(1)} %bitcast.116, f32[64,64]{1,0:T(8,128)S(1)} %fusion.17, ...), kind=kOutput, calls=%fused_computation.27 | convolution fusion | flops 410521600 | bytes 9474057 | tf_op jit(solution)/shard_map/sbzyx,syw->sbzwx/dot_general | solution.py:67
  104.1 0.0 copy-done.4
  105.3 2.5 %multiply_reduce_fusion.3 = (f32[]{:T(128)}, f32[1,1,64,64,128]{4,3,2,1,0:T(8,128)S(1)}) fusion(f32[1,1,64,64,128]{4,3,2,1,0:T(8,128)} %get-tuple-element.13, f32[]{:T(128)S(6)} %div.94, f32[64,64]{1,0:T(8,128)S(1)} %and_convert_fusion, bf16[1,1,64,64,128]{4,3,2,1,0:T(8,128)(2,1)S(1)} %copy-done.1), kind=kLoop, calls=%fused_computation.25 | loop fusion | flops 4194303 | bytes 5259272 | tf_op jit(solution)/shard_map/reduce_sum | solution.py:79
  108.6 1.8 fusion.22
  110.4 0.2 multiply_bitcast_fusion.1
  110.6 0.0 copy-start.3
  110.6 0.0 copy-start.5
  110.7 3.0 %fusion.10 = f32[64,64,128]{2,0,1:T(8,128)S(1)} fusion(f32[64,64,128]{2,1,0:T(8,128)S(1)} %multiply_bitcast_fusion.1, f32[64,64]{1,0:T(8,128)S(1)} %fusion.17, f32[32,32]{1,0:T(8,128)S(1)} %fusion.18, pred[]{:T(512)} %bitcast.9), kind=kOutput, calls=%fused_computation.15 | convolution fusion | flops 402657280 | bytes 4214785 | tf_op jit(solution)/shard_map/sbzyx,szw->sbwyx/dot_general | solution.py:64
  113.7 0.0 copy-done.3
  113.7 0.0 copy-done.5
  113.7 6.5 %multiply_reduce_fusion.1 = (f32[]{:T(128)}, f32[]{:T(128)}, f32[1,1,64,64,128]{4,3,2,1,0:T(8,128)}) fusion(f32[1,1,64,64,128]{4,3,2,1,0:T(8,128)S(1)} %get-tuple-element.10, f32[]{:T(128)} %bitcast.33, f32[64,64]{1,0:T(8,128)S(1)} %and_convert_fusion, f32[1,64,32,128]{3,2,1,0:T(8,128)S(1)} %bitcast.115, f32[1,64,32,128]{3,2,1,0:T(8,128)S(1)} %bitcast.117, ...), kind=kOutput, calls=%fused_computation.23 | convolution fusion | flops 409473024 | bytes 10522637 | tf_op jit(solution)/shard_map/sbzyx,syw->sbzwx/dot_general | solution.py:67
  121.5 2.8 %multiply_reduce_fusion = f32[]{:T(128)} fusion(f32[1,1,64,64,128]{4,3,2,1,0:T(8,128)} %get-tuple-element.14, f32[]{:T(128)S(6)} %div.96, f32[1,1,64,64,128]{4,3,2,1,0:T(8,128)S(1)} %get-tuple-element.10, f32[]{:T(128)} %bitcast.33), kind=kLoop, calls=%fused_computation.21 | loop fusion | flops 3670015 | bytes 4194316 | tf_op jit(solution)/shard_map/reduce_sum | solution.py:79
  125.0 2.2 %multiply_bitcast_fusion = f32[1,64,64,128]{3,2,1,0:T(8,128)S(1)} fusion(f32[]{:T(128)} %bitcast.41, f32[]{:T(128)} %bitcast.4, f32[1,1,64,64,128]{4,3,2,1,0:T(8,128)} %get-tuple-element.14, f32[]{:T(128)S(6)} %div.96, f32[1,1,64,64,128]{4,3,2,1,0:T(8,128)S(1)} %get-tuple-element.10, f32[]{:T(128)} %bitcast.33), kind=kLoop, calls=%fused_computation.20 | loop fusion | flops 4718592 | bytes 6291472 | tf_op jit(solution)/shard_map/div | solution.py:115
  127.2 0.2 slice_bitcast_fusion.1
  127.3 4.9 %multiply_add_fusion = f32[64,32,128,8]{2,1,3,0:T(8,128)} fusion(f32[8]{0:T(128)S(1)} %get-tuple-element.17, f32[64,32,128]{2,1,0:T(8,128)S(1)} %get-tuple-element.12, f32[8]{0:T(128)S(1)} %get-tuple-element.18, f32[64,32,128]{2,1,0:T(8,128)S(1)} %get-tuple-element.11), kind=kLoop, calls=%fused_computation | loop fusion | flops 6291456 | bytes 10485824 | tf_op jit(solution)/shard_map/add | solution.py:123
  132.3 0.0 reduce-scatter.2.cloned.1.call-update
  132.3 55.4 %reduce-scatter.2.cloned.1.call-done = f32[64,32,128]{2,1,0:T(8,128)} async-done(((f32[64,256,128]{2,1,0:T(8,128)}), f32[64,32,128]{2,1,0:T(8,128)}) %reduce-scatter.2.cloned.1.call-update) | async-done | bytes 1048592 | tf_op jit(solution)/shard_map/reduce_scatter | solution.py:130
  187.7 1.1 slice.19
  188.7 1.5 collective-permute-start.1
  190.3 16.1 %collective-permute-done.1 = f32[32,32,128]{2,1,0:T(8,128)S(1)} collective-permute-done((f32[32,32,128]{2,1,0:T(8,128)S(1)}, f32[32,32,128]{2,1,0:T(8,128)S(1)}, u32[]{:S(2)}, u32[]{:S(2)}) %collective-permute-start.1) | collective-permute-done | bytes 524320 | tf_op jit(solution)/shard_map/ppermute | solution.py:13
  206.3 1.9 slice_add_fusion
  (6 shorter events, 0.0 us)
Async XLA Ops:
  6.5 71.1 %all-gather.2.cloned.1.call-start = ((), (), s32[]{:S(2)}) async-start(), calls=%async_computation.1 | async-start | bytes 9437184 | tf_op jit(solution)/shard_map/all_gather | solution.py:107
  6.5 19.5 %collective-permute-start = (f32[32,32,128]{2,1,0:T(8,128)}, f32[32,32,128]{2,1,0:T(8,128)S(1)}, u32[]{:S(2)}, u32[]{:S(2)}) collective-permute-start(f32[32,32,128]{2,1,0:T(8,128)} %param.4), channel_id=1, source_target_pairs={{8,0},{16,8},{24,16},{32,24},{40,32},{48,40},{56,48},{64,56},{72,6... | collective-permute-start | bytes 1572872 | tf_op jit(solution)/shard_map/ppermute | solution.py:13
  28.2 3.2 %copy-start.1 = (bf16[1,1,64,64,128]{4,3,2,1,0:T(8,128)(2,1)S(1)}, bf16[1,1,64,64,128]{4,3,2,1,0:T(8,128)(2,1)}, u32[]{:S(2)}) copy-start(bf16[1,1,64,64,128]{4,3,2,1,0:T(8,128)(2,1)} %param.3) | copy-start | bytes 3145732
  28.2 159.5 %reduce-scatter.2.cloned.1.call-start = ((), (), s32[]{:S(2)}) async-start(), calls=%async_computation.2 | async-start | bytes 9437184 | tf_op jit(solution)/shard_map/reduce_scatter | solution.py:130
  77.6 12.2 %copy-start = (f32[64,256,128]{2,1,0:T(8,128)S(1)}, f32[64,256,128]{2,1,0:T(8,128)}, u32[]{:S(2)}) copy-start(f32[64,256,128]{2,1,0:T(8,128)} %all-gather.2.cloned.1.call-done) | copy-start | bytes 25165828
  89.8 7.4 %copy-start.2 = (f32[1,64,32,128]{3,0,2,1:T(1,128)}, f32[1,64,32,128]{3,0,2,1:T(1,128)S(1)}, u32[]{:S(2)}) copy-start(f32[1,64,32,128]{3,0,2,1:T(1,128)S(1)} %fusion) | copy-start | bytes 3145732
  89.8 7.4 %copy-start.6 = (f32[64,64,128]{2,0,1:T(8,128)S(1)}, f32[64,64,128]{2,0,1:T(8,128)}, u32[]{:S(2)}) copy-start(f32[64,64,128]{2,0,1:T(8,128)} %fusion.12) | copy-start | bytes 6291460
  97.2 6.9 %copy-start.4 = (f32[1,64,32,128]{3,0,2,1:T(1,128)}, f32[1,64,32,128]{3,0,2,1:T(1,128)S(1)}, u32[]{:S(2)}) copy-start(f32[1,64,32,128]{3,0,2,1:T(1,128)S(1)} %fusion.2) | copy-start | bytes 3145732
  110.6 3.1 %copy-start.3 = (f32[1,64,32,128]{3,0,2,1:T(1,128)S(1)}, f32[1,64,32,128]{3,0,2,1:T(1,128)}, u32[]{:S(2)}) copy-start(f32[1,64,32,128]{3,0,2,1:T(1,128)} %copy-done.2) | copy-start | bytes 3145732
  110.6 3.1 %copy-start.5 = (f32[1,64,32,128]{3,0,2,1:T(1,128)S(1)}, f32[1,64,32,128]{3,0,2,1:T(1,128)}, u32[]{:S(2)}) copy-start(f32[1,64,32,128]{3,0,2,1:T(1,128)} %copy-done.4) | copy-start | bytes 3145732
  188.7 17.6 %collective-permute-start.1 = (f32[32,32,128]{2,1,0:T(8,128)S(1)}, f32[32,32,128]{2,1,0:T(8,128)S(1)}, u32[]{:S(2)}, u32[]{:S(2)}) collective-permute-start(f32[32,32,128]{2,1,0:T(8,128)S(1)} %slice.19), channel_id=1, source_target_pairs={{248,0},{0,8},{8,16},{16,24},{24,32},{32,40},{40,48},{48,56},{56,6... | collective-permute-start | bytes 1572872 | tf_op jit(solution)/shard_map/ppermute | solution.py:13
Sparse Core Ops, SparseCore 0:
  28.3 49.2 all-gather.1
  132.4 55.1 reduce-scatter.1
where the time goes:
time: 217 us; the launch traced here: 215 us
  waiting for transfers between devices  122 us (56%)
  matrix products  46.1 us (21%)
  between operations  18.4 us (8%)
  other arithmetic  17.4 us (8%)
  starting transfers between devices  9.64 us (4%)
    reduce_scatter x1, waiting for transfers between devices, body(): lax.psum_scatter(placed, 'band', scatter_dimension=1, tiled=True)  55.4 us
    all_gather x1, waiting for transfers between devices, body(): lax.all_gather(jnp.concatenate([potential, following], axis=0), 'band', a...  39.4 us
    ppermute x2, waiting for transfers between devices, from_behind(): return lax.ppermute(block, axis, route)  27.6 us
    dot_general x2, matrix products, hamiltonian(): jnp.einsum('sbzyx,syw->sbzwx', states, y_ops, precision=lax.Precision.HIG...  13.3 us
    dot_general x1, matrix products, from_region(): jnp.einsum('sp,zpqx->szqx', upper_pick, region_cols, precision=lax.Precis...  12.2 us
    ppermute x2, starting transfers between devices, from_behind(): return lax.ppermute(block, axis, route)  9.59 us
    dot_general x2, matrix products, hamiltonian(): jnp.einsum('sbzyx,szw->sbwyx', states, z_ops, precision=lax.Precision.HIG...  7.47 us
    dot_general x1, matrix products, from_region(): jnp.einsum('sp,zpqx->szqx', lower_pick, region_cols, precision=lax.Precis...  7.4 us
  transfers between devices with their start and end apart: 4, of which 4 were waited for; matrix products, arithmetic and copies ran while one was open for 4% of the time, Pallas kernels for 0%

commit v1 on v0

v1 whole, which is shorter than its diff:
```python
import jax
import jax.numpy as jnp
import numpy as np
from jax import lax
from jax.experimental import pallas as pl
from jax.experimental.pallas import tpu as pltpu
from jax.sharding import PartitionSpec as P

STEP_LENGTH = 0.1
EPSILON = 1e-06
CHIPS = 4
VMEM = pl.BlockSpec(memory_space=pltpu.VMEM)
SMEM = pl.BlockSpec(memory_space=pltpu.SMEM)
BIG = pltpu.CompilerParams(vmem_limit_bytes=48 * 1024 * 1024)


def half_kinetic(extent, length):
    m = np.arange(length)
    weight = (2.0 * np.pi * np.minimum(m, length - m) / length) ** 2
    angle = 2.0 * np.pi * (m[:, None] * m[None, :] % length) / length
    matrix = (np.cos(angle) * weight) @ np.cos(angle).T + (np.sin(angle) * weight) @ np.sin(angle).T
    out = np.zeros((extent, extent))
    out[:length, :length] = 0.5 * matrix / length
    return out


def split_const(matrix):
    whole = jnp.asarray(matrix, jnp.float32)
    high = whole.astype(jnp.bfloat16)
    return high, (whole - high.astype(jnp.float32)).astype(jnp.bfloat16)


def operators(depth, width, length):
    x_high, x_low = split_const(half_kinetic(length, length))
    z_high, z_low = split_const(np.kron(half_kinetic(depth, depth), np.eye(8)))
    y_pair = np.stack(
        [np.kron(np.eye(4), half_kinetic(width, width // 2)), np.kron(np.eye(4), half_kinetic(width, width))]
    )
    y_high, y_low = split_const(y_pair)
    return jnp.stack([x_high, x_low]), jnp.stack([z_high, z_low]), jnp.stack([y_high, y_low])


def split(value):
    high = value.astype(jnp.bfloat16)
    return high, (value - high.astype(jnp.float32)).astype(jnp.bfloat16)


def dot(a, b):
    return jnp.dot(a, b, preferred_element_type=jnp.float32)


def xy_part(blocks, x_ref, y_ref, double, exact):
    parts = [(b.astype(jnp.bfloat16), None) if exact else split(b) for b in blocks]
    y_high, y_low = y_ref[0, double], y_ref[1, double]
    highs = jnp.concatenate([p[0] for p in parts], axis=1)
    y_out = dot(y_high, highs) + dot(y_low, highs)
    if not exact:
        y_out = y_out + dot(y_high, jnp.concatenate([p[1] for p in parts], axis=1))
    length = blocks[0].shape[1]
    result = []
    for i, (high, low) in enumerate(parts):
        if exact:
            x_out = dot(jnp.concatenate([high, high], 1), jnp.concatenate([x_ref[0], x_ref[1]], 0))
        else:
            x_out = dot(
                jnp.concatenate([high, low], 1), jnp.concatenate([x_ref[0], x_ref[0]], 0)
            ) + dot(high, x_ref[1])
        result.append(x_out + y_out[:, i * length : (i + 1) * length])
    return result


def z_part(blocks, z_ref, exact):
    both = jnp.concatenate(blocks, axis=1)
    if exact:
        high = both.astype(jnp.bfloat16)
        out = dot(z_ref[0], high) + dot(z_ref[1], high)
    else:
        high, low = split(both)
        out = dot(z_ref[0], high) + dot(z_ref[1], high) + dot(z_ref[0], low)
    length = blocks[0].shape[1]
    return out[:, :length], out[:, length:]


def first_kinetic(scalars, wave, x_ref, z_ref, y_ref, out, states):
    depth, width, length = out.shape
    double = scalars[0]
    live = lax.broadcasted_iota(jnp.int32, (1, width, length), 1) < (width // 2) * (1 + double)

    def xy(i, carry):
        z = i * 8
        s = jnp.where(live, wave[pl.ds(z, 8)].astype(jnp.float32), 0.0)
        states[pl.ds(z, 8)] = s
        rows = s.reshape(2, 4 * width, length)
        lower, upper = xy_part([rows[0], rows[1]], x_ref, y_ref, double, True)
        out[pl.ds(z, 4)] = lower.reshape(4, width, length)
        out[pl.ds(z + 4, 4)] = upper.reshape(4, width, length)
        return carry

    lax.fori_loop(0, depth // 8, xy, 0)

    def zz(i, carry):
        y = [pl.ds(pl.multiple_of(i * 16 + 8 * j, 8), 8) for j in range(2)]
        pieces = z_part([states[:, r].reshape(depth * 8, length) for r in y], z_ref, True)
        for r, piece in zip(y, pieces):
            out[:, r] = out[:, r] + piece.reshape(depth, 8, length)
        return carry

    lax.fori_loop(0, width // 16, zz, 0)


def total(vector):
    return jnp.sum(vector, axis=(0, 1), keepdims=True)


def fold(block):
    return jnp.sum(block.reshape(-1, 8, block.shape[-1]), axis=0)


def second_step(scalars, wave, kinetic, x_ref, z_ref, y_ref, *refs):
    chunks, (keep0, give0, keep1, give1), (trial, acc, pot) = refs[:16], refs[16:20], refs[20:]
    depth, width, length = kinetic.shape
    chunk, column = depth // 2 // CHIPS, width // 2
    double, chip, chip_keep, chip_give, at_keep = (scalars[i] for i in range(5))
    y_keep = pl.ds(pl.multiple_of(at_keep * column, column), column)
    y_give = pl.ds(pl.multiple_of((1 - at_keep) * column, column), column)
    live_rows = column * (1 + double)
    row_ids = lax.broadcasted_iota(jnp.int32, (column, length), 0)
    zero = jnp.zeros((8, length), jnp.float32)
    sums = (zero, zero, zero)
    for index, ref in enumerate(chunks):
        own, slab, m = index // 8 == 0, index // 4 % 2, index % 4
        owner, rows = (chip_keep, y_keep) if own else (chip_give, y_give)
        start = slab * (depth // 2) + lax.rem(chip - m - owner + 2 * CHIPS, CHIPS) * chunk
        half = at_keep if own else 1 - at_keep
        live = row_ids + half * column < live_rows

        def line(i, sums, ref=ref, rows=rows, start=start, live=live):
            z = start + i
            s = jnp.where(live, wave[z, rows].astype(jnp.float32), 0.0)
            v = ref[i]
            h = kinetic[z, rows] + v * s
            pot[z, rows] = v
            trial[z, rows] = h
            return (sums[0] + fold(s * s), sums[1] + fold(s * h), sums[2] + fold(h * h))

        sums = lax.fori_loop(0, chunk, line, sums, unroll=2)
    ss, sh, hh = (total(v) for v in sums)
    cells = (depth * column * length * (1 + double)).astype(jnp.float32)
    rayleigh = sh / (ss + EPSILON)
    shrink = 1.0 + STEP_LENGTH * rayleigh
    live_all = lax.broadcasted_iota(jnp.int32, (1, width, length), 1) < live_rows

    def xy(i, tt):
        z = i * 8
        s = jnp.where(live_all, wave[pl.ds(z, 8)].astype(jnp.float32), 0.0)
        t = shrink.reshape(1, 1, 1) * s - STEP_LENGTH * trial[pl.ds(z, 8)]
        trial[pl.ds(z, 8)] = t
        rows = t.reshape(2, 4 * width, length)
        lower, upper = xy_part([rows[0], rows[1]], x_ref, y_ref, double, False)
        acc[pl.ds(z, 4)] = lower.reshape(4, width, length)
        acc[pl.ds(z + 4, 4)] = upper.reshape(4, width, length)
        return tt + fold(t * t)

    tt = total(lax.fori_loop(0, depth // 8, xy, zero))

    def zz(i, sums):
        y = [pl.ds(pl.multiple_of(i * 16 + 8 * j, 8), 8) for j in range(2)]
        blocks = [trial[:, r].reshape(depth * 8, length) for r in y]
        pieces = z_part(blocks, z_ref, False)
        for r, t, piece in zip(y, blocks, pieces):
            h = acc[:, r].reshape(depth * 8, length) + piece + pot[:, r].reshape(depth * 8, length) * t
            acc[:, r] = h.reshape(depth, 8, length)
            sums = (sums[0] + fold(t * h), sums[1] + fold(h * h))
        return sums

    th, hh = (total(v) for v in lax.fori_loop(0, width // 16, zz, (zero, zero)))
    square = cells / (tt + EPSILON)
    rayleigh = square * th / (square * tt + EPSILON)
    shrink = 1.0 + STEP_LENGTH * rayleigh
    weight = shrink * shrink * tt - 2.0 * STEP_LENGTH * shrink * th + STEP_LENGTH * STEP_LENGTH * hh
    sign = (2 * double - 1).astype(jnp.float32)
    factor = sign / 8.0 * square * cells / (square * weight + EPSILON)
    for slab, kept, given in ((1, keep1, give1), (0, keep0, give0)):
        for k in range(CHIPS):
            for out, owner, rows in ((given, chip_give, y_give), (kept, chip_keep, y_keep)):
                start = slab * (depth // 2) + lax.rem(chip + k - owner + CHIPS, CHIPS) * chunk

                def line(i, carry, out=out, rows=rows, start=start, k=k):
                    z = start + i
                    u = shrink * trial[z, rows] - STEP_LENGTH * acc[z, rows]
                    out[k, i] = factor * (u * u)
                    return carry

                lax.fori_loop(0, chunk, line, 0, unroll=2)


def to_next_chip(block, k):
    return lax.ppermute(block, "band", [(b, (b + 2 * k) % (2 * CHIPS)) for b in range(2 * CHIPS)])


def to_other_core(block):
    return lax.ppermute(block, "band", [(b, b ^ 1) for b in range(2 * CHIPS)])


def to_group(block, distance):
    n = lax.axis_size("frag")
    return lax.ppermute(block, "frag", [(i, (i + distance) % n) for i in range(n)])


def place(code, core):
    low = code // 4
    upper = (low + core) % 2
    return (low + upper) % (2 * CHIPS) // 2, upper


def choose(index, options):
    out = options[0]
    for i, option in enumerate(options[1:], 1):
        out = jnp.where(index == i, option, out)
    return out


def body(wave_init, potential, fragment_order):
    _, _, depth, width, length = wave_init.shape
    chunk, column = depth // 2 // CHIPS, width // 2
    wave = wave_init[0, 0]
    band = lax.axis_index("band")
    chip, core = band // 2, band % 2
    code = fragment_order[0, 0]
    code_before = to_group(fragment_order, 1)[0, 0]
    double = code % 2
    chip_keep, at_keep = place(code, core)
    chip_give, _ = place(code, 1 - core)
    chip_before, _ = place(code_before, core)
    scalars = jnp.stack([double, chip, chip_keep, chip_give, at_keep]).astype(jnp.int32)

    pieces = potential.reshape(CHIPS, chunk, column, length)
    pieces = [pieces[0]] + [to_next_chip(pieces[k], k) for k in range(1, CHIPS)]
    below = to_group(choose((chip - chip_before) % CHIPS, pieces), -1)
    here = choose((chip - chip_keep) % CHIPS, pieces)
    own = [here] + [to_next_chip(here, k) for k in range(1, CHIPS)]
    own += [below] + [to_next_chip(below, k) for k in range(1, CHIPS)]
    other = [to_other_core(p) for p in own]

    x_op, z_op, y_op = operators(depth, width, length)
    box = jax.ShapeDtypeStruct((depth, width, length), jnp.float32)
    kinetic = pl.pallas_call(
        first_kinetic,
        out_shape=box,
        in_specs=[SMEM] + [VMEM] * 4,
        out_specs=VMEM,
        scratch_shapes=[pltpu.VMEM(box.shape, jnp.float32)],
        compiler_params=BIG,
        name="first_kinetic",
    )(scalars, wave, x_op, z_op, y_op)
    quarter = jax.ShapeDtypeStruct((CHIPS, chunk, column, length), jnp.float32)
    keep0, give0, keep1, give1 = pl.pallas_call(
        second_step,
        out_shape=[quarter] * 4,
        in_specs=[SMEM] + [VMEM] * 21,
        out_specs=[VMEM] * 4,
        scratch_shapes=[pltpu.VMEM(box.shape, jnp.float32)] * 3,
        compiler_params=BIG,
        name="second_step",
    )(scalars, wave, kinetic, x_op, z_op, y_op, *own, *other)

    def reduce_chip(keep, give):
        both = keep + to_other_core(give)
        result = both[0]
        for k in range(1, CHIPS):
            result = result + to_next_chip(both[k], k)
        return result

    above = to_group(reduce_chip(keep1, give1), 1)
    here = reduce_chip(keep0, give0)
    sends = []
    for k in range(CHIPS):
        target = (chip + k) % CHIPS
        sends.append(jnp.where(target == chip_keep, here, 0.0) + jnp.where(target == chip_before, above, 0.0))
    final = [sends[0]] + [to_next_chip(sends[k], k) for k in range(CHIPS - 1, 0, -1)]
    return jnp.concatenate(final, axis=0)


def solution(mesh):
    placed = (P("frag", "band", None, None, None), P("frag", "band", None), P("frag", None))
    return jax.shard_map(
        body, mesh=mesh, in_specs=placed, out_specs=P("frag", "band", None), check_vma=False
    )
```

time: 217 us -> 90.8 us (0.42)
  waiting for transfers between devices: 122 us -> 35.9 us
  matrix products: 46.1 us -> 0 us
  starting transfers between devices: 9.64 us -> 29.2 us
  other arithmetic: 17.4 us -> 2.08 us
  between operations: 18.4 us -> 3.66 us
  Pallas kernels: 0 us -> 14.6 us
  local copies, waits for them, and re-layouts: 1.28 us -> 4.74 us
    reduce_scatter x1 -> x0, waiting for transfers between devices: 55.4 us -> none  [body(): lax.psum_scatter(placed, 'band', scatter_dimension=1, tiled=True)]
    dot_general x14 -> x0, matrix products: 46.1 us -> none  [the longest x2 13.3 us: hamiltonian(): jnp.einsum('sbzyx,syw->sbzwx', states, y_ops, precision=lax.Precision.HIG...]
    all_gather x1 -> x0, waiting for transfers between devices: 39.4 us -> none  [body(): lax.all_gather(jnp.concatenate([potential, following], axis=0), 'band', a...]
    ppermute x2 -> x31, starting transfers between devices: 9.59 us -> 29.2 us  [the longest x18 23.6 us: to_next_chip(): lax.ppermute(block, 'band', [(b, (b + 2 * k) % (2 * CHIPS)) for b in rang...]
    pallas_call x0 -> x2, Pallas kernels: none -> 14.6 us  [the longest x1 9.92 us: body(): pl.pallas_call(second_step, out_shape=[quarter] * 4, in_specs=[SMEM] + [V...]
    ppermute x2 -> x31, waiting for transfers between devices: 27.6 us -> 35.9 us  [the longest x18 22.3 us: to_next_chip(): lax.ppermute(block, 'band', [(b, (b + 2 * k) % (2 * CHIPS)) for b in rang...]
    add x2 -> x5, other arithmetic: 6.85 us -> 0.31 us  [the longest x2 0.16 us: reduce_chip(): both = keep + to_other_core(give)]
    reduce_sum x2 -> x0, other arithmetic: 5.32 us -> none  [gradient_step(): weight = jnp.sum(stepped * stepped, axis=(2, 3, 4)) + EPSILON]
  transfers between devices with their start and end apart: 4 -> 31, of which waited for: 4 -> 13; matrix products, arithmetic and copies ran while one was open for 4% -> 0% of each run, Pallas kernels for 0% -> 5%
where the time goes in v1:
time: 90.8 us; the launch traced here: 90.2 us
  waiting for transfers between devices  35.9 us (40%)
  starting transfers between devices  29.2 us (32%)
  Pallas kernels  14.6 us (16%)
  local copies, waits for them, and re-layouts  4.74 us (5%)
  between operations  3.66 us (4%)
  other arithmetic  2.08 us (2%)
    ppermute x18, starting transfers between devices, to_next_chip(): lax.ppermute(block, 'band', [(b, (b + 2 * k) % (2 * CHIPS)) for b in rang...  23.6 us
    ppermute x18, waiting for transfers between devices, to_next_chip(): lax.ppermute(block, 'band', [(b, (b + 2 * k) % (2 * CHIPS)) for b in rang...  22.3 us
    ppermute x3, waiting for transfers between devices, to_group(): lax.ppermute(block, 'frag', [(i, (i + distance) % n) for i in range(n)])  12.2 us
    pallas_call x1, Pallas kernels, body(): pl.pallas_call(second_step, out_shape=[quarter] * 4, in_specs=[SMEM] + [V...  9.92 us
    pallas_call x1, Pallas kernels, body(): pl.pallas_call(first_kinetic, out_shape=box, in_specs=[SMEM] + [VMEM] * 4...  4.65 us
    ppermute x3, starting transfers between devices, to_group(): lax.ppermute(block, 'frag', [(i, (i + distance) % n) for i in range(n)])  3.67 us
    unnamed x10, local copies, waits for them, and re-layouts  3.43 us
    ppermute x10, starting transfers between devices, to_other_core(): return lax.ppermute(block, 'band', [(b, b ^ 1) for b in range(2 * CHIPS)])  1.98 us
  transfers between devices with their start and end apart: 31, of which 13 were waited for; matrix products, arithmetic and copies ran while one was open for 0% of the time, Pallas kernels for 5%

profile of v1, /device:TPU:24, one launch (start us, length us, event | category | flops | bytes accessed | tf_op | source)
XLA Modules:
  0.0 90.2 jit_solution(18208547674675111512)
XLA Ops:
  0.0 1.2 %fusion.7 = (f32[8,32,128]{2,1,0:T(8,128)S(1)}, f32[8,32,128]{2,1,0:T(8,128)S(1)}, f32[8,32,128]{2,1,0:T(8,128)S(1)}) fusion(f32[32,32,128]{2,1,0:T(8,128)} %param.7), kind=kLoop, calls=%fused_computation.21 | loop fusion | bytes 786432 | tf_op jit(solution)/shard_map/slice | solution.py:238
  1.2 0.8 collective-permute-start
  2.0 2.7 %collective-permute-start.1 = (f32[8,32,128]{2,1,0:T(8,128)S(1)}, f32[8,32,128]{2,1,0:T(8,128)S(1)}, u32[]{:S(2)}, u32[]{:S(2)}) collective-permute-start(f32[8,32,128]{2,1,0:T(8,128)S(1)} %get-tuple-element.24), channel_id=1, source_target_pairs={{0,4},{1,5},{2,6},{3,7},{4,0},{5,1},{6,2},{7,3},{8,12},{9,13},{10,... | collective-permute-start | bytes 393224 | tf_op jit(solution)/shard_map/ppermute | solution.py:198
  4.7 0.4 collective-permute-start.2
  5.1 1.5 %collective-permute-start.6 = (s32[1,1]{1,0:T(1,128)}, s32[1,1]{1,0:T(1,128)}, u32[]{:S(2)}, u32[]{:S(2)}) collective-permute-start(s32[1,1]{1,0:T(1,128)} %param.8), channel_id=1, source_target_pairs={{0,8},{8,16},{16,24},{24,32},{32,40},{40,48},{48,56},{56,64},{64,7... | collective-permute-start | bytes 20 | tf_op jit(solution)/shard_map/ppermute | solution.py:207
  7.4 7.4 %collective-permute-done.6 = s32[1,1]{1,0:T(1,128)} collective-permute-done((s32[1,1]{1,0:T(1,128)}, s32[1,1]{1,0:T(1,128)}, u32[]{:S(2)}, u32[]{:S(2)}) %collective-permute-start.6) | collective-permute-done | bytes 36 | tf_op jit(solution)/shard_map/ppermute | solution.py:207
  17.4 0.9 %select_select_fusion = (f32[8,32,128]{2,1,0:T(8,128)S(1)}, f32[8,32,128]{2,1,0:T(8,128)S(1)}) fusion(f32[8,32,128]{2,1,0:T(8,128)S(1)} %collective-permute-done, f32[8,32,128]{2,1,0:T(8,128)S(1)} %collective-permute-done.1, f32[8,32,128]{2,1,0:T(8,128)S(1)} %collective-permute-done.2, f32[32,32,128]{2,1,0:T(8,128)} %param.7, pred[]{:T(512)S(6)} %eq.63, ...), kind=kLoop, calls=%fused_computation.19 | loop fusion | flops 196608 | bytes 786438 | tf_op jit(solution)/shard_map/jit(_where)/select_n | solution.py:219
  18.4 2.1 %collective-permute-start.7 = (f32[8,32,128]{2,1,0:T(8,128)S(1)}, f32[8,32,128]{2,1,0:T(8,128)S(1)}, u32[]{:S(2)}, u32[]{:S(2)}) collective-permute-start(f32[8,32,128]{2,1,0:T(8,128)S(1)} %get-tuple-element.15), channel_id=1, source_target_pairs={{0,248},{8,0},{16,8},{24,16},{32,24},{40,32},{48,40},{56,48},{64,5... | collective-permute-start | bytes 393224 | tf_op jit(solution)/shard_map/ppermute | solution.py:207
  20.5 2.4 %collective-permute-start.3 = (f32[8,32,128]{2,1,0:T(8,128)S(1)}, f32[8,32,128]{2,1,0:T(8,128)S(1)}, u32[]{:S(2)}, u32[]{:S(2)}) collective-permute-start(f32[8,32,128]{2,1,0:T(8,128)S(1)} %get-tuple-element.16.refs_0_), channel_id=1, source_target_pairs={{0,2},{1,3},{2,4},{3,5},{4,6},{5,7},{6,0},{7,1},{8,10},{9,11},{10,... | collective-permute-start | bytes 393224 | tf_op jit(solution)/shard_map/ppermute | solution.py:198
  22.9 1.3 %collective-permute-start.5 = (f32[8,32,128]{2,1,0:T(8,128)S(1)}, f32[8,32,128]{2,1,0:T(8,128)S(1)}, u32[]{:S(2)}, u32[]{:S(2)}) collective-permute-start(f32[8,32,128]{2,1,0:T(8,128)S(1)} %get-tuple-element.16.refs_0_), channel_id=1, source_target_pairs={{0,6},{1,7},{2,0},{3,1},{4,2},{5,3},{6,4},{7,5},{8,14},{9,15},{10,... | collective-permute-start | bytes 393224 | tf_op jit(solution)/shard_map/ppermute | solution.py:198
  24.2 1.9 %collective-permute-start.8 = (f32[8,32,128]{2,1,0:T(8,128)S(1)}, f32[8,32,128]{2,1,0:T(8,128)S(1)}, u32[]{:S(2)}, u32[]{:S(2)}) collective-permute-start(f32[8,32,128]{2,1,0:T(8,128)S(1)} %collective-permute-done.7.refs_4_), channel_id=1, source_target_pairs={{0,2},{1,3},{2,4},{3,5},{4,6},{5,7},{6,0},{7,1},{8,10},{9,11},{10,... | collective-permute-start | bytes 393224 | tf_op jit(solution)/shard_map/ppermute | solution.py:198
  26.1 2.9 %collective-permute-done.3.refs_1_ = f32[8,32,128]{2,1,0:T(8,128)S(1)} collective-permute-done((f32[8,32,128]{2,1,0:T(8,128)S(1)}, f32[8,32,128]{2,1,0:T(8,128)S(1)}, u32[]{:S(2)}, u32[]{:S(2)}) %collective-permute-start.3) | collective-permute-done | bytes 131104 | tf_op jit(solution)/shard_map/ppermute | solution.py:198
  29.0 1.6 %collective-permute-done.4.refs_2_ = f32[8,32,128]{2,1,0:T(8,128)S(1)} collective-permute-done((f32[8,32,128]{2,1,0:T(8,128)S(1)}, f32[8,32,128]{2,1,0:T(8,128)S(1)}, u32[]{:S(2)}, u32[]{:S(2)}) %collective-permute-start.4) | collective-permute-done | bytes 131104 | tf_op jit(solution)/shard_map/ppermute | solution.py:198
  30.6 2.9 %collective-permute-start.10 = (f32[8,32,128]{2,1,0:T(8,128)S(1)}, f32[8,32,128]{2,1,0:T(8,128)S(1)}, u32[]{:S(2)}, u32[]{:S(2)}) collective-permute-start(f32[8,32,128]{2,1,0:T(8,128)S(1)} %collective-permute-done.7.refs_4_), channel_id=1, source_target_pairs={{0,6},{1,7},{2,0},{3,1},{4,2},{5,3},{6,4},{7,5},{8,14},{9,15},{10,... | collective-permute-start | bytes 393224 | tf_op jit(solution)/shard_map/ppermute | solution.py:198
  33.6 0.5 collective-permute-start.13
  34.1 0.1 collective-permute-start.15
  34.2 2.1 %collective-permute-done.9.refs_6_ = f32[8,32,128]{2,1,0:T(8,128)S(1)} collective-permute-done((f32[8,32,128]{2,1,0:T(8,128)S(1)}, f32[8,32,128]{2,1,0:T(8,128)S(1)}, u32[]{:S(2)}, u32[]{:S(2)}) %collective-permute-start.9) | collective-permute-done | bytes 131104 | tf_op jit(solution)/shard_map/ppermute | solution.py:198
  36.2 1.3 %collective-permute-done.10.refs_7_ = f32[8,32,128]{2,1,0:T(8,128)S(1)} collective-permute-done((f32[8,32,128]{2,1,0:T(8,128)S(1)}, f32[8,32,128]{2,1,0:T(8,128)S(1)}, u32[]{:S(2)}, u32[]{:S(2)}) %collective-permute-start.10) | collective-permute-done | bytes 131104 | tf_op jit(solution)/shard_map/ppermute | solution.py:198
  37.6 0.5 collective-permute-start.17
  38.1 0.3 collective-permute-start.18
  38.4 0.1 stack.50.scalars
  38.4 1.2 %copy-done.2 = bf16[2,512,512]{2,1,0:T(8,128)(2,1)S(1)} copy-done((bf16[2,512,512]{2,1,0:T(8,128)(2,1)S(1)}, bf16[2,512,512]{2,1,0:T(8,128)(2,1)}, u32[]{:S(2)}) %copy-start.2) | copy-done | bytes 1048600
  39.7 0.8 copy-done.4
  40.5 4.7 %first_kinetic.1.kinetic = f32[64,64,128]{2,1,0:T(8,128)S(1)} custom-call(s32[5]{0:T(128)S(1)} %stack.50.scalars, bf16[64,64,128]{2,1,0:T(8,128)(2,1)S(1)} %bitcast.41, bf16[2,128,128]{2,1,0:T(8,128)(2,1)S(1)} %copy-done.4, bf16[2,512,512]{2,1,0:T(8,128)(2,1)S(1)} %copy-done.2, bf16[2,2,256,256]{3,2,1,0:T(8,128)(2,1)S(1)} %copy-done.3), custom_call_target="tpu_custom_call" | custom-call | tf_op jit(solution)/shard_map/first_kinetic/pallas_call | solution.py:247
  45.2 1.4 %copy-done = f32[64,64,128]{2,1,0:T(8,128)} copy-done((f32[64,64,128]{2,1,0:T(8,128)}, f32[64,64,128]{2,1,0:T(8,128)S(1)}, u32[]{:S(2)}) %copy-start) | copy-done | bytes 2097176
  46.6 9.9 %second_step.1 = (f32[4,8,32,128]{3,2,1,0:T(8,128)S(1)}, f32[4,8,32,128]{3,2,1,0:T(8,128)S(1)}, f32[4,8,32,128]{3,2,1,0:T(8,128)S(1)}, f32[4,8,32,128]{3,2,1,0:T(8,128)S(1)}) custom-call(s32[5]{0:T(128)S(1)} %stack.50.scalars, bf16[64,64,128]{2,1,0:T(8,128)(2,1)S(1)} %bitcast.42, f32[64,64,128]{2,1,0:T(8,128)} %copy-done, ...), custom_call_target="tpu_custom_call" | custom-call | tf_op jit(solution)/shard_map/second_step/pallas_call | solution.py:257
  56.5 0.3 collective-permute-start.23
  56.8 0.3 collective-permute-start.19
  57.1 1.4 %collective-permute-done.23 = f32[4,8,32,128]{3,2,1,0:T(8,128)S(1)} collective-permute-done((f32[4,8,32,128]{3,2,1,0:T(8,128)S(1)}, f32[4,8,32,128]{3,2,1,0:T(8,128)S(1)}, u32[]{:S(2)}, u32[]{:S(2)}) %collective-permute-start.23) | collective-permute-done | bytes 524320 | tf_op jit(solution)/shard_map/ppermute | solution.py:202
  58.5 0.1 add.133
  58.6 1.9 %collective-permute-start.24 = (f32[8,32,128]{2,1,0:T(8,128)S(1)}, f32[8,32,128]{2,1,0:T(8,128)S(1)}, u32[]{:S(2)}, u32[]{:S(2)}) collective-permute-start(f32[8,32,128]{2,1,0:T(8,128)S(1)} %get-tuple-element.20), channel_id=1, source_target_pairs={{0,2},{1,3},{2,4},{3,5},{4,6},{5,7},{6,0},{7,1},{8,10},{9,11},{10,... | collective-permute-start | bytes 393224 | tf_op jit(solution)/shard_map/ppermute | solution.py:198
  60.5 1.2 %collective-permute-start.25 = (f32[8,32,128]{2,1,0:T(8,128)S(1)}, f32[8,32,128]{2,1,0:T(8,128)S(1)}, u32[]{:S(2)}, u32[]{:S(2)}) collective-permute-start(f32[8,32,128]{2,1,0:T(8,128)S(1)} %get-tuple-element.22), channel_id=1, source_target_pairs={{0,4},{1,5},{2,6},{3,7},{4,0},{5,1},{6,2},{7,3},{8,12},{9,13},{10,... | collective-permute-start | bytes 393224 | tf_op jit(solution)/shard_map/ppermute | solution.py:198
  61.7 0.1 add.129
  61.8 3.3 %collective-permute-start.20 = (f32[8,32,128]{2,1,0:T(8,128)S(1)}, f32[8,32,128]{2,1,0:T(8,128)S(1)}, u32[]{:S(2)}, u32[]{:S(2)}) collective-permute-start(f32[8,32,128]{2,1,0:T(8,128)S(1)} %get-tuple-element.17), channel_id=1, source_target_pairs={{0,2},{1,3},{2,4},{3,5},{4,6},{5,7},{6,0},{7,1},{8,10},{9,11},{10,... | collective-permute-start | bytes 393224 | tf_op jit(solution)/shard_map/ppermute | solution.py:198
  65.2 1.1 %collective-permute-start.21 = (f32[8,32,128]{2,1,0:T(8,128)S(1)}, f32[8,32,128]{2,1,0:T(8,128)S(1)}, u32[]{:S(2)}, u32[]{:S(2)}) collective-permute-start(f32[8,32,128]{2,1,0:T(8,128)S(1)} %get-tuple-element.19), channel_id=1, source_target_pairs={{0,4},{1,5},{2,6},{3,7},{4,0},{5,1},{6,2},{7,3},{8,12},{9,13},{10,... | collective-permute-start | bytes 393224 | tf_op jit(solution)/shard_map/ppermute | solution.py:198
  66.3 0.2 collective-permute-start.22
  66.5 1.9 %collective-permute-done.25 = f32[8,32,128]{2,1,0:T(8,128)S(1)} collective-permute-done((f32[8,32,128]{2,1,0:T(8,128)S(1)}, f32[8,32,128]{2,1,0:T(8,128)S(1)}, u32[]{:S(2)}, u32[]{:S(2)}) %collective-permute-start.25) | collective-permute-done | bytes 131104 | tf_op jit(solution)/shard_map/ppermute | solution.py:198
  68.4 3.9 %collective-permute-done.26 = f32[8,32,128]{2,1,0:T(8,128)S(1)} collective-permute-done((f32[8,32,128]{2,1,0:T(8,128)S(1)}, f32[8,32,128]{2,1,0:T(8,128)S(1)}, u32[]{:S(2)}, u32[]{:S(2)}) %collective-permute-start.26) | collective-permute-done | bytes 131104 | tf_op jit(solution)/shard_map/ppermute | solution.py:198
  72.3 0.1 collective-permute-start.27
  72.5 1.5 %collective-permute-done.21 = f32[8,32,128]{2,1,0:T(8,128)S(1)} collective-permute-done((f32[8,32,128]{2,1,0:T(8,128)S(1)}, f32[8,32,128]{2,1,0:T(8,128)S(1)}, u32[]{:S(2)}, u32[]{:S(2)}) %collective-permute-start.21) | collective-permute-done | bytes 131104 | tf_op jit(solution)/shard_map/ppermute | solution.py:198
  74.0 1.8 %collective-permute-done.22 = f32[8,32,128]{2,1,0:T(8,128)S(1)} collective-permute-done((f32[8,32,128]{2,1,0:T(8,128)S(1)}, f32[8,32,128]{2,1,0:T(8,128)S(1)}, u32[]{:S(2)}, u32[]{:S(2)}) %collective-permute-start.22) | collective-permute-done | bytes 131104 | tf_op jit(solution)/shard_map/ppermute | solution.py:198
  75.9 4.8 %collective-permute-done.27 = f32[8,32,128]{2,1,0:T(8,128)S(1)} collective-permute-done((f32[8,32,128]{2,1,0:T(8,128)S(1)}, f32[8,32,128]{2,1,0:T(8,128)S(1)}, u32[]{:S(2)}, u32[]{:S(2)}) %collective-permute-start.27) | collective-permute-done | bytes 131104 | tf_op jit(solution)/shard_map/ppermute | solution.py:207
  80.8 0.1 collective-permute-start.28
  80.9 1.0 %collective-permute-start.29 = (f32[8,32,128]{2,1,0:T(8,128)S(1)}, f32[8,32,128]{2,1,0:T(8,128)S(1)}, u32[]{:S(2)}, u32[]{:S(2)}) collective-permute-start(f32[8,32,128]{2,1,0:T(8,128)S(1)} %get-tuple-element.28), channel_id=1, source_target_pairs={{0,4},{1,5},{2,6},{3,7},{4,0},{5,1},{6,2},{7,3},{8,12},{9,13},{10,... | collective-permute-start | bytes 393224 | tf_op jit(solution)/shard_map/ppermute | solution.py:198
  81.8 2.3 %collective-permute-start.30 = (f32[8,32,128]{2,1,0:T(8,128)S(1)}, f32[8,32,128]{2,1,0:T(8,128)S(1)}, u32[]{:S(2)}, u32[]{:S(2)}) collective-permute-start(f32[8,32,128]{2,1,0:T(8,128)S(1)} %get-tuple-element.27), channel_id=1, source_target_pairs={{0,2},{1,3},{2,4},{3,5},{4,6},{5,7},{6,0},{7,1},{8,10},{9,11},{10,... | collective-permute-start | bytes 393224 | tf_op jit(solution)/shard_map/ppermute | solution.py:198
  84.1 4.3 %collective-permute-done.28 = f32[8,32,128]{2,1,0:T(8,128)S(1)} collective-permute-done((f32[8,32,128]{2,1,0:T(8,128)S(1)}, f32[8,32,128]{2,1,0:T(8,128)S(1)}, u32[]{:S(2)}, u32[]{:S(2)}) %collective-permute-start.28) | collective-permute-done | bytes 131104 | tf_op jit(solution)/shard_map/ppermute | solution.py:198
  88.5 0.9 collective-permute-done.30
  89.3 0.8 pad_maximum_fusion
  (37 shorter events, 0.3 us)
Async XLA Ops:
  0.0 38.4 %copy-start.3 = (bf16[2,2,256,256]{3,2,1,0:T(8,128)(2,1)S(1)}, bf16[2,2,256,256]{3,2,1,0:T(8,128)(2,1)}, u32[]{:S(2)}) copy-start(bf16[2,2,256,256]{3,2,1,0:T(8,128)(2,1)} %constant.165.y_ref) | copy-start | bytes 1572868
  0.0 38.4 %copy-start.1 = (bf16[1,1,64,64,128]{4,3,2,1,0:T(8,128)(2,1)S(1)}, bf16[1,1,64,64,128]{4,3,2,1,0:T(8,128)(2,1)}, u32[]{:S(2)}) copy-start(bf16[1,1,64,64,128]{4,3,2,1,0:T(8,128)(2,1)} %param.6) | copy-start | bytes 3145732
  1.2 16.2 %collective-permute-start = (f32[8,32,128]{2,1,0:T(8,128)S(1)}, f32[8,32,128]{2,1,0:T(8,128)S(1)}, u32[]{:S(2)}, u32[]{:S(2)}) collective-permute-start(f32[8,32,128]{2,1,0:T(8,128)S(1)} %get-tuple-element.25), channel_id=1, source_target_pairs={{0,6},{1,7},{2,0},{3,1},{4,2},{5,3},{6,4},{7,5},{8,14},{9,15},{10,... | collective-permute-start | bytes 393224 | tf_op jit(solution)/shard_map/ppermute | solution.py:198
  2.0 15.4 %collective-permute-start.1 = (f32[8,32,128]{2,1,0:T(8,128)S(1)}, f32[8,32,128]{2,1,0:T(8,128)S(1)}, u32[]{:S(2)}, u32[]{:S(2)}) collective-permute-start(f32[8,32,128]{2,1,0:T(8,128)S(1)} %get-tuple-element.24), channel_id=1, source_target_pairs={{0,4},{1,5},{2,6},{3,7},{4,0},{5,1},{6,2},{7,3},{8,12},{9,13},{10,... | collective-permute-start | bytes 393224 | tf_op jit(solution)/shard_map/ppermute | solution.py:198
  4.7 12.7 %collective-permute-start.2 = (f32[8,32,128]{2,1,0:T(8,128)S(1)}, f32[8,32,128]{2,1,0:T(8,128)S(1)}, u32[]{:S(2)}, u32[]{:S(2)}) collective-permute-start(f32[8,32,128]{2,1,0:T(8,128)S(1)} %get-tuple-element.23), channel_id=1, source_target_pairs={{0,2},{1,3},{2,4},{3,5},{4,6},{5,7},{6,0},{7,1},{8,10},{9,11},{10,... | collective-permute-start | bytes 393224 | tf_op jit(solution)/shard_map/ppermute | solution.py:198
  5.1 9.7 %collective-permute-start.6 = (s32[1,1]{1,0:T(1,128)}, s32[1,1]{1,0:T(1,128)}, u32[]{:S(2)}, u32[]{:S(2)}) collective-permute-start(s32[1,1]{1,0:T(1,128)} %param.8), channel_id=1, source_target_pairs={{0,8},{8,16},{16,24},{24,32},{32,40},{40,48},{48,56},{56,64},{64,7... | collective-permute-start | bytes 20 | tf_op jit(solution)/shard_map/ppermute | solution.py:207
  18.4 5.8 %collective-permute-start.7 = (f32[8,32,128]{2,1,0:T(8,128)S(1)}, f32[8,32,128]{2,1,0:T(8,128)S(1)}, u32[]{:S(2)}, u32[]{:S(2)}) collective-permute-start(f32[8,32,128]{2,1,0:T(8,128)S(1)} %get-tuple-element.15), channel_id=1, source_target_pairs={{0,248},{8,0},{16,8},{24,16},{32,24},{40,32},{48,40},{56,48},{64,5... | collective-permute-start | bytes 393224 | tf_op jit(solution)/shard_map/ppermute | solution.py:207
  20.5 8.5 %collective-permute-start.3 = (f32[8,32,128]{2,1,0:T(8,128)S(1)}, f32[8,32,128]{2,1,0:T(8,128)S(1)}, u32[]{:S(2)}, u32[]{:S(2)}) collective-permute-start(f32[8,32,128]{2,1,0:T(8,128)S(1)} %get-tuple-element.16.refs_0_), channel_id=1, source_target_pairs={{0,2},{1,3},{2,4},{3,5},{4,6},{5,7},{6,0},{7,1},{8,10},{9,11},{10,... | collective-permute-start | bytes 393224 | tf_op jit(solution)/shard_map/ppermute | solution.py:198
  22.8 7.8 %collective-permute-start.4 = (f32[8,32,128]{2,1,0:T(8,128)S(1)}, f32[8,32,128]{2,1,0:T(8,128)S(1)}, u32[]{:S(2)}, u32[]{:S(2)}) collective-permute-start(f32[8,32,128]{2,1,0:T(8,128)S(1)} %get-tuple-element.16.refs_0_), channel_id=1, source_target_pairs={{0,4},{1,5},{2,6},{3,7},{4,0},{5,1},{6,2},{7,3},{8,12},{9,13},{10,... | collective-permute-start | bytes 393224 | tf_op jit(solution)/shard_map/ppermute | solution.py:198
  22.9 10.7 %collective-permute-start.5 = (f32[8,32,128]{2,1,0:T(8,128)S(1)}, f32[8,32,128]{2,1,0:T(8,128)S(1)}, u32[]{:S(2)}, u32[]{:S(2)}) collective-permute-start(f32[8,32,128]{2,1,0:T(8,128)S(1)} %get-tuple-element.16.refs_0_), channel_id=1, source_target_pairs={{0,6},{1,7},{2,0},{3,1},{4,2},{5,3},{6,4},{7,5},{8,14},{9,15},{10,... | collective-permute-start | bytes 393224 | tf_op jit(solution)/shard_map/ppermute | solution.py:198
  24.2 9.4 %collective-permute-start.11 = (f32[8,32,128]{2,1,0:T(8,128)S(1)}, f32[8,32,128]{2,1,0:T(8,128)S(1)}, u32[]{:S(2)}, u32[]{:S(2)}) collective-permute-start(f32[8,32,128]{2,1,0:T(8,128)S(1)} %get-tuple-element.16.refs_0_), channel_id=1, source_target_pairs={{0,1},{1,0},{2,3},{3,2},{4,5},{5,4},{6,7},{7,6},{8,9},{9,8},{10,11... | collective-permute-start | bytes 393224 | tf_op jit(solution)/shard_map/ppermute | solution.py:202
  24.2 9.9 %collective-permute-start.8 = (f32[8,32,128]{2,1,0:T(8,128)S(1)}, f32[8,32,128]{2,1,0:T(8,128)S(1)}, u32[]{:S(2)}, u32[]{:S(2)}) collective-permute-start(f32[8,32,128]{2,1,0:T(8,128)S(1)} %collective-permute-done.7.refs_4_), channel_id=1, source_target_pairs={{0,2},{1,3},{2,4},{3,5},{4,6},{5,7},{6,0},{7,1},{8,10},{9,11},{10,... | collective-permute-start | bytes 393224 | tf_op jit(solution)/shard_map/ppermute | solution.py:198
  29.0 7.2 %collective-permute-start.9 = (f32[8,32,128]{2,1,0:T(8,128)S(1)}, f32[8,32,128]{2,1,0:T(8,128)S(1)}, u32[]{:S(2)}, u32[]{:S(2)}) collective-permute-start(f32[8,32,128]{2,1,0:T(8,128)S(1)} %collective-permute-done.7.refs_4_), channel_id=1, source_target_pairs={{0,4},{1,5},{2,6},{3,7},{4,0},{5,1},{6,2},{7,3},{8,12},{9,13},{10,... | collective-permute-start | bytes 393224 | tf_op jit(solution)/shard_map/ppermute | solution.py:198
  30.6 7.0 %collective-permute-start.10 = (f32[8,32,128]{2,1,0:T(8,128)S(1)}, f32[8,32,128]{2,1,0:T(8,128)S(1)}, u32[]{:S(2)}, u32[]{:S(2)}) collective-permute-start(f32[8,32,128]{2,1,0:T(8,128)S(1)} %collective-permute-done.7.refs_4_), channel_id=1, source_target_pairs={{0,6},{1,7},{2,0},{3,1},{4,2},{5,3},{6,4},{7,5},{8,14},{9,15},{10,... | collective-permute-start | bytes 393224 | tf_op jit(solution)/shard_map/ppermute | solution.py:198
  33.5 4.0 %collective-permute-start.12 = (f32[8,32,128]{2,1,0:T(8,128)S(1)}, f32[8,32,128]{2,1,0:T(8,128)S(1)}, u32[]{:S(2)}, u32[]{:S(2)}) collective-permute-start(f32[8,32,128]{2,1,0:T(8,128)S(1)} %collective-permute-done.3.refs_1_), channel_id=1, source_target_pairs={{0,1},{1,0},{2,3},{3,2},{4,5},{5,4},{6,7},{7,6},{8,9},{9,8},{10,11... | collective-permute-start | bytes 393224 | tf_op jit(solution)/shard_map/ppermute | solution.py:202
  33.6 4.5 %collective-permute-start.13 = (f32[8,32,128]{2,1,0:T(8,128)S(1)}, f32[8,32,128]{2,1,0:T(8,128)S(1)}, u32[]{:S(2)}, u32[]{:S(2)}) collective-permute-start(f32[8,32,128]{2,1,0:T(8,128)S(1)} %collective-permute-done.4.refs_2_), channel_id=1, source_target_pairs={{0,1},{1,0},{2,3},{3,2},{4,5},{5,4},{6,7},{7,6},{8,9},{9,8},{10,11... | collective-permute-start | bytes 393224 | tf_op jit(solution)/shard_map/ppermute | solution.py:202
  34.1 12.5 %collective-permute-start.15 = (f32[8,32,128]{2,1,0:T(8,128)S(1)}, f32[8,32,128]{2,1,0:T(8,128)S(1)}, u32[]{:S(2)}, u32[]{:S(2)}) collective-permute-start(f32[8,32,128]{2,1,0:T(8,128)S(1)} %collective-permute-done.7.refs_4_), channel_id=1, source_target_pairs={{0,1},{1,0},{2,3},{3,2},{4,5},{5,4},{6,7},{7,6},{8,9},{9,8},{10,11... | collective-permute-start | bytes 393224 | tf_op jit(solution)/shard_map/ppermute | solution.py:202
  36.2 10.3 %collective-permute-start.14 = (f32[8,32,128]{2,1,0:T(8,128)S(1)}, f32[8,32,128]{2,1,0:T(8,128)S(1)}, u32[]{:S(2)}, u32[]{:S(2)}) collective-permute-start(f32[8,32,128]{2,1,0:T(8,128)S(1)} %collective-permute-done.5.refs_3_), channel_id=1, source_target_pairs={{0,1},{1,0},{2,3},{3,2},{4,5},{5,4},{6,7},{7,6},{8,9},{9,8},{10,11... | collective-permute-start | bytes 393224 | tf_op jit(solution)/shard_map/ppermute | solution.py:202
  37.6 9.0 %collective-permute-start.16 = (f32[8,32,128]{2,1,0:T(8,128)S(1)}, f32[8,32,128]{2,1,0:T(8,128)S(1)}, u32[]{:S(2)}, u32[]{:S(2)}) collective-permute-start(f32[8,32,128]{2,1,0:T(8,128)S(1)} %collective-permute-done.8.refs_5_), channel_id=1, source_target_pairs={{0,1},{1,0},{2,3},{3,2},{4,5},{5,4},{6,7},{7,6},{8,9},{9,8},{10,11... | collective-permute-start | bytes 393224 | tf_op jit(solution)/shard_map/ppermute | solution.py:202
  37.6 9.0 %collective-permute-start.17 = (f32[8,32,128]{2,1,0:T(8,128)S(1)}, f32[8,32,128]{2,1,0:T(8,128)S(1)}, u32[]{:S(2)}, u32[]{:S(2)}) collective-permute-start(f32[8,32,128]{2,1,0:T(8,128)S(1)} %collective-permute-done.9.refs_6_), channel_id=1, source_target_pairs={{0,1},{1,0},{2,3},{3,2},{4,5},{5,4},{6,7},{7,6},{8,9},{9,8},{10,11... | collective-permute-start | bytes 393224 | tf_op jit(solution)/shard_map/ppermute | solution.py:202
  38.1 8.5 %collective-permute-start.18 = (f32[8,32,128]{2,1,0:T(8,128)S(1)}, f32[8,32,128]{2,1,0:T(8,128)}, u32[]{:S(2)}, u32[]{:S(2)}) collective-permute-start(f32[8,32,128]{2,1,0:T(8,128)S(1)} %collective-permute-done.10.refs_7_), channel_id=1, source_target_pairs={{0,1},{1,0},{2,3},{3,2},{4,5},{5,4},{6,7},{7,6},{8,9},{9,8},{10,11... | collective-permute-start | bytes 393224 | tf_op jit(solution)/shard_map/ppermute | solution.py:202
  38.4 1.2 %copy-start.2 = (bf16[2,512,512]{2,1,0:T(8,128)(2,1)S(1)}, bf16[2,512,512]{2,1,0:T(8,128)(2,1)}, u32[]{:S(2)}) copy-start(bf16[2,512,512]{2,1,0:T(8,128)(2,1)} %constant.158.z_ref) | copy-start | bytes 3145732
  39.7 0.8 copy-start.4
  45.2 1.4 %copy-start = (f32[64,64,128]{2,1,0:T(8,128)}, f32[64,64,128]{2,1,0:T(8,128)S(1)}, u32[]{:S(2)}) copy-start(f32[64,64,128]{2,1,0:T(8,128)S(1)} %first_kinetic.1.kinetic) | copy-start | bytes 6291460
  56.5 2.0 %collective-permute-start.23 = (f32[4,8,32,128]{3,2,1,0:T(8,128)S(1)}, f32[4,8,32,128]{3,2,1,0:T(8,128)S(1)}, u32[]{:S(2)}, u32[]{:S(2)}) collective-permute-start(f32[4,8,32,128]{3,2,1,0:T(8,128)S(1)} %get-tuple-element.12), channel_id=1, source_target_pairs={{0,1},{1,0},{2,3},{3,2},{4,5},{5,4},{6,7},{7,6},{8,9},{9,8},{10,11... | collective-permute-start | bytes 1572872 | tf_op jit(solution)/shard_map/ppermute | solution.py:202
  56.8 4.9 %collective-permute-start.19 = (f32[4,8,32,128]{3,2,1,0:T(8,128)S(1)}, f32[4,8,32,128]{3,2,1,0:T(8,128)S(1)}, u32[]{:S(2)}, u32[]{:S(2)}) collective-permute-start(f32[4,8,32,128]{3,2,1,0:T(8,128)S(1)} %get-tuple-element.10), channel_id=1, source_target_pairs={{0,1},{1,0},{2,3},{3,2},{4,5},{5,4},{6,7},{7,6},{8,9},{9,8},{10,11... | collective-permute-start | bytes 1572872 | tf_op jit(solution)/shard_map/ppermute | solution.py:202
  58.6 7.7 %collective-permute-start.24 = (f32[8,32,128]{2,1,0:T(8,128)S(1)}, f32[8,32,128]{2,1,0:T(8,128)S(1)}, u32[]{:S(2)}, u32[]{:S(2)}) collective-permute-start(f32[8,32,128]{2,1,0:T(8,128)S(1)} %get-tuple-element.20), channel_id=1, source_target_pairs={{0,2},{1,3},{2,4},{3,5},{4,6},{5,7},{6,0},{7,1},{8,10},{9,11},{10,... | collective-permute-start | bytes 393224 | tf_op jit(solution)/shard_map/ppermute | solution.py:198
  60.5 7.9 %collective-permute-start.25 = (f32[8,32,128]{2,1,0:T(8,128)S(1)}, f32[8,32,128]{2,1,0:T(8,128)S(1)}, u32[]{:S(2)}, u32[]{:S(2)}) collective-permute-start(f32[8,32,128]{2,1,0:T(8,128)S(1)} %get-tuple-element.22), channel_id=1, source_target_pairs={{0,4},{1,5},{2,6},{3,7},{4,0},{5,1},{6,2},{7,3},{8,12},{9,13},{10,... | collective-permute-start | bytes 393224 | tf_op jit(solution)/shard_map/ppermute | solution.py:198
  61.7 10.5 %collective-permute-start.26 = (f32[8,32,128]{2,1,0:T(8,128)S(1)}, f32[8,32,128]{2,1,0:T(8,128)S(1)}, u32[]{:S(2)}, u32[]{:S(2)}) collective-permute-start(f32[8,32,128]{2,1,0:T(8,128)S(1)} %get-tuple-element.21), channel_id=1, source_target_pairs={{0,6},{1,7},{2,0},{3,1},{4,2},{5,3},{6,4},{7,5},{8,14},{9,15},{10,... | collective-permute-start | bytes 393224 | tf_op jit(solution)/shard_map/ppermute | solution.py:198
  61.8 10.6 %collective-permute-start.20 = (f32[8,32,128]{2,1,0:T(8,128)S(1)}, f32[8,32,128]{2,1,0:T(8,128)S(1)}, u32[]{:S(2)}, u32[]{:S(2)}) collective-permute-start(f32[8,32,128]{2,1,0:T(8,128)S(1)} %get-tuple-element.17), channel_id=1, source_target_pairs={{0,2},{1,3},{2,4},{3,5},{4,6},{5,7},{6,0},{7,1},{8,10},{9,11},{10,... | collective-permute-start | bytes 393224 | tf_op jit(solution)/shard_map/ppermute | solution.py:198
  65.2 8.9 %collective-permute-start.21 = (f32[8,32,128]{2,1,0:T(8,128)S(1)}, f32[8,32,128]{2,1,0:T(8,128)S(1)}, u32[]{:S(2)}, u32[]{:S(2)}) collective-permute-start(f32[8,32,128]{2,1,0:T(8,128)S(1)} %get-tuple-element.19), channel_id=1, source_target_pairs={{0,4},{1,5},{2,6},{3,7},{4,0},{5,1},{6,2},{7,3},{8,12},{9,13},{10,... | collective-permute-start | bytes 393224 | tf_op jit(solution)/shard_map/ppermute | solution.py:198
  66.3 9.6 %collective-permute-start.22 = (f32[8,32,128]{2,1,0:T(8,128)S(1)}, f32[8,32,128]{2,1,0:T(8,128)S(1)}, u32[]{:S(2)}, u32[]{:S(2)}) collective-permute-start(f32[8,32,128]{2,1,0:T(8,128)S(1)} %get-tuple-element.18), channel_id=1, source_target_pairs={{0,6},{1,7},{2,0},{3,1},{4,2},{5,3},{6,4},{7,5},{8,14},{9,15},{10,... | collective-permute-start | bytes 393224 | tf_op jit(solution)/shard_map/ppermute | solution.py:198
  72.3 8.4 %collective-permute-start.27 = (f32[8,32,128]{2,1,0:T(8,128)S(1)}, f32[8,32,128]{2,1,0:T(8,128)S(1)}, u32[]{:S(2)}, u32[]{:S(2)}) collective-permute-start(f32[8,32,128]{2,1,0:T(8,128)S(1)} %fusion.2), channel_id=1, source_target_pairs={{0,8},{8,16},{16,24},{24,32},{32,40},{40,48},{48,56},{56,64},{64,7... | collective-permute-start | bytes 393224 | tf_op jit(solution)/shard_map/ppermute | solution.py:207
  80.8 7.7 %collective-permute-start.28 = (f32[8,32,128]{2,1,0:T(8,128)S(1)}, f32[8,32,128]{2,1,0:T(8,128)S(1)}, u32[]{:S(2)}, u32[]{:S(2)}) collective-permute-start(f32[8,32,128]{2,1,0:T(8,128)S(1)} %get-tuple-element.26), channel_id=1, source_target_pairs={{0,6},{1,7},{2,0},{3,1},{4,2},{5,3},{6,4},{7,5},{8,14},{9,15},{10,... | collective-permute-start | bytes 393224 | tf_op jit(solution)/shard_map/ppermute | solution.py:198
  80.9 7.6 %collective-permute-start.29 = (f32[8,32,128]{2,1,0:T(8,128)S(1)}, f32[8,32,128]{2,1,0:T(8,128)S(1)}, u32[]{:S(2)}, u32[]{:S(2)}) collective-permute-start(f32[8,32,128]{2,1,0:T(8,128)S(1)} %get-tuple-element.28), channel_id=1, source_target_pairs={{0,4},{1,5},{2,6},{3,7},{4,0},{5,1},{6,2},{7,3},{8,12},{9,13},{10,... | collective-permute-start | bytes 393224 | tf_op jit(solution)/shard_map/ppermute | solution.py:198
  81.8 7.5 %collective-permute-start.30 = (f32[8,32,128]{2,1,0:T(8,128)S(1)}, f32[8,32,128]{2,1,0:T(8,128)S(1)}, u32[]{:S(2)}, u32[]{:S(2)}) collective-permute-start(f32[8,32,128]{2,1,0:T(8,128)S(1)} %get-tuple-element.27), channel_id=1, source_target_pairs={{0,2},{1,3},{2,4},{3,5},{4,6},{5,7},{6,0},{7,1},{8,10},{9,11},{10,... | collective-permute-start | bytes 393224 | tf_op jit(solution)/shard_map/ppermute | solution.py:198

commit v2 on v1

--- a/solution.py
+++ b/solution.py
@@ -10,8 +10,9 @@
 EPSILON = 1e-06
 CHIPS = 4
 VMEM = pl.BlockSpec(memory_space=pltpu.VMEM)
+ANY = pl.BlockSpec(memory_space=pl.ANY)
 SMEM = pl.BlockSpec(memory_space=pltpu.SMEM)
-BIG = pltpu.CompilerParams(vmem_limit_bytes=48 * 1024 * 1024)
+BIG = pltpu.CompilerParams(vmem_limit_bytes=24 * 1024 * 1024)
 
 
 def half_kinetic(extent, length):
@@ -130,7 +131,7 @@
     for index, ref in enumerate(chunks):
         own, slab, m = index // 8 == 0, index // 4 % 2, index % 4
         owner, rows = (chip_keep, y_keep) if own else (chip_give, y_give)
-        start = slab * (depth // 2) + lax.rem(chip - m - owner + 2 * CHIPS, CHIPS) * chunk
+        start = slab * (depth // 2) + ((chip - m - owner) & (CHIPS - 1)) * chunk
         half = at_keep if own else 1 - at_keep
         live = row_ids + half * column < live_rows
 
@@ -183,7 +184,7 @@
     for slab, kept, given in ((1, keep1, give1), (0, keep0, give0)):
         for k in range(CHIPS):
             for out, owner, rows in ((given, chip_give, y_give), (kept, chip_keep, y_keep)):
-                start = slab * (depth // 2) + lax.rem(chip + k - owner + CHIPS, CHIPS) * chunk
+                start = slab * (depth // 2) + ((chip + k - owner) & (CHIPS - 1)) * chunk
 
                 def line(i, carry, out=out, rows=rows, start=start, k=k):
                     z = start + i
@@ -202,22 +203,29 @@
     return lax.ppermute(block, "band", [(b, b ^ 1) for b in range(2 * CHIPS)])
 
 
-def to_group(block, distance):
-    n = lax.axis_size("frag")
-    return lax.ppermute(block, "frag", [(i, (i + distance) % n) for i in range(n)])
+def to_group(block, distance, k=0):
+    n, m = lax.axis_size("frag"), 2 * CHIPS
+    route = [(i * m + b, (i + distance) % n * m + (b + 2 * k) % m) for i in range(n) for b in range(m)]
+    return lax.ppermute(block, ("frag", "band"), route)
 
 
 def place(code, core):
-    low = code // 4
-    upper = (low + core) % 2
-    return (low + upper) % (2 * CHIPS) // 2, upper
-
-
-def choose(index, options):
-    out = options[0]
-    for i, option in enumerate(options[1:], 1):
-        out = jnp.where(index == i, option, out)
-    return out
+    low = code >> 2
+    upper = (low + core) & 1
+    return ((low + upper) & (2 * CHIPS - 1)) >> 1, upper
+
+
+def pick(band, code, code_before, after, *refs):
+    pieces, outs = refs[:CHIPS], refs[CHIPS:]
+    chip, core = band[0] >> 1, band[0] & 1
+    for out, order in zip(outs, (code_before, code)):
+        owner, _ = place(order[0, 0], core)
+        source = (chip - owner) & (CHIPS - 1)
+        for k, piece in enumerate(pieces):
+
+            @pl.when(source == k)
+            def _(piece=piece, out=out):
+                out[...] = piece[...]
 
 
 def body(wave_init, potential, fragment_order):
@@ -225,22 +233,16 @@
     chunk, column = depth // 2 // CHIPS, width // 2
     wave = wave_init[0, 0]
     band = lax.axis_index("band")
-    chip, core = band // 2, band % 2
+    chip, core = band >> 1, band & 1
     code = fragment_order[0, 0]
-    code_before = to_group(fragment_order, 1)[0, 0]
-    double = code % 2
+    order_before = to_group(fragment_order, 1)
+    double = code & 1
     chip_keep, at_keep = place(code, core)
     chip_give, _ = place(code, 1 - core)
-    chip_before, _ = place(code_before, core)
     scalars = jnp.stack([double, chip, chip_keep, chip_give, at_keep]).astype(jnp.int32)
 
     pieces = potential.reshape(CHIPS, chunk, column, length)
     pieces = [pieces[0]] + [to_next_chip(pieces[k], k) for k in range(1, CHIPS)]
-    below = to_group(choose((chip - chip_before) % CHIPS, pieces), -1)
-    here = choose((chip - chip_keep) % CHIPS, pieces)
-    own = [here] + [to_next_chip(here, k) for k in range(1, CHIPS)]
-    own += [below] + [to_next_chip(below, k) for k in range(1, CHIPS)]
-    other = [to_other_core(p) for p in own]
 
     x_op, z_op, y_op = operators(depth, width, length)
     box = jax.ShapeDtypeStruct((depth, width, length), jnp.float32)
@@ -251,8 +253,22 @@
         out_specs=VMEM,
         scratch_shapes=[pltpu.VMEM(box.shape, jnp.float32)],
         compiler_params=BIG,
+        cost_estimate=pl.CostEstimate(flops=5_000_000_000, bytes_accessed=4_000_000, transcendentals=0),
         name="first_kinetic",
     )(scalars, wave, x_op, z_op, y_op)
+    piece = jax.ShapeDtypeStruct((chunk, column, length), jnp.float32)
+    below, here = pl.pallas_call(
+        pick,
+        out_shape=[piece] * 2,
+        in_specs=[SMEM] * 3 + [ANY] + [VMEM] * CHIPS,
+        out_specs=[VMEM] * 2,
+        compiler_params=pltpu.CompilerParams(vmem_limit_bytes=4 * 1024 * 1024),
+        name="pick",
+    )(band[None].astype(jnp.int32), fragment_order, order_before, kinetic, *pieces)
+    below = to_group(below, -1)
+    own = [here] + [to_next_chip(here, k) for k in range(1, CHIPS)]
+    own += [below] + [to_next_chip(below, k) for k in range(1, CHIPS)]
+    other = [to_other_core(p) for p in own]
     quarter = jax.ShapeDtypeStruct((CHIPS, chunk, column, length), jnp.float32)
     keep0, give0, keep1, give1 = pl.pallas_call(
         second_step,
@@ -273,9 +289,10 @@
 
     above = to_group(reduce_chip(keep1, give1), 1)
     here = reduce_chip(keep0, give0)
+    chip_before, _ = place(order_before[0, 0], core)
     sends = []
     for k in range(CHIPS):
-        target = (chip + k) % CHIPS
+        target = (chip + k) & (CHIPS - 1)
         sends.append(jnp.where(target == chip_keep, here, 0.0) + jnp.where(target == chip_before, above, 0.0))
     final = [sends[0]] + [to_next_chip(sends[k], k) for k in range(CHIPS - 1, 0, -1)]
     return jnp.concatenate(final, axis=0)

time: 90.8 us -> 84.5 us (0.931)
  waiting for transfers between devices: 35.9 us -> 27 us
  starting transfers between devices: 29.2 us -> 34.4 us
  between operations: 3.66 us -> 1.53 us
  other arithmetic: 2.08 us -> 1.13 us
    ppermute x3, waiting for transfers between devices: 12.2 us -> 4.78 us  [to_group(): return lax.ppermute(block, ('frag', 'band'), route)]
    ppermute x3, starting transfers between devices: 3.67 us -> 8.12 us  [to_group(): return lax.ppermute(block, ('frag', 'band'), route)]
    ppermute x18, waiting for transfers between devices: 22.3 us -> 19.5 us  [to_next_chip(): lax.ppermute(block, 'band', [(b, (b + 2 * k) % (2 * CHIPS)) for b in rang...]
    pallas_call x1, Pallas kernels: 9.92 us -> 8.59 us  [body(): pl.pallas_call(second_step, out_shape=[quarter] * 4, in_specs=[SMEM] + [V...]
    ppermute x10, waiting for transfers between devices: 1.42 us -> 2.66 us  [to_other_core(): return lax.ppermute(block, 'band', [(b, b ^ 1) for b in range(2 * CHIPS)])]
    select_n x1 -> x0, other arithmetic: 0.95 us -> none  [choose(): out = jnp.where(index == i, option, out)]
    unnamed x10 -> x8, local copies, waits for them, and re-layouts: 3.43 us -> 4.33 us
  transfers between devices with their start and end apart: 31 -> 31, of which waited for: 13 -> 15; matrix products, arithmetic and copies ran while one was open for 0% -> 0% of each run, Pallas kernels for 5% -> 6%
where the time goes in v2:
time: 84.5 us; the launch traced here: 83.5 us
  starting transfers between devices  34.4 us (41%)
  waiting for transfers between devices  27 us (32%)
  Pallas kernels  13.9 us (16%)
  local copies, waits for them, and re-layouts  5.6 us (7%)
  between operations  1.53 us (2%)
  other arithmetic  1.13 us (1%)
    ppermute x18, starting transfers between devices, to_next_chip(): lax.ppermute(block, 'band', [(b, (b + 2 * k) % (2 * CHIPS)) for b in rang...  24.4 us
    ppermute x18, waiting for transfers between devices, to_next_chip(): lax.ppermute(block, 'band', [(b, (b + 2 * k) % (2 * CHIPS)) for b in rang...  19.5 us
    pallas_call x1, Pallas kernels, body(): pl.pallas_call(second_step, out_shape=[quarter] * 4, in_specs=[SMEM] + [V...  8.59 us
    ppermute x3, starting transfers between devices, to_group(): return lax.ppermute(block, ('frag', 'band'), route)  8.12 us
    ppermute x3, waiting for transfers between devices, to_group(): return lax.ppermute(block, ('frag', 'band'), route)  4.78 us
    pallas_call x1, Pallas kernels, body(): pl.pallas_call(first_kinetic, out_shape=box, in_specs=[SMEM] + [VMEM] * 4...  4.64 us
    unnamed x8, local copies, waits for them, and re-layouts  4.33 us
    ppermute x10, waiting for transfers between devices, to_other_core(): return lax.ppermute(block, 'band', [(b, b ^ 1) for b in range(2 * CHIPS)])  2.66 us
  transfers between devices with their start and end apart: 31, of which 15 were waited for; matrix products, arithmetic and copies ran while one was open for 0% of the time, Pallas kernels for 6%

profile of v2, /device:TPU:24, one launch (start us, length us, event | category | flops | bytes accessed | tf_op | source)
XLA Modules:
  0.0 83.5 jit_solution(2305375455440296566)
XLA Ops:
  0.0 1.1 %fusion.7 = (f32[8,32,128]{2,1,0:T(8,128)S(1)}, f32[8,32,128]{2,1,0:T(8,128)S(1)}, f32[8,32,128]{2,1,0:T(8,128)S(1)}, f32[8,32,128]{2,1,0:T(8,128)S(1)}) fusion(f32[32,32,128]{2,1,0:T(8,128)} %param.7), kind=kLoop, calls=%fused_computation.19 | loop fusion | bytes 1048576 | tf_op jit(solution)/shard_map/slice | solution.py:245
  1.1 2.0 %collective-permute-start.1 = (f32[8,32,128]{2,1,0:T(8,128)S(1)}, f32[8,32,128]{2,1,0:T(8,128)S(1)}, u32[]{:S(2)}, u32[]{:S(2)}) collective-permute-start(f32[8,32,128]{2,1,0:T(8,128)S(1)} %get-tuple-element.26), channel_id=1, source_target_pairs={{0,2},{1,3},{2,4},{3,5},{4,6},{5,7},{6,0},{7,1},{8,10},{9,11},{10,... | collective-permute-start | bytes 393224 | tf_op jit(solution)/shard_map/ppermute | solution.py:199
  3.2 0.9 %collective-permute-start.2 = (f32[8,32,128]{2,1,0:T(8,128)S(1)}, f32[8,32,128]{2,1,0:T(8,128)S(1)}, u32[]{:S(2)}, u32[]{:S(2)}) collective-permute-start(f32[8,32,128]{2,1,0:T(8,128)S(1)} %get-tuple-element.28), channel_id=1, source_target_pairs={{0,4},{1,5},{2,6},{3,7},{4,0},{5,1},{6,2},{7,3},{8,12},{9,13},{10,... | collective-permute-start | bytes 393224 | tf_op jit(solution)/shard_map/ppermute | solution.py:199
  4.0 0.1 collective-permute-start.3
  4.1 1.4 %collective-permute-start = (s32[1,1]{1,0:T(1,128)}, s32[1,1]{1,0:T(1,128)}, u32[]{:S(2)}, u32[]{:S(2)}) collective-permute-start(s32[1,1]{1,0:T(1,128)} %param.8), channel_id=1, source_target_pairs={{0,8},{1,9},{2,10},{3,11},{4,12},{5,13},{6,14},{7,15},{8,16},{9,17... | collective-permute-start | bytes 20 | tf_op jit(solution)/shard_map/ppermute | solution.py:209
  6.3 1.2 %copy-done = bf16[1,1,64,64,128]{4,3,2,1,0:T(8,128)(2,1)S(1)} copy-done((bf16[1,1,64,64,128]{4,3,2,1,0:T(8,128)(2,1)S(1)}, bf16[1,1,64,64,128]{4,3,2,1,0:T(8,128)(2,1)}, u32[]{:S(2)}) %copy-start) | copy-done | bytes 1048600
  7.5 1.2 %copy-done.1 = bf16[2,512,512]{2,1,0:T(8,128)(2,1)S(1)} copy-done((bf16[2,512,512]{2,1,0:T(8,128)(2,1)S(1)}, bf16[2,512,512]{2,1,0:T(8,128)(2,1)}, u32[]{:S(2)}) %copy-start.1) | copy-done | bytes 1048600
  8.8 1.0 %copy-done.2 = bf16[2,2,256,256]{3,2,1,0:T(8,128)(2,1)S(1)} copy-done((bf16[2,2,256,256]{3,2,1,0:T(8,128)(2,1)S(1)}, bf16[2,2,256,256]{3,2,1,0:T(8,128)(2,1)}, u32[]{:S(2)}) %copy-start.2) | copy-done | bytes 524312
  9.8 0.8 %copy-done.3 = bf16[2,128,128]{2,1,0:T(8,128)(2,1)S(1)} copy-done((bf16[2,128,128]{2,1,0:T(8,128)(2,1)S(1)}, bf16[2,128,128]{2,1,0:T(8,128)(2,1)}, u32[]{:S(2)}) %copy-start.3) | copy-done | bytes 65560
  10.6 4.6 %first_kinetic.1.after.kinetic = f32[64,64,128]{2,1,0:T(8,128)S(1)} custom-call(s32[5]{0:T(128)S(1)} %stack.50.scalars, bf16[64,64,128]{2,1,0:T(8,128)(2,1)S(1)} %bitcast.38, bf16[2,128,128]{2,1,0:T(8,128)(2,1)S(1)} %copy-done.3, bf16[2,512,512]{2,1,0:T(8,128)(2,1)S(1)} %copy-done.1, bf16[2,2,256,256]{3,2,1,0:T(8,128)(2,1)S(1)} %copy-done.2), custom_call_target="tpu_custom_call" | custom-call | flops 5000000000 | bytes 4000000 | tf_op jit(solution)/shard_map/first_kinetic/pallas_call | solution.py:249
  15.3 0.7 pick.1
  16.0 6.6 %collective-permute-start.7 = (f32[8,32,128]{2,1,0:T(8,128)S(1)}, f32[8,32,128]{2,1,0:T(8,128)S(1)}, u32[]{:S(2)}, u32[]{:S(2)}) collective-permute-start(f32[8,32,128]{2,1,0:T(8,128)S(1)} %get-tuple-element.12), channel_id=1, source_target_pairs={{0,248},{1,249},{2,250},{3,251},{4,252},{5,253},{6,254},{7,255},{8... | collective-permute-start | bytes 393224 | tf_op jit(solution)/shard_map/ppermute | solution.py:209
  22.7 3.2 %collective-permute-start.4 = (f32[8,32,128]{2,1,0:T(8,128)S(1)}, f32[8,32,128]{2,1,0:T(8,128)S(1)}, u32[]{:S(2)}, u32[]{:S(2)}) collective-permute-start(f32[8,32,128]{2,1,0:T(8,128)S(1)} %get-tuple-element.11.refs_0_), channel_id=1, source_target_pairs={{0,2},{1,3},{2,4},{3,5},{4,6},{5,7},{6,0},{7,1},{8,10},{9,11},{10,... | collective-permute-start | bytes 393224 | tf_op jit(solution)/shard_map/ppermute | solution.py:199
  25.9 0.1 collective-permute-start.5
  26.0 1.4 %collective-permute-start.6 = (f32[8,32,128]{2,1,0:T(8,128)S(1)}, f32[8,32,128]{2,1,0:T(8,128)S(1)}, u32[]{:S(2)}, u32[]{:S(2)}) collective-permute-start(f32[8,32,128]{2,1,0:T(8,128)S(1)} %get-tuple-element.11.refs_0_), channel_id=1, source_target_pairs={{0,6},{1,7},{2,0},{3,1},{4,2},{5,3},{6,4},{7,5},{8,14},{9,15},{10,... | collective-permute-start | bytes 393224 | tf_op jit(solution)/shard_map/ppermute | solution.py:199
  27.4 1.8 %collective-permute-start.8 = (f32[8,32,128]{2,1,0:T(8,128)S(1)}, f32[8,32,128]{2,1,0:T(8,128)S(1)}, u32[]{:S(2)}, u32[]{:S(2)}) collective-permute-start(f32[8,32,128]{2,1,0:T(8,128)S(1)} %collective-permute-done.7.refs_4_), channel_id=1, source_target_pairs={{0,2},{1,3},{2,4},{3,5},{4,6},{5,7},{6,0},{7,1},{8,10},{9,11},{10,... | collective-permute-start | bytes 393224 | tf_op jit(solution)/shard_map/ppermute | solution.py:199
  29.3 1.5 %collective-permute-done.4.refs_1_ = f32[8,32,128]{2,1,0:T(8,128)S(1)} collective-permute-done((f32[8,32,128]{2,1,0:T(8,128)S(1)}, f32[8,32,128]{2,1,0:T(8,128)S(1)}, u32[]{:S(2)}, u32[]{:S(2)}) %collective-permute-start.4) | collective-permute-done | bytes 131104 | tf_op jit(solution)/shard_map/ppermute | solution.py:199
  30.7 0.8 collective-permute-start.9
  31.5 1.3 %collective-permute-done.5.refs_2_ = f32[8,32,128]{2,1,0:T(8,128)S(1)} collective-permute-done((f32[8,32,128]{2,1,0:T(8,128)S(1)}, f32[8,32,128]{2,1,0:T(8,128)S(1)}, u32[]{:S(2)}, u32[]{:S(2)}) %collective-permute-start.5) | collective-permute-done | bytes 131104 | tf_op jit(solution)/shard_map/ppermute | solution.py:199
  32.8 2.6 %collective-permute-start.10 = (f32[8,32,128]{2,1,0:T(8,128)S(1)}, f32[8,32,128]{2,1,0:T(8,128)S(1)}, u32[]{:S(2)}, u32[]{:S(2)}) collective-permute-start(f32[8,32,128]{2,1,0:T(8,128)S(1)} %collective-permute-done.7.refs_4_), channel_id=1, source_target_pairs={{0,6},{1,7},{2,0},{3,1},{4,2},{5,3},{6,4},{7,5},{8,14},{9,15},{10,... | collective-permute-start | bytes 393224 | tf_op jit(solution)/shard_map/ppermute | solution.py:199
  35.5 0.5 collective-permute-start.13
  36.0 0.1 collective-permute-start.15
  36.1 2.3 %collective-permute-done.9.refs_6_ = f32[8,32,128]{2,1,0:T(8,128)S(1)} collective-permute-done((f32[8,32,128]{2,1,0:T(8,128)S(1)}, f32[8,32,128]{2,1,0:T(8,128)S(1)}, u32[]{:S(2)}, u32[]{:S(2)}) %collective-permute-start.9) | collective-permute-done | bytes 131104 | tf_op jit(solution)/shard_map/ppermute | solution.py:199
  38.4 1.4 %collective-permute-done.10.refs_7_ = f32[8,32,128]{2,1,0:T(8,128)S(1)} collective-permute-done((f32[8,32,128]{2,1,0:T(8,128)S(1)}, f32[8,32,128]{2,1,0:T(8,128)S(1)}, u32[]{:S(2)}, u32[]{:S(2)}) %collective-permute-start.10) | collective-permute-done | bytes 131104 | tf_op jit(solution)/shard_map/ppermute | solution.py:199
  39.8 0.5 collective-permute-start.17
  40.3 0.1 collective-permute-start.18
  40.4 0.7 collective-permute-done.16.refs_13_
  41.1 0.2 collective-permute-done.17.refs_14_
  41.3 0.3 collective-permute-done.18.refs_15_
  41.6 8.6 %second_step.1 = (f32[4,8,32,128]{3,2,1,0:T(8,128)S(1)}, f32[4,8,32,128]{3,2,1,0:T(8,128)S(1)}, f32[4,8,32,128]{3,2,1,0:T(8,128)S(1)}, f32[4,8,32,128]{3,2,1,0:T(8,128)S(1)}) custom-call(s32[5]{0:T(128)S(1)} %stack.50.scalars, bf16[64,64,128]{2,1,0:T(8,128)(2,1)S(1)} %bitcast.39, f32[64,64,128]{2,1,0:T(8,128)S(1)} %first_kinetic.1.after.kinetic, ...), custom_call_target="tpu_custom_call" | custom-call | tf_op jit(solution)/shard_map/second_step/pallas_call | solution.py:273
  50.2 0.3 collective-permute-start.23
  50.5 0.3 collective-permute-start.19
  50.8 1.4 %collective-permute-done.23 = f32[4,8,32,128]{3,2,1,0:T(8,128)S(1)} collective-permute-done((f32[4,8,32,128]{3,2,1,0:T(8,128)S(1)}, f32[4,8,32,128]{3,2,1,0:T(8,128)S(1)}, u32[]{:S(2)}, u32[]{:S(2)}) %collective-permute-start.23) | collective-permute-done | bytes 524320 | tf_op jit(solution)/shard_map/ppermute | solution.py:203
  52.3 1.6 %collective-permute-start.24 = (f32[8,32,128]{2,1,0:T(8,128)S(1)}, f32[8,32,128]{2,1,0:T(8,128)S(1)}, u32[]{:S(2)}, u32[]{:S(2)}) collective-permute-start(f32[8,32,128]{2,1,0:T(8,128)S(1)} %get-tuple-element.22), channel_id=1, source_target_pairs={{0,2},{1,3},{2,4},{3,5},{4,6},{5,7},{6,0},{7,1},{8,10},{9,11},{10,... | collective-permute-start | bytes 393224 | tf_op jit(solution)/shard_map/ppermute | solution.py:199
  54.0 1.2 %collective-permute-start.25 = (f32[8,32,128]{2,1,0:T(8,128)S(1)}, f32[8,32,128]{2,1,0:T(8,128)S(1)}, u32[]{:S(2)}, u32[]{:S(2)}) collective-permute-start(f32[8,32,128]{2,1,0:T(8,128)S(1)} %get-tuple-element.24), channel_id=1, source_target_pairs={{0,4},{1,5},{2,6},{3,7},{4,0},{5,1},{6,2},{7,3},{8,12},{9,13},{10,... | collective-permute-start | bytes 393224 | tf_op jit(solution)/shard_map/ppermute | solution.py:199
  55.3 3.3 %collective-permute-start.20 = (f32[8,32,128]{2,1,0:T(8,128)S(1)}, f32[8,32,128]{2,1,0:T(8,128)S(1)}, u32[]{:S(2)}, u32[]{:S(2)}) collective-permute-start(f32[8,32,128]{2,1,0:T(8,128)S(1)} %get-tuple-element.19), channel_id=1, source_target_pairs={{0,2},{1,3},{2,4},{3,5},{4,6},{5,7},{6,0},{7,1},{8,10},{9,11},{10,... | collective-permute-start | bytes 393224 | tf_op jit(solution)/shard_map/ppermute | solution.py:199
  58.6 1.2 %collective-permute-start.21 = (f32[8,32,128]{2,1,0:T(8,128)S(1)}, f32[8,32,128]{2,1,0:T(8,128)S(1)}, u32[]{:S(2)}, u32[]{:S(2)}) collective-permute-start(f32[8,32,128]{2,1,0:T(8,128)S(1)} %get-tuple-element.21), channel_id=1, source_target_pairs={{0,4},{1,5},{2,6},{3,7},{4,0},{5,1},{6,2},{7,3},{8,12},{9,13},{10,... | collective-permute-start | bytes 393224 | tf_op jit(solution)/shard_map/ppermute | solution.py:199
  59.7 0.5 collective-permute-start.22
  60.2 1.7 %collective-permute-done.25 = f32[8,32,128]{2,1,0:T(8,128)S(1)} collective-permute-done((f32[8,32,128]{2,1,0:T(8,128)S(1)}, f32[8,32,128]{2,1,0:T(8,128)S(1)}, u32[]{:S(2)}, u32[]{:S(2)}) %collective-permute-start.25) | collective-permute-done | bytes 131104 | tf_op jit(solution)/shard_map/ppermute | solution.py:199
  61.9 3.8 %collective-permute-done.26 = f32[8,32,128]{2,1,0:T(8,128)S(1)} collective-permute-done((f32[8,32,128]{2,1,0:T(8,128)S(1)}, f32[8,32,128]{2,1,0:T(8,128)S(1)}, u32[]{:S(2)}, u32[]{:S(2)}) %collective-permute-start.26) | collective-permute-done | bytes 131104 | tf_op jit(solution)/shard_map/ppermute | solution.py:199
  66.5 1.0 %collective-permute-done.21 = f32[8,32,128]{2,1,0:T(8,128)S(1)} collective-permute-done((f32[8,32,128]{2,1,0:T(8,128)S(1)}, f32[8,32,128]{2,1,0:T(8,128)S(1)}, u32[]{:S(2)}, u32[]{:S(2)}) %collective-permute-start.21) | collective-permute-done | bytes 131104 | tf_op jit(solution)/shard_map/ppermute | solution.py:199
  67.5 1.8 %collective-permute-done.22 = f32[8,32,128]{2,1,0:T(8,128)S(1)} collective-permute-done((f32[8,32,128]{2,1,0:T(8,128)S(1)}, f32[8,32,128]{2,1,0:T(8,128)S(1)}, u32[]{:S(2)}, u32[]{:S(2)}) %collective-permute-start.22) | collective-permute-done | bytes 131104 | tf_op jit(solution)/shard_map/ppermute | solution.py:199
  69.3 4.8 %collective-permute-done.27 = f32[8,32,128]{2,1,0:T(8,128)S(1)} collective-permute-done((f32[8,32,128]{2,1,0:T(8,128)S(1)}, f32[8,32,128]{2,1,0:T(8,128)S(1)}, u32[]{:S(2)}, u32[]{:S(2)}) %collective-permute-start.27) | collective-permute-done | bytes 131104 | tf_op jit(solution)/shard_map/ppermute | solution.py:209
  74.3 1.1 %collective-permute-start.29 = (f32[8,32,128]{2,1,0:T(8,128)S(1)}, f32[8,32,128]{2,1,0:T(8,128)S(1)}, u32[]{:S(2)}, u32[]{:S(2)}) collective-permute-start(f32[8,32,128]{2,1,0:T(8,128)S(1)} %get-tuple-element.31), channel_id=1, source_target_pairs={{0,4},{1,5},{2,6},{3,7},{4,0},{5,1},{6,2},{7,3},{8,12},{9,13},{10,... | collective-permute-start | bytes 393224 | tf_op jit(solution)/shard_map/ppermute | solution.py:199
  75.3 2.5 %collective-permute-start.30 = (f32[8,32,128]{2,1,0:T(8,128)S(1)}, f32[8,32,128]{2,1,0:T(8,128)S(1)}, u32[]{:S(2)}, u32[]{:S(2)}) collective-permute-start(f32[8,32,128]{2,1,0:T(8,128)S(1)} %get-tuple-element.30), channel_id=1, source_target_pairs={{0,2},{1,3},{2,4},{3,5},{4,6},{5,7},{6,0},{7,1},{8,10},{9,11},{10,... | collective-permute-start | bytes 393224 | tf_op jit(solution)/shard_map/ppermute | solution.py:199
  77.9 4.0 %collective-permute-done.28 = f32[8,32,128]{2,1,0:T(8,128)S(1)} collective-permute-done((f32[8,32,128]{2,1,0:T(8,128)S(1)}, f32[8,32,128]{2,1,0:T(8,128)S(1)}, u32[]{:S(2)}, u32[]{:S(2)}) %collective-permute-start.28) | collective-permute-done | bytes 131104 | tf_op jit(solution)/shard_map/ppermute | solution.py:199
  81.8 0.9 %collective-permute-done.30 = f32[8,32,128]{2,1,0:T(8,128)S(1)} collective-permute-done((f32[8,32,128]{2,1,0:T(8,128)S(1)}, f32[8,32,128]{2,1,0:T(8,128)S(1)}, u32[]{:S(2)}, u32[]{:S(2)}) %collective-permute-start.30) | collective-permute-done | bytes 131104 | tf_op jit(solution)/shard_map/ppermute | solution.py:199
  82.7 0.8 pad_maximum_fusion
  (35 shorter events, 0.7 us)
Async XLA Ops:
  1.1 14.2 %collective-permute-start.1 = (f32[8,32,128]{2,1,0:T(8,128)S(1)}, f32[8,32,128]{2,1,0:T(8,128)S(1)}, u32[]{:S(2)}, u32[]{:S(2)}) collective-permute-start(f32[8,32,128]{2,1,0:T(8,128)S(1)} %get-tuple-element.26), channel_id=1, source_target_pairs={{0,2},{1,3},{2,4},{3,5},{4,6},{5,7},{6,0},{7,1},{8,10},{9,11},{10,... | collective-permute-start | bytes 393224 | tf_op jit(solution)/shard_map/ppermute | solution.py:199
  3.2 12.1 %collective-permute-start.2 = (f32[8,32,128]{2,1,0:T(8,128)S(1)}, f32[8,32,128]{2,1,0:T(8,128)S(1)}, u32[]{:S(2)}, u32[]{:S(2)}) collective-permute-start(f32[8,32,128]{2,1,0:T(8,128)S(1)} %get-tuple-element.28), channel_id=1, source_target_pairs={{0,4},{1,5},{2,6},{3,7},{4,0},{5,1},{6,2},{7,3},{8,12},{9,13},{10,... | collective-permute-start | bytes 393224 | tf_op jit(solution)/shard_map/ppermute | solution.py:199
  4.0 11.3 %collective-permute-start.3 = (f32[8,32,128]{2,1,0:T(8,128)S(1)}, f32[8,32,128]{2,1,0:T(8,128)S(1)}, u32[]{:S(2)}, u32[]{:S(2)}) collective-permute-start(f32[8,32,128]{2,1,0:T(8,128)S(1)} %get-tuple-element.25), channel_id=1, source_target_pairs={{0,6},{1,7},{2,0},{3,1},{4,2},{5,3},{6,4},{7,5},{8,14},{9,15},{10,... | collective-permute-start | bytes 393224 | tf_op jit(solution)/shard_map/ppermute | solution.py:199
  4.1 11.2 %collective-permute-start = (s32[1,1]{1,0:T(1,128)}, s32[1,1]{1,0:T(1,128)}, u32[]{:S(2)}, u32[]{:S(2)}) collective-permute-start(s32[1,1]{1,0:T(1,128)} %param.8), channel_id=1, source_target_pairs={{0,8},{1,9},{2,10},{3,11},{4,12},{5,13},{6,14},{7,15},{8,16},{9,17... | collective-permute-start | bytes 20 | tf_op jit(solution)/shard_map/ppermute | solution.py:209
  6.3 1.2 %copy-start = (bf16[1,1,64,64,128]{4,3,2,1,0:T(8,128)(2,1)S(1)}, bf16[1,1,64,64,128]{4,3,2,1,0:T(8,128)(2,1)}, u32[]{:S(2)}) copy-start(bf16[1,1,64,64,128]{4,3,2,1,0:T(8,128)(2,1)} %param.6) | copy-start | bytes 3145732
  7.5 1.2 %copy-start.1 = (bf16[2,512,512]{2,1,0:T(8,128)(2,1)S(1)}, bf16[2,512,512]{2,1,0:T(8,128)(2,1)}, u32[]{:S(2)}) copy-start(bf16[2,512,512]{2,1,0:T(8,128)(2,1)} %constant.43.z_ref) | copy-start | bytes 3145732
  8.8 1.0 %copy-start.2 = (bf16[2,2,256,256]{3,2,1,0:T(8,128)(2,1)S(1)}, bf16[2,2,256,256]{3,2,1,0:T(8,128)(2,1)}, u32[]{:S(2)}) copy-start(bf16[2,2,256,256]{3,2,1,0:T(8,128)(2,1)} %constant.50.y_ref) | copy-start | bytes 1572868
  9.8 0.8 %copy-start.3 = (bf16[2,128,128]{2,1,0:T(8,128)(2,1)S(1)}, bf16[2,128,128]{2,1,0:T(8,128)(2,1)}, u32[]{:S(2)}) copy-start(bf16[2,128,128]{2,1,0:T(8,128)(2,1)} %constant.36.x_ref) | copy-start | bytes 196612
  16.0 11.4 %collective-permute-start.7 = (f32[8,32,128]{2,1,0:T(8,128)S(1)}, f32[8,32,128]{2,1,0:T(8,128)S(1)}, u32[]{:S(2)}, u32[]{:S(2)}) collective-permute-start(f32[8,32,128]{2,1,0:T(8,128)S(1)} %get-tuple-element.12), channel_id=1, source_target_pairs={{0,248},{1,249},{2,250},{3,251},{4,252},{5,253},{6,254},{7,255},{8... | collective-permute-start | bytes 393224 | tf_op jit(solution)/shard_map/ppermute | solution.py:209
  22.7 8.1 %collective-permute-start.4 = (f32[8,32,128]{2,1,0:T(8,128)S(1)}, f32[8,32,128]{2,1,0:T(8,128)S(1)}, u32[]{:S(2)}, u32[]{:S(2)}) collective-permute-start(f32[8,32,128]{2,1,0:T(8,128)S(1)} %get-tuple-element.11.refs_0_), channel_id=1, source_target_pairs={{0,2},{1,3},{2,4},{3,5},{4,6},{5,7},{6,0},{7,1},{8,10},{9,11},{10,... | collective-permute-start | bytes 393224 | tf_op jit(solution)/shard_map/ppermute | solution.py:199
  25.9 6.9 %collective-permute-start.5 = (f32[8,32,128]{2,1,0:T(8,128)S(1)}, f32[8,32,128]{2,1,0:T(8,128)S(1)}, u32[]{:S(2)}, u32[]{:S(2)}) collective-permute-start(f32[8,32,128]{2,1,0:T(8,128)S(1)} %get-tuple-element.11.refs_0_), channel_id=1, source_target_pairs={{0,4},{1,5},{2,6},{3,7},{4,0},{5,1},{6,2},{7,3},{8,12},{9,13},{10,... | collective-permute-start | bytes 393224 | tf_op jit(solution)/shard_map/ppermute | solution.py:199
  26.0 9.4 %collective-permute-start.6 = (f32[8,32,128]{2,1,0:T(8,128)S(1)}, f32[8,32,128]{2,1,0:T(8,128)S(1)}, u32[]{:S(2)}, u32[]{:S(2)}) collective-permute-start(f32[8,32,128]{2,1,0:T(8,128)S(1)} %get-tuple-element.11.refs_0_), channel_id=1, source_target_pairs={{0,6},{1,7},{2,0},{3,1},{4,2},{5,3},{6,4},{7,5},{8,14},{9,15},{10,... | collective-permute-start | bytes 393224 | tf_op jit(solution)/shard_map/ppermute | solution.py:199
  27.4 8.0 %collective-permute-start.11 = (f32[8,32,128]{2,1,0:T(8,128)S(1)}, f32[8,32,128]{2,1,0:T(8,128)S(1)}, u32[]{:S(2)}, u32[]{:S(2)}) collective-permute-start(f32[8,32,128]{2,1,0:T(8,128)S(1)} %get-tuple-element.11.refs_0_), channel_id=1, source_target_pairs={{0,1},{1,0},{2,3},{3,2},{4,5},{5,4},{6,7},{7,6},{8,9},{9,8},{10,11... | collective-permute-start | bytes 393224 | tf_op jit(solution)/shard_map/ppermute | solution.py:203
  27.4 8.5 %collective-permute-start.8 = (f32[8,32,128]{2,1,0:T(8,128)S(1)}, f32[8,32,128]{2,1,0:T(8,128)S(1)}, u32[]{:S(2)}, u32[]{:S(2)}) collective-permute-start(f32[8,32,128]{2,1,0:T(8,128)S(1)} %collective-permute-done.7.refs_4_), channel_id=1, source_target_pairs={{0,2},{1,3},{2,4},{3,5},{4,6},{5,7},{6,0},{7,1},{8,10},{9,11},{10,... | collective-permute-start | bytes 393224 | tf_op jit(solution)/shard_map/ppermute | solution.py:199
  30.7 7.6 %collective-permute-start.9 = (f32[8,32,128]{2,1,0:T(8,128)S(1)}, f32[8,32,128]{2,1,0:T(8,128)S(1)}, u32[]{:S(2)}, u32[]{:S(2)}) collective-permute-start(f32[8,32,128]{2,1,0:T(8,128)S(1)} %collective-permute-done.7.refs_4_), channel_id=1, source_target_pairs={{0,4},{1,5},{2,6},{3,7},{4,0},{5,1},{6,2},{7,3},{8,12},{9,13},{10,... | collective-permute-start | bytes 393224 | tf_op jit(solution)/shard_map/ppermute | solution.py:199
  32.8 7.0 %collective-permute-start.10 = (f32[8,32,128]{2,1,0:T(8,128)S(1)}, f32[8,32,128]{2,1,0:T(8,128)S(1)}, u32[]{:S(2)}, u32[]{:S(2)}) collective-permute-start(f32[8,32,128]{2,1,0:T(8,128)S(1)} %collective-permute-done.7.refs_4_), channel_id=1, source_target_pairs={{0,6},{1,7},{2,0},{3,1},{4,2},{5,3},{6,4},{7,5},{8,14},{9,15},{10,... | collective-permute-start | bytes 393224 | tf_op jit(solution)/shard_map/ppermute | solution.py:199
  35.4 4.3 %collective-permute-start.12 = (f32[8,32,128]{2,1,0:T(8,128)S(1)}, f32[8,32,128]{2,1,0:T(8,128)S(1)}, u32[]{:S(2)}, u32[]{:S(2)}) collective-permute-start(f32[8,32,128]{2,1,0:T(8,128)S(1)} %collective-permute-done.4.refs_1_), channel_id=1, source_target_pairs={{0,1},{1,0},{2,3},{3,2},{4,5},{5,4},{6,7},{7,6},{8,9},{9,8},{10,11... | collective-permute-start | bytes 393224 | tf_op jit(solution)/shard_map/ppermute | solution.py:203
  35.5 4.8 %collective-permute-start.13 = (f32[8,32,128]{2,1,0:T(8,128)S(1)}, f32[8,32,128]{2,1,0:T(8,128)S(1)}, u32[]{:S(2)}, u32[]{:S(2)}) collective-permute-start(f32[8,32,128]{2,1,0:T(8,128)S(1)} %collective-permute-done.5.refs_2_), channel_id=1, source_target_pairs={{0,1},{1,0},{2,3},{3,2},{4,5},{5,4},{6,7},{7,6},{8,9},{9,8},{10,11... | collective-permute-start | bytes 393224 | tf_op jit(solution)/shard_map/ppermute | solution.py:203
  36.0 4.4 %collective-permute-start.15 = (f32[8,32,128]{2,1,0:T(8,128)S(1)}, f32[8,32,128]{2,1,0:T(8,128)S(1)}, u32[]{:S(2)}, u32[]{:S(2)}) collective-permute-start(f32[8,32,128]{2,1,0:T(8,128)S(1)} %collective-permute-done.7.refs_4_), channel_id=1, source_target_pairs={{0,1},{1,0},{2,3},{3,2},{4,5},{5,4},{6,7},{7,6},{8,9},{9,8},{10,11... | collective-permute-start | bytes 393224 | tf_op jit(solution)/shard_map/ppermute | solution.py:203
  38.4 2.0 %collective-permute-start.14 = (f32[8,32,128]{2,1,0:T(8,128)S(1)}, f32[8,32,128]{2,1,0:T(8,128)S(1)}, u32[]{:S(2)}, u32[]{:S(2)}) collective-permute-start(f32[8,32,128]{2,1,0:T(8,128)S(1)} %collective-permute-done.6.refs_3_), channel_id=1, source_target_pairs={{0,1},{1,0},{2,3},{3,2},{4,5},{5,4},{6,7},{7,6},{8,9},{9,8},{10,11... | collective-permute-start | bytes 393224 | tf_op jit(solution)/shard_map/ppermute | solution.py:203
  39.8 1.3 %collective-permute-start.16 = (f32[8,32,128]{2,1,0:T(8,128)S(1)}, f32[8,32,128]{2,1,0:T(8,128)S(1)}, u32[]{:S(2)}, u32[]{:S(2)}) collective-permute-start(f32[8,32,128]{2,1,0:T(8,128)S(1)} %collective-permute-done.8.refs_5_), channel_id=1, source_target_pairs={{0,1},{1,0},{2,3},{3,2},{4,5},{5,4},{6,7},{7,6},{8,9},{9,8},{10,11... | collective-permute-start | bytes 393224 | tf_op jit(solution)/shard_map/ppermute | solution.py:203
  39.8 1.5 %collective-permute-start.17 = (f32[8,32,128]{2,1,0:T(8,128)S(1)}, f32[8,32,128]{2,1,0:T(8,128)S(1)}, u32[]{:S(2)}, u32[]{:S(2)}) collective-permute-start(f32[8,32,128]{2,1,0:T(8,128)S(1)} %collective-permute-done.9.refs_6_), channel_id=1, source_target_pairs={{0,1},{1,0},{2,3},{3,2},{4,5},{5,4},{6,7},{7,6},{8,9},{9,8},{10,11... | collective-permute-start | bytes 393224 | tf_op jit(solution)/shard_map/ppermute | solution.py:203
  40.3 1.3 %collective-permute-start.18 = (f32[8,32,128]{2,1,0:T(8,128)S(1)}, f32[8,32,128]{2,1,0:T(8,128)S(1)}, u32[]{:S(2)}, u32[]{:S(2)}) collective-permute-start(f32[8,32,128]{2,1,0:T(8,128)S(1)} %collective-permute-done.10.refs_7_), channel_id=1, source_target_pairs={{0,1},{1,0},{2,3},{3,2},{4,5},{5,4},{6,7},{7,6},{8,9},{9,8},{10,11... | collective-permute-start | bytes 393224 | tf_op jit(solution)/shard_map/ppermute | solution.py:203
  50.2 2.0 %collective-permute-start.23 = (f32[4,8,32,128]{3,2,1,0:T(8,128)S(1)}, f32[4,8,32,128]{3,2,1,0:T(8,128)S(1)}, u32[]{:S(2)}, u32[]{:S(2)}) collective-permute-start(f32[4,8,32,128]{3,2,1,0:T(8,128)S(1)} %get-tuple-element.16), channel_id=1, source_target_pairs={{0,1},{1,0},{2,3},{3,2},{4,5},{5,4},{6,7},{7,6},{8,9},{9,8},{10,11... | collective-permute-start | bytes 1572872 | tf_op jit(solution)/shard_map/ppermute | solution.py:203
  50.5 4.7 %collective-permute-start.19 = (f32[4,8,32,128]{3,2,1,0:T(8,128)S(1)}, f32[4,8,32,128]{3,2,1,0:T(8,128)S(1)}, u32[]{:S(2)}, u32[]{:S(2)}) collective-permute-start(f32[4,8,32,128]{3,2,1,0:T(8,128)S(1)} %get-tuple-element.14), channel_id=1, source_target_pairs={{0,1},{1,0},{2,3},{3,2},{4,5},{5,4},{6,7},{7,6},{8,9},{9,8},{10,11... | collective-permute-start | bytes 1572872 | tf_op jit(solution)/shard_map/ppermute | solution.py:203
  52.3 7.4 %collective-permute-start.24 = (f32[8,32,128]{2,1,0:T(8,128)S(1)}, f32[8,32,128]{2,1,0:T(8,128)S(1)}, u32[]{:S(2)}, u32[]{:S(2)}) collective-permute-start(f32[8,32,128]{2,1,0:T(8,128)S(1)} %get-tuple-element.22), channel_id=1, source_target_pairs={{0,2},{1,3},{2,4},{3,5},{4,6},{5,7},{6,0},{7,1},{8,10},{9,11},{10,... | collective-permute-start | bytes 393224 | tf_op jit(solution)/shard_map/ppermute | solution.py:199
  54.0 7.9 %collective-permute-start.25 = (f32[8,32,128]{2,1,0:T(8,128)S(1)}, f32[8,32,128]{2,1,0:T(8,128)S(1)}, u32[]{:S(2)}, u32[]{:S(2)}) collective-permute-start(f32[8,32,128]{2,1,0:T(8,128)S(1)} %get-tuple-element.24), channel_id=1, source_target_pairs={{0,4},{1,5},{2,6},{3,7},{4,0},{5,1},{6,2},{7,3},{8,12},{9,13},{10,... | collective-permute-start | bytes 393224 | tf_op jit(solution)/shard_map/ppermute | solution.py:199
  55.1 10.5 %collective-permute-start.26 = (f32[8,32,128]{2,1,0:T(8,128)S(1)}, f32[8,32,128]{2,1,0:T(8,128)S(1)}, u32[]{:S(2)}, u32[]{:S(2)}) collective-permute-start(f32[8,32,128]{2,1,0:T(8,128)S(1)} %get-tuple-element.23), channel_id=1, source_target_pairs={{0,6},{1,7},{2,0},{3,1},{4,2},{5,3},{6,4},{7,5},{8,14},{9,15},{10,... | collective-permute-start | bytes 393224 | tf_op jit(solution)/shard_map/ppermute | solution.py:199
  55.3 11.2 %collective-permute-start.20 = (f32[8,32,128]{2,1,0:T(8,128)S(1)}, f32[8,32,128]{2,1,0:T(8,128)S(1)}, u32[]{:S(2)}, u32[]{:S(2)}) collective-permute-start(f32[8,32,128]{2,1,0:T(8,128)S(1)} %get-tuple-element.19), channel_id=1, source_target_pairs={{0,2},{1,3},{2,4},{3,5},{4,6},{5,7},{6,0},{7,1},{8,10},{9,11},{10,... | collective-permute-start | bytes 393224 | tf_op jit(solution)/shard_map/ppermute | solution.py:199
  58.6 8.9 %collective-permute-start.21 = (f32[8,32,128]{2,1,0:T(8,128)S(1)}, f32[8,32,128]{2,1,0:T(8,128)S(1)}, u32[]{:S(2)}, u32[]{:S(2)}) collective-permute-start(f32[8,32,128]{2,1,0:T(8,128)S(1)} %get-tuple-element.21), channel_id=1, source_target_pairs={{0,4},{1,5},{2,6},{3,7},{4,0},{5,1},{6,2},{7,3},{8,12},{9,13},{10,... | collective-permute-start | bytes 393224 | tf_op jit(solution)/shard_map/ppermute | solution.py:199
  59.7 9.5 %collective-permute-start.22 = (f32[8,32,128]{2,1,0:T(8,128)S(1)}, f32[8,32,128]{2,1,0:T(8,128)S(1)}, u32[]{:S(2)}, u32[]{:S(2)}) collective-permute-start(f32[8,32,128]{2,1,0:T(8,128)S(1)} %get-tuple-element.20), channel_id=1, source_target_pairs={{0,6},{1,7},{2,0},{3,1},{4,2},{5,3},{6,4},{7,5},{8,14},{9,15},{10,... | collective-permute-start | bytes 393224 | tf_op jit(solution)/shard_map/ppermute | solution.py:199
  65.7 8.4 %collective-permute-start.27 = (f32[8,32,128]{2,1,0:T(8,128)S(1)}, f32[8,32,128]{2,1,0:T(8,128)S(1)}, u32[]{:S(2)}, u32[]{:S(2)}) collective-permute-start(f32[8,32,128]{2,1,0:T(8,128)S(1)} %fusion.2), channel_id=1, source_target_pairs={{0,8},{1,9},{2,10},{3,11},{4,12},{5,13},{6,14},{7,15},{8,16},{9,17... | collective-permute-start | bytes 393224 | tf_op jit(solution)/shard_map/ppermute | solution.py:209
  74.2 7.7 %collective-permute-start.28 = (f32[8,32,128]{2,1,0:T(8,128)S(1)}, f32[8,32,128]{2,1,0:T(8,128)S(1)}, u32[]{:S(2)}, u32[]{:S(2)}) collective-permute-start(f32[8,32,128]{2,1,0:T(8,128)S(1)} %get-tuple-element.29), channel_id=1, source_target_pairs={{0,6},{1,7},{2,0},{3,1},{4,2},{5,3},{6,4},{7,5},{8,14},{9,15},{10,... | collective-permute-start | bytes 393224 | tf_op jit(solution)/shard_map/ppermute | solution.py:199
  74.3 7.6 %collective-permute-start.29 = (f32[8,32,128]{2,1,0:T(8,128)S(1)}, f32[8,32,128]{2,1,0:T(8,128)S(1)}, u32[]{:S(2)}, u32[]{:S(2)}) collective-permute-start(f32[8,32,128]{2,1,0:T(8,128)S(1)} %get-tuple-element.31), channel_id=1, source_target_pairs={{0,4},{1,5},{2,6},{3,7},{4,0},{5,1},{6,2},{7,3},{8,12},{9,13},{10,... | collective-permute-start | bytes 393224 | tf_op jit(solution)/shard_map/ppermute | solution.py:199
  75.3 7.3 %collective-permute-start.30 = (f32[8,32,128]{2,1,0:T(8,128)S(1)}, f32[8,32,128]{2,1,0:T(8,128)S(1)}, u32[]{:S(2)}, u32[]{:S(2)}) collective-permute-start(f32[8,32,128]{2,1,0:T(8,128)S(1)} %get-tuple-element.30), channel_id=1, source_target_pairs={{0,2},{1,3},{2,4},{3,5},{4,6},{5,7},{6,0},{7,1},{8,10},{9,11},{10,... | collective-permute-start | bytes 393224 | tf_op jit(solution)/shard_map/ppermute | solution.py:199

commit v3 on v1

v3 whole, which is shorter than its diff:
```python
import jax
import jax.numpy as jnp
import numpy as np
from jax import lax
from jax.experimental import pallas as pl
from jax.experimental.pallas import tpu as pltpu
from jax.sharding import PartitionSpec as P

STEP_LENGTH = 0.1
EPSILON = 1e-06
CHIPS = 4
ORDER = (1, 3, 2)
VMEM = pl.BlockSpec(memory_space=pltpu.VMEM)
ANY = pl.BlockSpec(memory_space=pl.ANY)
SMEM = pl.BlockSpec(memory_space=pltpu.SMEM)
MIDDLE = pltpu.CompilerParams(vmem_limit_bytes=16 * 1024 * 1024)
BIG = pltpu.CompilerParams(vmem_limit_bytes=24 * 1024 * 1024)


def half_kinetic(extent, length):
    m = np.arange(length)
    weight = (2.0 * np.pi * np.minimum(m, length - m) / length) ** 2
    angle = 2.0 * np.pi * (m[:, None] * m[None, :] % length) / length
    matrix = (np.cos(angle) * weight) @ np.cos(angle).T + (np.sin(angle) * weight) @ np.sin(angle).T
    out = np.zeros((extent, extent))
    out[:length, :length] = 0.5 * matrix / length
    return out


def split_const(matrix):
    whole = jnp.asarray(matrix, jnp.float32)
    high = whole.astype(jnp.bfloat16)
    return high, (whole - high.astype(jnp.float32)).astype(jnp.bfloat16)


def operators(depth, width, length):
    y_pair = [half_kinetic(width, width // 2), half_kinetic(width, width)]
    z_op, half = half_kinetic(depth, depth), depth // 2
    z_parts = [(z_op[:half, :half] + sign * z_op[:half, half:]) / 2 for sign in (1, -1)]
    rows = list(split_const(half_kinetic(length, length)))
    for matrix in y_pair:
        rows += [jnp.concatenate([part, part], axis=1) for part in split_const(matrix)]
    rows.append(jnp.concatenate([part for matrix in z_parts for part in split_const(matrix)], axis=1))
    return jnp.concatenate(rows, axis=0)


def split(value):
    high = value.astype(jnp.bfloat16)
    return high, (value - high.astype(jnp.float32)).astype(jnp.bfloat16)


def dot(a, b):
    return jnp.dot(a, b, preferred_element_type=jnp.float32)


def xy_part(blocks, x_ref, y_ref, exact):
    parts = [(b.astype(jnp.bfloat16), None) if exact else split(b) for b in blocks]
    y_high, y_low = y_ref[0], y_ref[1]
    highs = jnp.concatenate([p[0] for p in parts], axis=1)
    y_out = dot(y_high, highs) + dot(y_low, highs)
    if not exact:
        y_out = y_out + dot(y_high, jnp.concatenate([p[1] for p in parts], axis=1))
    length = blocks[0].shape[1]
    result = []
    for i, (high, low) in enumerate(parts):
        if exact:
            x_out = dot(high, x_ref[:length])
        else:
            x_out = dot(jnp.concatenate([high, low], 1), x_ref[...])
        result.append(x_out[:, :length] + x_out[:, length:] + y_out[:, i * length : (i + 1) * length])
    return result


def z_part(lowers, uppers, z_ref):
    def side_by_side(pieces):
        return jnp.concatenate([p.reshape(-1, p.shape[2]) for p in pieces], axis=1)

    upper = side_by_side(uppers)
    if lowers is None:
        inputs = [split(upper)] * 2
    else:
        lower = side_by_side(lowers)
        inputs = [split(lower + upper), split(lower - upper)]
    even, odd = (
        dot(z_ref[2 * i], high) + dot(z_ref[2 * i + 1], high) + dot(z_ref[2 * i], low)
        for i, (high, low) in enumerate(inputs)
    )
    return (even - odd, even + odd) if lowers is None else (even + odd, even - odd)


def tiles(i):
    return [pl.ds(pl.multiple_of(i * 16 + 8 * j, 8), 8) for j in range(2)]


def cut(out, j, length):
    return out[:, j * length : (j + 1) * length].reshape(-1, 8, length)


def total(vector):
    return jnp.sum(vector, axis=(0, 1), keepdims=True)


def fold(block):
    return jnp.sum(block.reshape(-1, 8, block.shape[-1]), axis=0)


def prepare(code, order_before, wave, consts, states, x_ref, y_ref, z_ref):
    depth, width, length = states.shape
    double = code[0, 0] & 1
    x_row = jnp.concatenate([consts[:length], consts[length : 2 * length]], axis=1)
    x_ref[...] = jnp.concatenate([x_row, x_row], axis=0)
    rows, cols = (lax.broadcasted_iota(jnp.int32, (4 * width, 4 * width), d) for d in range(2))
    for i in range(2):
        at = pl.ds(pl.multiple_of(2 * length + (2 * double + i) * width, width), width)
        square = jnp.concatenate([jnp.concatenate([consts[at]] * 2, axis=1)] * 4, axis=0)
        y_ref[i] = jnp.where(rows // width == cols // width, square, jnp.zeros_like(square))
    half = depth // 2
    z_rows = consts[2 * length + 4 * width : 2 * length + 4 * width + half]
    down = lax.broadcasted_iota(jnp.int32, (8 * half, half), 0) // 8 == lax.broadcasted_iota(jnp.int32, (8 * half, half), 1)
    tall = dot(down.astype(jnp.bfloat16), z_rows).astype(jnp.bfloat16)
    source, target = (lax.broadcasted_iota(jnp.int32, (length, 8 * half), d) for d in range(2))
    for i in range(4):
        full = dot(tall, (source == target // 8 + half * i).astype(jnp.bfloat16))
        z_ref[i] = jnp.where((rows & 7) == (cols & 7), full, 0.0).astype(jnp.bfloat16)
    live = lax.broadcasted_iota(jnp.int32, (1, width, length), 1) < (width // 2) * (1 + double)

    def masked(i, carry):
        states[pl.ds(i * 4, 4)] = jnp.where(live, wave[pl.ds(i * 4, 4)].astype(jnp.float32), 0.0)
        return carry

    lax.fori_loop(0, depth // 4, masked, 0)


def xy_pass(read, out, start, lines, x_ref, y_ref, exact):
    _, width, length = out.shape

    def step(i, carry):
        z = start + i * 8
        rows = read(z).reshape(2, 4 * width, length)
        lower, upper = xy_part([rows[0], rows[1]], x_ref, y_ref, exact)
        out[pl.ds(z, 4)] = lower.reshape(4, width, length)
        out[pl.ds(z + 4, 4)] = upper.reshape(4, width, length)
        return carry

    lax.fori_loop(0, lines // 8, step, 0)


def first_kinetic(after, states, x_ref, y_ref, z_ref, out):
    depth, width, length = out.shape
    half = depth // 2
    xy_pass(lambda z: states[pl.ds(z, 8)], out, 0, depth, x_ref, y_ref, True)

    def zz(i, carry):
        halves = [[states[pl.ds(j * half, half), r] for r in tiles(i)] for j in range(2)]
        for j, part in enumerate(z_part(*halves, z_ref)):
            for k, r in enumerate(tiles(i)):
                at = pl.ds(j * half, half)
                out[at, r] = out[at, r] + cut(part, k, length)
        return carry

    lax.fori_loop(0, width // 16, zz, 0)


def box_rows(band, code, column):
    at, _ = place(band[0] & 1, code[0, 0])
    return [pl.ds(pl.multiple_of(i * column, column), column) for i in (at, 1 - at)]


def line_loop(band, code, columns, use):
    chip = band[0] >> 1
    for ref, rows in zip(columns, box_rows(band, code, columns[0].shape[2])):
        chunk = ref.shape[1]
        for m in range(CHIPS):
            start = ((chip - m) & (CHIPS - 1)) * chunk

            def line(i, carry, ref=ref, rows=rows, m=m, start=start):
                use(rows, start + i, ref[m, i])
                return carry

            lax.fori_loop(0, chunk, line, 0, unroll=2)


def lower_half(band, code, states, kinetic, x_ref, y_ref, z_ref, own, other, pot, applied, again):
    half, width, length = pot.shape

    def use(rows, z, v):
        pot[z, rows] = v
        applied[z, rows] = kinetic[z, rows] + v * states[z, rows]

    line_loop(band, code, (own, other), use)
    xy_pass(lambda z: applied[pl.ds(z, 8)], again, 0, half, x_ref, y_ref, False)
    xy_pass(lambda z: kinetic[pl.ds(z, 8)], again, half, half, x_ref, y_ref, False)

    def zz(i, carry):
        lowers = [applied[:, r] for r in tiles(i)]
        uppers = [kinetic[pl.ds(half, half), r] for r in tiles(i)]
        for j, part in enumerate(z_part(lowers, uppers, z_ref)):
            for k, r in enumerate(tiles(i)):
                at = pl.ds(j * half, half)
                again[at, r] = again[at, r] + cut(part, k, length)
        return carry

    lax.fori_loop(0, width // 16, zz, 0)


def both_steps(band, code, states, kinetic, x_ref, y_ref, z_ref, pot, applied, again, own, other, *refs):
    (keep0, give0, keep1, give1), (pot_up, forced, applied_up, extra, twice) = refs[:4], refs[4:]
    half, width, length = pot.shape
    chunk, column, double = half // CHIPS, width // 2, code[0, 0] & 1

    def use(rows, z, v):
        change = v * states[half + z, rows]
        pot_up[z, rows] = v
        forced[z, rows] = change
        applied_up[z, rows] = kinetic[half + z, rows] + change

    line_loop(band, code, (own, other), use)
    xy_pass(lambda z: forced[pl.ds(z, 8)], extra, 0, half, x_ref, y_ref, False)

    def zz(i, sums):
        low_part, high_part = z_part(None, [forced[:, r] for r in tiles(i)], z_ref)
        for k, r in enumerate(tiles(i)):
            low, high = pl.ds(0, half), pl.ds(half, half)
            h, h_up = applied[:, r], applied_up[:, r]
            w = again[low, r] + cut(low_part, k, length) + pot[:, r] * h
            w_up = again[high, r] + extra[:, r] + cut(high_part, k, length) + pot_up[:, r] * h_up
            twice[low, r] = w
            twice[high, r] = w_up
            pairs = []
            for s, h, w in ((states[low, r], h, w), (states[high, r], h_up, w_up)):
                pairs.append((s * s, s * h, h * h, s * w, h * w, w * w))
            sums = tuple(v + fold(a + b) for v, a, b in zip(sums, *pairs))
        return sums

    zero = jnp.zeros((8, length), jnp.float32)
    ss, sh, hh, sw, hw, ww = (total(v) for v in lax.fori_loop(0, width // 16, zz, (zero,) * 6))
    cells = (2 * half * column * length * (1 + double)).astype(jnp.float32)
    first = 1.0 + STEP_LENGTH * sh / (ss + EPSILON)
    tt = first * first * ss - 2.0 * STEP_LENGTH * first * sh + STEP_LENGTH * STEP_LENGTH * hh
    th = first * first * sh - STEP_LENGTH * first * (hh + sw) + STEP_LENGTH * STEP_LENGTH * hw
    hh = first * first * hh - 2.0 * STEP_LENGTH * first * hw + STEP_LENGTH * STEP_LENGTH * ww
    square = cells / (tt + EPSILON)
    second = 1.0 + STEP_LENGTH * square * th / (square * tt + EPSILON)
    weight = second * second * tt - 2.0 * STEP_LENGTH * second * th + STEP_LENGTH * STEP_LENGTH * hh
    sign = (2 * double - 1).astype(jnp.float32)
    factor = sign / 8.0 * square * cells / (square * weight + EPSILON)
    by_s, by_h, by_w = second * first, -STEP_LENGTH * (first + second), STEP_LENGTH * STEP_LENGTH
    for slab, outs, source in ((1, (keep1, give1), applied_up), (0, (keep0, give0), applied)):
        for out, rows in zip(outs, box_rows(band, code, column)):
            for k in range(CHIPS):
                start = (((band[0] >> 1) + k) & (CHIPS - 1)) * chunk

                def line(i, carry, out=out, rows=rows, start=start, k=k, slab=slab, source=source):
                    z = start + i
                    at = slab * half + z
                    u = by_s * states[at, rows] + by_h * source[z, rows] + by_w * twice[at, rows]
                    out[k, i] = factor * (u * u)
                    return carry

                lax.fori_loop(0, chunk, line, 0, unroll=2)


def stack(after, *refs):
    for i, block in enumerate(refs[:-1]):
        refs[-1][i] = block[...]


def to_next_chip(block, k):
    m = 2 * CHIPS
    return lax.ppermute(block, "band", [(b, (b + 2 * k) % m) for b in range(m)])


def exchange(blocks):
    cores = [[2 * chip + core for chip in range(CHIPS)] for core in range(2)]
    return lax.all_to_all(blocks, "band", 0, 0, axis_index_groups=cores)


def around(blocks):
    sent = {k: to_next_chip(blocks[k], k) for k in ORDER}
    return [blocks[0]] + [sent[k] for k in range(1, CHIPS)]


def to_other_core(block):
    return lax.ppermute(block, "band", [(b, b ^ 1) for b in range(2 * CHIPS)])


def to_group(block, distance):
    n = lax.axis_size("frag")
    return lax.ppermute(block, "frag", [(i, (i + distance) % n) for i in range(n)])


def place(core, code):
    low = code >> 2
    upper = (low + core) & 1
    return upper, ((low + upper) & (2 * CHIPS - 1)) >> 1


def pick(band, code, code_before, after, pieces, below, here):
    for out, order in ((below, code_before), (here, code)):
        _, owner = place(band[0] & 1, order[0, 0])
        out[...] = pieces[owner]


def settle(band, *refs):
    for k, block in enumerate(refs[:CHIPS]):
        chip = ((band[0] >> 1) - k) & (CHIPS - 1)
        refs[CHIPS][pl.ds(chip * block.shape[0], block.shape[0])] = block[...]


def body(wave_init, potential, fragment_order):
    _, _, depth, width, length = wave_init.shape
    chunk, column = depth // 2 // CHIPS, width // 2
    wave = wave_init[0, 0]
    band = lax.axis_index("band").astype(jnp.int32)
    core = band & 1
    order_before = to_group(fragment_order, 1)
    pieces = exchange(potential.reshape(CHIPS, chunk, column, length))

    small = pltpu.CompilerParams(vmem_limit_bytes=4 * 1024 * 1024)
    piece, quarter, half_box, box = (
        jax.ShapeDtypeStruct(shape + (length,), jnp.float32)
        for shape in ((chunk, column), (CHIPS, chunk, column), (depth // 2, width), (depth, width))
    )
    square = (4 * width, 4 * width)
    ops = [jax.ShapeDtypeStruct(lead + square, jnp.bfloat16) for lead in ((), (2,), (4,))]

    def kernel(function, outs, spaces, params, scratch=(), flops=0):
        return pl.pallas_call(
            function,
            out_shape=outs,
            in_specs=spaces,
            out_specs=[VMEM] * len(outs),
            scratch_shapes=[pltpu.VMEM(a.shape, a.dtype) for a in scratch],
            compiler_params=params,
            cost_estimate=pl.CostEstimate(flops=flops, bytes_accessed=4_000_000, transcendentals=0) if flops else None,
            name=function.__name__,
        )

    states, *ops = kernel(prepare, [box] + ops, [SMEM, ANY, VMEM, VMEM], MIDDLE)(
        fragment_order, order_before, wave, operators(depth, width, length)
    )
    below, here = kernel(pick, [piece] * 2, [SMEM] * 3 + [ANY, VMEM], small)(
        band[None], fragment_order, order_before, states, pieces
    )
    below = to_group(below, -1)
    lower, upper = around([here] * CHIPS), around([below] * CHIPS)
    (kinetic,) = kernel(first_kinetic, [box], [ANY] + [VMEM] * 4, MIDDLE, flops=3_000_000_000)(below, states, *ops)

    def two_columns(after, blocks):
        (own,) = kernel(stack, [quarter], [ANY] + [VMEM] * CHIPS, small)(after, *blocks)
        return own, to_other_core(own)

    pot, applied, again = kernel(
        lower_half, [half_box] * 2 + [box], [SMEM] * 2 + [VMEM] * 7, MIDDLE, flops=4_000_000_000
    )(band[None], fragment_order, states, kinetic, *ops, *two_columns(kinetic, lower))
    keep0, give0, keep1, give1 = kernel(
        both_steps, [quarter] * 4, [SMEM] * 2 + [VMEM] * 10, BIG, scratch=[half_box] * 4 + [box]
    )(band[None], fragment_order, states, kinetic, *ops, pot, applied, again, *two_columns(again, upper))

    def reduce_chip(keep, give):
        result, *arrived = around(list(keep + to_other_core(give)))
        for block in arrived:
            result = result + block
        return result

    above = to_group(reduce_chip(keep1, give1), 1)
    here = reduce_chip(keep0, give0)
    owner, owner_before = (place(core, code[0, 0])[1] for code in (fragment_order, order_before))
    sends = []
    for k in range(CHIPS):
        target = ((band >> 1) + k) & (CHIPS - 1)
        sends.append(jnp.where(target == owner, here, 0.0) + jnp.where(target == owner_before, above, 0.0))
    return pl.pallas_call(
        settle,
        out_shape=jax.ShapeDtypeStruct(potential.shape, jnp.float32),
        in_specs=[SMEM] + [VMEM] * CHIPS,
        out_specs=VMEM,
        compiler_params=small,
        name="settle",
    )(band[None], *around(sends))


def solution(mesh):
    placed = (P("frag", "band", None, None, None), P("frag", "band", None), P("frag", None))
    return jax.shard_map(
        body, mesh=mesh, in_specs=placed, out_specs=P("frag", "band", None), check_vma=False
    )
```

time: 90.8 us -> 81.1 us (0.89)
  starting transfers between devices: 29.2 us -> 25.8 us
  local copies, waits for them, and re-layouts: 4.74 us -> 2.19 us
  between operations: 3.66 us -> 1.49 us
  other arithmetic: 2.08 us -> 0.3 us
  Pallas kernels: 14.6 us -> 16.2 us
  waiting for transfers between devices: 35.9 us -> 34.9 us
    ppermute x18 -> x15, starting transfers between devices: 23.6 us -> 16.2 us  [to_next_chip(): return lax.ppermute(block, 'band', [(b, (b + 2 * k) % m) for b in range(m)])]
    all_to_all x0 -> x1, starting transfers between devices: none -> 5.4 us  [exchange(): return lax.all_to_all(blocks, 'band', 0, 0, axis_index_groups=cores)]
    ppermute x18 -> x15, waiting for transfers between devices: 22.3 us -> 19.4 us  [to_next_chip(): return lax.ppermute(block, 'band', [(b, (b + 2 * k) % m) for b in range(m)])]
    ppermute x10 -> x4, waiting for transfers between devices: 1.42 us -> 3.29 us  [to_other_core(): return lax.ppermute(block, 'band', [(b, b ^ 1) for b in range(2 * CHIPS)])]
    pallas_call x2 -> x8, Pallas kernels: 14.6 us -> 16.2 us  [the longest x1 4.98 us: body(): kernel(both_steps, [quarter] * 4, [SMEM] * 2 + [VMEM] * 10, BIG, scratch=...]
    unnamed x10 -> x4, local copies, waits for them, and re-layouts: 3.43 us -> 2.13 us
    ppermute x10 -> x4, starting transfers between devices: 1.98 us -> 0.8 us  [to_other_core(): return lax.ppermute(block, 'band', [(b, b ^ 1) for b in range(2 * CHIPS)])]
    slice x1 -> x0, local copies, waits for them, and re-layouts: 1.17 us -> none  [body(): pieces = [pieces[0]] + [to_next_chip(pieces[k], k) for k in range(1, CHIPS)]]
  transfers between devices with their start and end apart: 31 -> 23, of which waited for: 13 -> 15; matrix products, arithmetic and copies ran while one was open for 0% -> 0% of each run, Pallas kernels for 5% -> 12%
where the time goes in v3:
time: 81.1 us; the launch traced here: 80.8 us
  waiting for transfers between devices  34.9 us (43%)
  starting transfers between devices  25.8 us (32%)
  Pallas kernels  16.2 us (20%)
  local copies, waits for them, and re-layouts  2.19 us (3%)
  between operations  1.49 us (2%)
    ppermute x15, waiting for transfers between devices, to_next_chip(): return lax.ppermute(block, 'band', [(b, (b + 2 * k) % m) for b in range(m)])  19.4 us
    ppermute x15, starting transfers between devices, to_next_chip(): return lax.ppermute(block, 'band', [(b, (b + 2 * k) % m) for b in range(m)])  16.2 us
    ppermute x3, waiting for transfers between devices, to_group(): lax.ppermute(block, 'frag', [(i, (i + distance) % n) for i in range(n)])  12.1 us
    all_to_all x1, starting transfers between devices, exchange(): return lax.all_to_all(blocks, 'band', 0, 0, axis_index_groups=cores)  5.4 us
    pallas_call x1, Pallas kernels, body(): kernel(both_steps, [quarter] * 4, [SMEM] * 2 + [VMEM] * 10, BIG, scratch=...  4.98 us
    pallas_call x1, Pallas kernels, body(): kernel(lower_half, [half_box] * 2 + [box], [SMEM] * 2 + [VMEM] * 7, MIDDL...  4.6 us
    pallas_call x1, Pallas kernels, body(): kernel(first_kinetic, [box], [ANY] + [VMEM] * 4, MIDDLE, flops=3000000000)  3.91 us
    ppermute x3, starting transfers between devices, to_group(): lax.ppermute(block, 'frag', [(i, (i + distance) % n) for i in range(n)])  3.39 us
  transfers between devices with their start and end apart: 23, of which 15 were waited for; matrix products, arithmetic and copies ran while one was open for 0% of the time, Pallas kernels for 12%

profile of v3, /device:TPU:24, one launch (start us, length us, event | category | flops | bytes accessed | tf_op | source)
XLA Modules:
  0.0 80.8 jit_solution(8391123521511318599)
XLA Ops:
  0.0 5.4 %all-to-all-start = ((f32[4,8,32,128]{3,2,1,0:T(8,128)}), f32[4,8,32,128]{3,2,1,0:T(8,128)S(1)}, u32[]{:S(2)}, u32[]{:S(2)}) async-start(f32[4,8,32,128]{3,2,1,0:T(8,128)} %bitcast.35), calls=%async_computation | async-start | bytes 1048576 | tf_op jit(solution)/shard_map/all_to_all | solution.py:275
  5.4 0.8 collective-permute-start
  6.9 7.5 %collective-permute-done.order_before.code_before = s32[1,1]{1,0:T(1,128)} collective-permute-done((s32[1,1]{1,0:T(1,128)}, s32[1,1]{1,0:T(1,128)}, u32[]{:S(2)}, u32[]{:S(2)}) %collective-permute-start) | collective-permute-done | bytes 36 | tf_op jit(solution)/shard_map/ppermute | solution.py:289
  14.3 1.2 %copy-done = bf16[1,1,64,64,128]{4,3,2,1,0:T(8,128)(2,1)S(1)} copy-done((bf16[1,1,64,64,128]{4,3,2,1,0:T(8,128)(2,1)S(1)}, bf16[1,1,64,64,128]{4,3,2,1,0:T(8,128)(2,1)}, u32[]{:S(2)}) %copy-start) | copy-done | bytes 1048600
  15.6 0.9 %copy-done.1 = bf16[544,128]{1,0:T(8,128)(2,1)S(1)} copy-done((bf16[544,128]{1,0:T(8,128)(2,1)S(1)}, bf16[544,128]{1,0:T(8,128)(2,1)}, u32[]{:S(2)}) %copy-start.1) | copy-done | bytes 139288
  16.5 1.2 %prepare.1 = (f32[64,64,128]{2,1,0:T(8,128)S(1)}, bf16[256,256]{1,0:T(8,128)(2,1)S(1)}, bf16[2,256,256]{2,1,0:T(8,128)(2,1)S(1)}, bf16[4,256,256]{2,1,0:T(8,128)(2,1)S(1)}) custom-call(s32[1,1]{1,0:T(1,128)S(6)} %copy.9.code, s32[1,1]{1,0:T(1,128)} %collective-permute-done.order_before.code_before, bf16[64,64,128]{2,1,0:T(8,128)(2,1)S(1)} %bitcast.34, ...), custom_call_target="tpu_custom_call" | custom-call | tf_op jit(solution)/shard_map/prepare/pallas_call | solution.py:339
  17.7 0.6 pick.1
  18.3 2.5 %collective-permute-start.1 = (f32[8,32,128]{2,1,0:T(8,128)S(1)}, f32[8,32,128]{2,1,0:T(8,128)S(1)}, u32[]{:S(2)}, u32[]{:S(2)}) collective-permute-start(f32[8,32,128]{2,1,0:T(8,128)S(1)} %get-tuple-element.19), channel_id=1, source_target_pairs={{0,248},{8,0},{16,8},{24,16},{32,24},{40,32},{48,40},{56,48},{64,5... | collective-permute-start | bytes 393224 | tf_op jit(solution)/shard_map/ppermute | solution.py:289
  20.9 2.1 %collective-permute-start.2 = (f32[8,32,128]{2,1,0:T(8,128)S(1)}, f32[8,32,128]{2,1,0:T(8,128)S(1)}, u32[]{:S(2)}, u32[]{:S(2)}) collective-permute-start(f32[8,32,128]{2,1,0:T(8,128)S(1)} %get-tuple-element.23.refs_0_), channel_id=1, source_target_pairs={{0,2},{1,3},{2,4},{3,5},{4,6},{5,7},{6,0},{7,1},{8,10},{9,11},{10,... | collective-permute-start | bytes 393224 | tf_op jit(solution)/shard_map/ppermute | solution.py:270
  22.9 0.4 collective-permute-start.3
  23.4 1.0 %collective-permute-start.4 = (f32[8,32,128]{2,1,0:T(8,128)S(1)}, f32[8,32,128]{2,1,0:T(8,128)S(1)}, u32[]{:S(2)}, u32[]{:S(2)}) collective-permute-start(f32[8,32,128]{2,1,0:T(8,128)S(1)} %get-tuple-element.23.refs_0_), channel_id=1, source_target_pairs={{0,6},{1,7},{2,0},{3,1},{4,2},{5,3},{6,4},{7,5},{8,14},{9,15},{10,... | collective-permute-start | bytes 393224 | tf_op jit(solution)/shard_map/ppermute | solution.py:270
  24.4 3.9 %first_kinetic.1.after.kinetic = f32[64,64,128]{2,1,0:T(8,128)S(1)} custom-call(f32[8,32,128]{2,1,0:T(8,128)S(1)} %collective-permute-done.1.after.refs_0_, f32[64,64,128]{2,1,0:T(8,128)S(1)} %get-tuple-element.18.after.states, bf16[256,256]{1,0:T(8,128)(2,1)S(1)} %get-tuple-element.20.x_ref, bf16[2,256,256]{2,1,0:T(8,128)(2,1)S(1)} %get-tuple-element.21.y_ref, ...), custom_call_target="tpu_custom_call" | custom-call | flops 3000000000 | bytes 4000000 | tf_op jit(solution)/shard_map/first_kinetic/pallas_call | solution.py:347
  28.3 1.2 %collective-permute-done.3.refs_2_ = f32[8,32,128]{2,1,0:T(8,128)S(1)} collective-permute-done((f32[8,32,128]{2,1,0:T(8,128)S(1)}, f32[8,32,128]{2,1,0:T(8,128)S(1)}, u32[]{:S(2)}, u32[]{:S(2)}) %collective-permute-start.3) | collective-permute-done | bytes 131104 | tf_op jit(solution)/shard_map/ppermute | solution.py:270
  29.5 1.3 %collective-permute-done.4.refs_3_ = f32[8,32,128]{2,1,0:T(8,128)S(1)} collective-permute-done((f32[8,32,128]{2,1,0:T(8,128)S(1)}, f32[8,32,128]{2,1,0:T(8,128)S(1)}, u32[]{:S(2)}, u32[]{:S(2)}) %collective-permute-start.4) | collective-permute-done | bytes 131104 | tf_op jit(solution)/shard_map/ppermute | solution.py:270
  30.8 0.1 collective-permute-start.5
  30.9 0.6 collective-permute-start.6
  31.6 1.1 %collective-permute-start.7 = (f32[8,32,128]{2,1,0:T(8,128)S(1)}, f32[8,32,128]{2,1,0:T(8,128)S(1)}, u32[]{:S(2)}, u32[]{:S(2)}) collective-permute-start(f32[8,32,128]{2,1,0:T(8,128)S(1)} %collective-permute-done.1.after.refs_0_), channel_id=1, source_target_pairs={{0,4},{1,5},{2,6},{3,7},{4,0},{5,1},{6,2},{7,3},{8,12},{9,13},{10,... | collective-permute-start | bytes 393224 | tf_op jit(solution)/shard_map/ppermute | solution.py:270
  32.7 0.4 collective-permute-start.8
  33.1 4.6 %lower_half.1 = (f32[32,64,128]{2,1,0:T(8,128)S(1)}, f32[32,64,128]{2,1,0:T(8,128)S(1)}, f32[64,64,128]{2,1,0:T(8,128)S(1)}) custom-call(s32[1]{0:T(128)} %bitcast.band, s32[1,1]{1,0:T(1,128)S(6)} %copy.9.code, f32[64,64,128]{2,1,0:T(8,128)S(1)} %get-tuple-element.18.after.states, f32[64,64,128]{2,1,0:T(8,128)S(1)} %first_kinetic.1.after.kinetic, ...), custom_call_target="tpu_custom_call" | custom-call | flops 4000000000 | bytes 4000000 | tf_op jit(solution)/shard_map/lower_half/pallas_call | solution.py:353
  37.7 1.7 %collective-permute-done.7.refs_2_ = f32[8,32,128]{2,1,0:T(8,128)S(1)} collective-permute-done((f32[8,32,128]{2,1,0:T(8,128)S(1)}, f32[8,32,128]{2,1,0:T(8,128)S(1)}, u32[]{:S(2)}, u32[]{:S(2)}) %collective-permute-start.7) | collective-permute-done | bytes 131104 | tf_op jit(solution)/shard_map/ppermute | solution.py:270
  39.4 2.0 %collective-permute-done.8.refs_3_ = f32[8,32,128]{2,1,0:T(8,128)S(1)} collective-permute-done((f32[8,32,128]{2,1,0:T(8,128)S(1)}, f32[8,32,128]{2,1,0:T(8,128)S(1)}, u32[]{:S(2)}, u32[]{:S(2)}) %collective-permute-start.8) | collective-permute-done | bytes 131104 | tf_op jit(solution)/shard_map/ppermute | solution.py:270
  41.5 0.1 collective-permute-start.9
  41.6 1.9 %collective-permute-done.9.other = f32[4,8,32,128]{3,2,1,0:T(8,128)S(1)} collective-permute-done((f32[4,8,32,128]{3,2,1,0:T(8,128)S(1)}, f32[4,8,32,128]{3,2,1,0:T(8,128)S(1)}, u32[]{:S(2)}, u32[]{:S(2)}) %collective-permute-start.9) | collective-permute-done | bytes 524320 | tf_op jit(solution)/shard_map/ppermute | solution.py:284
  43.5 5.0 %both_steps.1 = (f32[4,8,32,128]{3,2,1,0:T(8,128)S(1)}, f32[4,8,32,128]{3,2,1,0:T(8,128)S(1)}, f32[4,8,32,128]{3,2,1,0:T(8,128)S(1)}, f32[4,8,32,128]{3,2,1,0:T(8,128)S(1)}) custom-call(s32[1]{0:T(128)} %bitcast.band, s32[1,1]{1,0:T(1,128)S(6)} %copy.9.code, f32[64,64,128]{2,1,0:T(8,128)S(1)} %get-tuple-element.18.after.states, ...), custom_call_target="tpu_custom_call" | custom-call | tf_op jit(solution)/shard_map/both_steps/pallas_call | solution.py:356
  48.5 0.2 collective-permute-start.14
  48.7 0.4 collective-permute-start.10
  49.1 1.4 %collective-permute-done.14 = f32[4,8,32,128]{3,2,1,0:T(8,128)S(1)} collective-permute-done((f32[4,8,32,128]{3,2,1,0:T(8,128)S(1)}, f32[4,8,32,128]{3,2,1,0:T(8,128)S(1)}, u32[]{:S(2)}, u32[]{:S(2)}) %collective-permute-start.14) | collective-permute-done | bytes 524320 | tf_op jit(solution)/shard_map/ppermute | solution.py:284
  50.5 0.1 add.65
  50.6 1.0 %collective-permute-start.15 = (f32[8,32,128]{2,1,0:T(8,128)S(1)}, f32[8,32,128]{2,1,0:T(8,128)S(1)}, u32[]{:S(2)}, u32[]{:S(2)}) collective-permute-start(f32[8,32,128]{2,1,0:T(8,128)S(1)} %get-tuple-element.36), channel_id=1, source_target_pairs={{0,2},{1,3},{2,4},{3,5},{4,6},{5,7},{6,0},{7,1},{8,10},{9,11},{10,... | collective-permute-start | bytes 393224 | tf_op jit(solution)/shard_map/ppermute | solution.py:270
  51.6 0.7 collective-permute-start.16
  52.3 0.9 %collective-permute-start.17 = (f32[8,32,128]{2,1,0:T(8,128)S(1)}, f32[8,32,128]{2,1,0:T(8,128)S(1)}, u32[]{:S(2)}, u32[]{:S(2)}) collective-permute-start(f32[8,32,128]{2,1,0:T(8,128)S(1)} %get-tuple-element.37), channel_id=1, source_target_pairs={{0,6},{1,7},{2,0},{3,1},{4,2},{5,3},{6,4},{7,5},{8,14},{9,15},{10,... | collective-permute-start | bytes 393224 | tf_op jit(solution)/shard_map/ppermute | solution.py:270
  53.2 0.1 add.59
  53.3 2.5 %collective-permute-start.11 = (f32[8,32,128]{2,1,0:T(8,128)S(1)}, f32[8,32,128]{2,1,0:T(8,128)S(1)}, u32[]{:S(2)}, u32[]{:S(2)}) collective-permute-start(f32[8,32,128]{2,1,0:T(8,128)S(1)} %get-tuple-element.33), channel_id=1, source_target_pairs={{0,2},{1,3},{2,4},{3,5},{4,6},{5,7},{6,0},{7,1},{8,10},{9,11},{10,... | collective-permute-start | bytes 393224 | tf_op jit(solution)/shard_map/ppermute | solution.py:270
  55.7 1.6 %collective-permute-start.12 = (f32[8,32,128]{2,1,0:T(8,128)S(1)}, f32[8,32,128]{2,1,0:T(8,128)S(1)}, u32[]{:S(2)}, u32[]{:S(2)}) collective-permute-start(f32[8,32,128]{2,1,0:T(8,128)S(1)} %get-tuple-element.35), channel_id=1, source_target_pairs={{0,4},{1,5},{2,6},{3,7},{4,0},{5,1},{6,2},{7,3},{8,12},{9,13},{10,... | collective-permute-start | bytes 393224 | tf_op jit(solution)/shard_map/ppermute | solution.py:270
  57.3 1.1 %collective-permute-start.13 = (f32[8,32,128]{2,1,0:T(8,128)S(1)}, f32[8,32,128]{2,1,0:T(8,128)S(1)}, u32[]{:S(2)}, u32[]{:S(2)}) collective-permute-start(f32[8,32,128]{2,1,0:T(8,128)S(1)} %get-tuple-element.34), channel_id=1, source_target_pairs={{0,6},{1,7},{2,0},{3,1},{4,2},{5,3},{6,4},{7,5},{8,14},{9,15},{10,... | collective-permute-start | bytes 393224 | tf_op jit(solution)/shard_map/ppermute | solution.py:270
  58.5 1.0 %collective-permute-done.16 = f32[8,32,128]{2,1,0:T(8,128)S(1)} collective-permute-done((f32[8,32,128]{2,1,0:T(8,128)S(1)}, f32[8,32,128]{2,1,0:T(8,128)S(1)}, u32[]{:S(2)}, u32[]{:S(2)}) %collective-permute-start.16) | collective-permute-done | bytes 131104 | tf_op jit(solution)/shard_map/ppermute | solution.py:270
  59.4 3.6 %collective-permute-done.17 = f32[8,32,128]{2,1,0:T(8,128)S(1)} collective-permute-done((f32[8,32,128]{2,1,0:T(8,128)S(1)}, f32[8,32,128]{2,1,0:T(8,128)S(1)}, u32[]{:S(2)}, u32[]{:S(2)}) %collective-permute-start.17) | collective-permute-done | bytes 131104 | tf_op jit(solution)/shard_map/ppermute | solution.py:270
  63.0 0.1 collective-permute-start.18
  63.8 1.3 %collective-permute-done.12 = f32[8,32,128]{2,1,0:T(8,128)S(1)} collective-permute-done((f32[8,32,128]{2,1,0:T(8,128)S(1)}, f32[8,32,128]{2,1,0:T(8,128)S(1)}, u32[]{:S(2)}, u32[]{:S(2)}) %collective-permute-start.12) | collective-permute-done | bytes 131104 | tf_op jit(solution)/shard_map/ppermute | solution.py:270
  65.1 1.7 %collective-permute-done.13 = f32[8,32,128]{2,1,0:T(8,128)S(1)} collective-permute-done((f32[8,32,128]{2,1,0:T(8,128)S(1)}, f32[8,32,128]{2,1,0:T(8,128)S(1)}, u32[]{:S(2)}, u32[]{:S(2)}) %collective-permute-start.13) | collective-permute-done | bytes 131104 | tf_op jit(solution)/shard_map/ppermute | solution.py:270
  66.8 4.7 %collective-permute-done.18 = f32[8,32,128]{2,1,0:T(8,128)S(1)} collective-permute-done((f32[8,32,128]{2,1,0:T(8,128)S(1)}, f32[8,32,128]{2,1,0:T(8,128)S(1)}, u32[]{:S(2)}, u32[]{:S(2)}) %collective-permute-start.18) | collective-permute-done | bytes 131104 | tf_op jit(solution)/shard_map/ppermute | solution.py:289
  71.5 0.1 collective-permute-start.19
  71.6 1.5 %collective-permute-start.20 = (f32[8,32,128]{2,1,0:T(8,128)S(1)}, f32[8,32,128]{2,1,0:T(8,128)S(1)}, u32[]{:S(2)}, u32[]{:S(2)}) collective-permute-start(f32[8,32,128]{2,1,0:T(8,128)S(1)} %get-tuple-element.39), channel_id=1, source_target_pairs={{0,4},{1,5},{2,6},{3,7},{4,0},{5,1},{6,2},{7,3},{8,12},{9,13},{10,... | collective-permute-start | bytes 393224 | tf_op jit(solution)/shard_map/ppermute | solution.py:270
  73.1 1.3 %collective-permute-start.21 = (f32[8,32,128]{2,1,0:T(8,128)S(1)}, f32[8,32,128]{2,1,0:T(8,128)S(1)}, u32[]{:S(2)}, u32[]{:S(2)}) collective-permute-start(f32[8,32,128]{2,1,0:T(8,128)S(1)} %get-tuple-element.31), channel_id=1, source_target_pairs={{0,6},{1,7},{2,0},{3,1},{4,2},{5,3},{6,4},{7,5},{8,14},{9,15},{10,... | collective-permute-start | bytes 393224 | tf_op jit(solution)/shard_map/ppermute | solution.py:270
  74.4 2.2 %collective-permute-done.19.refs_1_ = f32[8,32,128]{2,1,0:T(8,128)S(1)} collective-permute-done((f32[8,32,128]{2,1,0:T(8,128)S(1)}, f32[8,32,128]{2,1,0:T(8,128)S(1)}, u32[]{:S(2)}, u32[]{:S(2)}) %collective-permute-start.19) | collective-permute-done | bytes 131104 | tf_op jit(solution)/shard_map/ppermute | solution.py:270
  76.6 2.1 %collective-permute-done.20.refs_2_ = f32[8,32,128]{2,1,0:T(8,128)S(1)} collective-permute-done((f32[8,32,128]{2,1,0:T(8,128)S(1)}, f32[8,32,128]{2,1,0:T(8,128)S(1)}, u32[]{:S(2)}, u32[]{:S(2)}) %collective-permute-start.20) | collective-permute-done | bytes 131104 | tf_op jit(solution)/shard_map/ppermute | solution.py:270
  78.7 1.3 %collective-permute-done.21.refs_3_ = f32[8,32,128]{2,1,0:T(8,128)S(1)} collective-permute-done((f32[8,32,128]{2,1,0:T(8,128)S(1)}, f32[8,32,128]{2,1,0:T(8,128)S(1)}, u32[]{:S(2)}, u32[]{:S(2)}) %collective-permute-start.21) | collective-permute-done | bytes 131104 | tf_op jit(solution)/shard_map/ppermute | solution.py:270
  80.0 0.8 %settle.1 = f32[32,32,128]{2,1,0:T(8,128)} custom-call(s32[1]{0:T(128)} %bitcast.band, f32[8,32,128]{2,1,0:T(8,128)S(1)} %get-tuple-element.41.refs_0_, f32[8,32,128]{2,1,0:T(8,128)S(1)} %collective-permute-done.19.refs_1_, f32[8,32,128]{2,1,0:T(8,128)S(1)} %collective-permute-done.20.refs_2_, f32[8,32,128]{2,1,0:T(8,128)S(1)} %collective-permute-done.21.refs_3_), custom_call_target="tpu_custom_call" | custom-call | tf_op jit(solution)/shard_map/settle/pallas_call | solution.py:373
  (17 shorter events, 0.3 us)
Async XLA Ops:
  0.0 17.7 %all-to-all-start = ((f32[4,8,32,128]{3,2,1,0:T(8,128)}), f32[4,8,32,128]{3,2,1,0:T(8,128)S(1)}, u32[]{:S(2)}, u32[]{:S(2)}) async-start(f32[4,8,32,128]{3,2,1,0:T(8,128)} %bitcast.35), calls=%async_computation | async-start | bytes 1048576 | tf_op jit(solution)/shard_map/all_to_all | solution.py:275
  5.4 8.9 %collective-permute-start = (s32[1,1]{1,0:T(1,128)}, s32[1,1]{1,0:T(1,128)}, u32[]{:S(2)}, u32[]{:S(2)}) collective-permute-start(s32[1,1]{1,0:T(1,128)} %param.10), channel_id=1, source_target_pairs={{0,8},{8,16},{16,24},{24,32},{32,40},{40,48},{48,56},{56,64},{64,7... | collective-permute-start | bytes 20 | tf_op jit(solution)/shard_map/ppermute | solution.py:289
  14.3 1.2 %copy-start = (bf16[1,1,64,64,128]{4,3,2,1,0:T(8,128)(2,1)S(1)}, bf16[1,1,64,64,128]{4,3,2,1,0:T(8,128)(2,1)}, u32[]{:S(2)}) copy-start(bf16[1,1,64,64,128]{4,3,2,1,0:T(8,128)(2,1)} %param.8) | copy-start | bytes 3145732
  15.6 0.9 %copy-start.1 = (bf16[544,128]{1,0:T(8,128)(2,1)S(1)}, bf16[544,128]{1,0:T(8,128)(2,1)}, u32[]{:S(2)}) copy-start(bf16[544,128]{1,0:T(8,128)(2,1)} %constant.59.consts) | copy-start | bytes 417796
  18.3 6.0 %collective-permute-start.1 = (f32[8,32,128]{2,1,0:T(8,128)S(1)}, f32[8,32,128]{2,1,0:T(8,128)S(1)}, u32[]{:S(2)}, u32[]{:S(2)}) collective-permute-start(f32[8,32,128]{2,1,0:T(8,128)S(1)} %get-tuple-element.19), channel_id=1, source_target_pairs={{0,248},{8,0},{16,8},{24,16},{32,24},{40,32},{48,40},{56,48},{64,5... | collective-permute-start | bytes 393224 | tf_op jit(solution)/shard_map/ppermute | solution.py:289
  20.9 7.4 %collective-permute-start.2 = (f32[8,32,128]{2,1,0:T(8,128)S(1)}, f32[8,32,128]{2,1,0:T(8,128)S(1)}, u32[]{:S(2)}, u32[]{:S(2)}) collective-permute-start(f32[8,32,128]{2,1,0:T(8,128)S(1)} %get-tuple-element.23.refs_0_), channel_id=1, source_target_pairs={{0,2},{1,3},{2,4},{3,5},{4,6},{5,7},{6,0},{7,1},{8,10},{9,11},{10,... | collective-permute-start | bytes 393224 | tf_op jit(solution)/shard_map/ppermute | solution.py:270
  22.9 6.6 %collective-permute-start.3 = (f32[8,32,128]{2,1,0:T(8,128)S(1)}, f32[8,32,128]{2,1,0:T(8,128)S(1)}, u32[]{:S(2)}, u32[]{:S(2)}) collective-permute-start(f32[8,32,128]{2,1,0:T(8,128)S(1)} %get-tuple-element.23.refs_0_), channel_id=1, source_target_pairs={{0,4},{1,5},{2,6},{3,7},{4,0},{5,1},{6,2},{7,3},{8,12},{9,13},{10,... | collective-permute-start | bytes 393224 | tf_op jit(solution)/shard_map/ppermute | solution.py:270
  23.4 7.4 %collective-permute-start.4 = (f32[8,32,128]{2,1,0:T(8,128)S(1)}, f32[8,32,128]{2,1,0:T(8,128)S(1)}, u32[]{:S(2)}, u32[]{:S(2)}) collective-permute-start(f32[8,32,128]{2,1,0:T(8,128)S(1)} %get-tuple-element.23.refs_0_), channel_id=1, source_target_pairs={{0,6},{1,7},{2,0},{3,1},{4,2},{5,3},{6,4},{7,5},{8,14},{9,15},{10,... | collective-permute-start | bytes 393224 | tf_op jit(solution)/shard_map/ppermute | solution.py:270
  30.8 2.2 %collective-permute-start.5 = (f32[4,8,32,128]{3,2,1,0:T(8,128)S(1)}, f32[4,8,32,128]{3,2,1,0:T(8,128)S(1)}, u32[]{:S(2)}, u32[]{:S(2)}) collective-permute-start(f32[4,8,32,128]{3,2,1,0:T(8,128)S(1)} %stack.2.own), channel_id=1, source_target_pairs={{0,1},{1,0},{2,3},{3,2},{4,5},{5,4},{6,7},{7,6},{8,9},{9,8},{10,11... | collective-permute-start | bytes 1572872 | tf_op jit(solution)/shard_map/ppermute | solution.py:284
  30.9 6.7 %collective-permute-start.6 = (f32[8,32,128]{2,1,0:T(8,128)S(1)}, f32[8,32,128]{2,1,0:T(8,128)S(1)}, u32[]{:S(2)}, u32[]{:S(2)}) collective-permute-start(f32[8,32,128]{2,1,0:T(8,128)S(1)} %collective-permute-done.1.after.refs_0_), channel_id=1, source_target_pairs={{0,2},{1,3},{2,4},{3,5},{4,6},{5,7},{6,0},{7,1},{8,10},{9,11},{10,... | collective-permute-start | bytes 393224 | tf_op jit(solution)/shard_map/ppermute | solution.py:270
  31.6 7.8 %collective-permute-start.7 = (f32[8,32,128]{2,1,0:T(8,128)S(1)}, f32[8,32,128]{2,1,0:T(8,128)S(1)}, u32[]{:S(2)}, u32[]{:S(2)}) collective-permute-start(f32[8,32,128]{2,1,0:T(8,128)S(1)} %collective-permute-done.1.after.refs_0_), channel_id=1, source_target_pairs={{0,4},{1,5},{2,6},{3,7},{4,0},{5,1},{6,2},{7,3},{8,12},{9,13},{10,... | collective-permute-start | bytes 393224 | tf_op jit(solution)/shard_map/ppermute | solution.py:270
  32.7 8.8 %collective-permute-start.8 = (f32[8,32,128]{2,1,0:T(8,128)S(1)}, f32[8,32,128]{2,1,0:T(8,128)S(1)}, u32[]{:S(2)}, u32[]{:S(2)}) collective-permute-start(f32[8,32,128]{2,1,0:T(8,128)S(1)} %collective-permute-done.1.after.refs_0_), channel_id=1, source_target_pairs={{0,6},{1,7},{2,0},{3,1},{4,2},{5,3},{6,4},{7,5},{8,14},{9,15},{10,... | collective-permute-start | bytes 393224 | tf_op jit(solution)/shard_map/ppermute | solution.py:270
  41.5 2.0 %collective-permute-start.9 = (f32[4,8,32,128]{3,2,1,0:T(8,128)S(1)}, f32[4,8,32,128]{3,2,1,0:T(8,128)S(1)}, u32[]{:S(2)}, u32[]{:S(2)}) collective-permute-start(f32[4,8,32,128]{3,2,1,0:T(8,128)S(1)} %stack.3.own), channel_id=1, source_target_pairs={{0,1},{1,0},{2,3},{3,2},{4,5},{5,4},{6,7},{7,6},{8,9},{9,8},{10,11... | collective-permute-start | bytes 1572872 | tf_op jit(solution)/shard_map/ppermute | solution.py:284
  48.5 2.0 %collective-permute-start.14 = (f32[4,8,32,128]{3,2,1,0:T(8,128)S(1)}, f32[4,8,32,128]{3,2,1,0:T(8,128)S(1)}, u32[]{:S(2)}, u32[]{:S(2)}) collective-permute-start(f32[4,8,32,128]{3,2,1,0:T(8,128)S(1)} %get-tuple-element.30), channel_id=1, source_target_pairs={{0,1},{1,0},{2,3},{3,2},{4,5},{5,4},{6,7},{7,6},{8,9},{9,8},{10,11... | collective-permute-start | bytes 1572872 | tf_op jit(solution)/shard_map/ppermute | solution.py:284
  48.7 4.5 %collective-permute-start.10 = (f32[4,8,32,128]{3,2,1,0:T(8,128)S(1)}, f32[4,8,32,128]{3,2,1,0:T(8,128)S(1)}, u32[]{:S(2)}, u32[]{:S(2)}) collective-permute-start(f32[4,8,32,128]{3,2,1,0:T(8,128)S(1)} %get-tuple-element.28), channel_id=1, source_target_pairs={{0,1},{1,0},{2,3},{3,2},{4,5},{5,4},{6,7},{7,6},{8,9},{9,8},{10,11... | collective-permute-start | bytes 1572872 | tf_op jit(solution)/shard_map/ppermute | solution.py:284
  50.6 6.7 %collective-permute-start.15 = (f32[8,32,128]{2,1,0:T(8,128)S(1)}, f32[8,32,128]{2,1,0:T(8,128)S(1)}, u32[]{:S(2)}, u32[]{:S(2)}) collective-permute-start(f32[8,32,128]{2,1,0:T(8,128)S(1)} %get-tuple-element.36), channel_id=1, source_target_pairs={{0,2},{1,3},{2,4},{3,5},{4,6},{5,7},{6,0},{7,1},{8,10},{9,11},{10,... | collective-permute-start | bytes 393224 | tf_op jit(solution)/shard_map/ppermute | solution.py:270
  51.6 7.9 %collective-permute-start.16 = (f32[8,32,128]{2,1,0:T(8,128)S(1)}, f32[8,32,128]{2,1,0:T(8,128)S(1)}, u32[]{:S(2)}, u32[]{:S(2)}) collective-permute-start(f32[8,32,128]{2,1,0:T(8,128)S(1)} %get-tuple-element.38), channel_id=1, source_target_pairs={{0,4},{1,5},{2,6},{3,7},{4,0},{5,1},{6,2},{7,3},{8,12},{9,13},{10,... | collective-permute-start | bytes 393224 | tf_op jit(solution)/shard_map/ppermute | solution.py:270
  52.3 10.7 %collective-permute-start.17 = (f32[8,32,128]{2,1,0:T(8,128)S(1)}, f32[8,32,128]{2,1,0:T(8,128)S(1)}, u32[]{:S(2)}, u32[]{:S(2)}) collective-permute-start(f32[8,32,128]{2,1,0:T(8,128)S(1)} %get-tuple-element.37), channel_id=1, source_target_pairs={{0,6},{1,7},{2,0},{3,1},{4,2},{5,3},{6,4},{7,5},{8,14},{9,15},{10,... | collective-permute-start | bytes 393224 | tf_op jit(solution)/shard_map/ppermute | solution.py:270
  53.3 10.5 %collective-permute-start.11 = (f32[8,32,128]{2,1,0:T(8,128)S(1)}, f32[8,32,128]{2,1,0:T(8,128)S(1)}, u32[]{:S(2)}, u32[]{:S(2)}) collective-permute-start(f32[8,32,128]{2,1,0:T(8,128)S(1)} %get-tuple-element.33), channel_id=1, source_target_pairs={{0,2},{1,3},{2,4},{3,5},{4,6},{5,7},{6,0},{7,1},{8,10},{9,11},{10,... | collective-permute-start | bytes 393224 | tf_op jit(solution)/shard_map/ppermute | solution.py:270
  55.7 9.3 %collective-permute-start.12 = (f32[8,32,128]{2,1,0:T(8,128)S(1)}, f32[8,32,128]{2,1,0:T(8,128)S(1)}, u32[]{:S(2)}, u32[]{:S(2)}) collective-permute-start(f32[8,32,128]{2,1,0:T(8,128)S(1)} %get-tuple-element.35), channel_id=1, source_target_pairs={{0,4},{1,5},{2,6},{3,7},{4,0},{5,1},{6,2},{7,3},{8,12},{9,13},{10,... | collective-permute-start | bytes 393224 | tf_op jit(solution)/shard_map/ppermute | solution.py:270
  57.3 9.4 %collective-permute-start.13 = (f32[8,32,128]{2,1,0:T(8,128)S(1)}, f32[8,32,128]{2,1,0:T(8,128)S(1)}, u32[]{:S(2)}, u32[]{:S(2)}) collective-permute-start(f32[8,32,128]{2,1,0:T(8,128)S(1)} %get-tuple-element.34), channel_id=1, source_target_pairs={{0,6},{1,7},{2,0},{3,1},{4,2},{5,3},{6,4},{7,5},{8,14},{9,15},{10,... | collective-permute-start | bytes 393224 | tf_op jit(solution)/shard_map/ppermute | solution.py:270
  63.0 8.4 %collective-permute-start.18 = (f32[8,32,128]{2,1,0:T(8,128)S(1)}, f32[8,32,128]{2,1,0:T(8,128)S(1)}, u32[]{:S(2)}, u32[]{:S(2)}) collective-permute-start(f32[8,32,128]{2,1,0:T(8,128)S(1)} %fusion.2), channel_id=1, source_target_pairs={{0,8},{8,16},{16,24},{24,32},{32,40},{40,48},{48,56},{56,64},{64,7... | collective-permute-start | bytes 393224 | tf_op jit(solution)/shard_map/ppermute | solution.py:289
  71.5 5.0 %collective-permute-start.19 = (f32[8,32,128]{2,1,0:T(8,128)S(1)}, f32[8,32,128]{2,1,0:T(8,128)S(1)}, u32[]{:S(2)}, u32[]{:S(2)}) collective-permute-start(f32[8,32,128]{2,1,0:T(8,128)S(1)} %get-tuple-element.40), channel_id=1, source_target_pairs={{0,2},{1,3},{2,4},{3,5},{4,6},{5,7},{6,0},{7,1},{8,10},{9,11},{10,... | collective-permute-start | bytes 393224 | tf_op jit(solution)/shard_map/ppermute | solution.py:270
  71.6 7.1 %collective-permute-start.20 = (f32[8,32,128]{2,1,0:T(8,128)S(1)}, f32[8,32,128]{2,1,0:T(8,128)S(1)}, u32[]{:S(2)}, u32[]{:S(2)}) collective-permute-start(f32[8,32,128]{2,1,0:T(8,128)S(1)} %get-tuple-element.39), channel_id=1, source_target_pairs={{0,4},{1,5},{2,6},{3,7},{4,0},{5,1},{6,2},{7,3},{8,12},{9,13},{10,... | collective-permute-start | bytes 393224 | tf_op jit(solution)/shard_map/ppermute | solution.py:270
  73.1 6.9 %collective-permute-start.21 = (f32[8,32,128]{2,1,0:T(8,128)S(1)}, f32[8,32,128]{2,1,0:T(8,128)S(1)}, u32[]{:S(2)}, u32[]{:S(2)}) collective-permute-start(f32[8,32,128]{2,1,0:T(8,128)S(1)} %get-tuple-element.31), channel_id=1, source_target_pairs={{0,6},{1,7},{2,0},{3,1},{4,2},{5,3},{6,4},{7,5},{8,14},{9,15},{10,... | collective-permute-start | bytes 393224 | tf_op jit(solution)/shard_map/ppermute | solution.py:270

commit v4 on v3

--- a/solution.py
+++ b/solution.py
@@ -75,17 +75,13 @@
     def side_by_side(pieces):
         return jnp.concatenate([p.reshape(-1, p.shape[2]) for p in pieces], axis=1)
 
-    upper = side_by_side(uppers)
-    if lowers is None:
-        inputs = [split(upper)] * 2
-    else:
-        lower = side_by_side(lowers)
-        inputs = [split(lower + upper), split(lower - upper)]
+    lower, upper = side_by_side(lowers), side_by_side(uppers)
+    inputs = [split(lower + upper), split(lower - upper)]
     even, odd = (
         dot(z_ref[2 * i], high) + dot(z_ref[2 * i + 1], high) + dot(z_ref[2 * i], low)
         for i, (high, low) in enumerate(inputs)
     )
-    return (even - odd, even + odd) if lowers is None else (even + odd, even - odd)
+    return even + odd, even - odd
 
 
 def tiles(i):
@@ -104,7 +100,7 @@
     return jnp.sum(block.reshape(-1, 8, block.shape[-1]), axis=0)
 
 
-def prepare(code, order_before, wave, consts, states, x_ref, y_ref, z_ref):
+def prepare(code, wave, consts, states, partly, x_ref, y_ref, z_ref):
     depth, width, length = states.shape
     double = code[0, 0] & 1
     x_row = jnp.concatenate([consts[:length], consts[length : 2 * length]], axis=1)
@@ -124,11 +120,12 @@
         z_ref[i] = jnp.where((rows & 7) == (cols & 7), full, 0.0).astype(jnp.bfloat16)
     live = lax.broadcasted_iota(jnp.int32, (1, width, length), 1) < (width // 2) * (1 + double)
 
-    def masked(i, carry):
-        states[pl.ds(i * 4, 4)] = jnp.where(live, wave[pl.ds(i * 4, 4)].astype(jnp.float32), 0.0)
-        return carry
-
-    lax.fori_loop(0, depth // 4, masked, 0)
+    def masked(z):
+        s = jnp.where(live, wave[pl.ds(z, 8)].astype(jnp.float32), 0.0)
+        states[pl.ds(z, 8)] = s
+        return s
+
+    xy_pass(masked, partly, 0, depth, x_ref, y_ref, True)
 
 
 def xy_pass(read, out, start, lines, x_ref, y_ref, exact):
@@ -145,20 +142,24 @@
     lax.fori_loop(0, lines // 8, step, 0)
 
 
-def first_kinetic(after, states, x_ref, y_ref, z_ref, out):
-    depth, width, length = out.shape
+def kinetics(after, states, partly, x_ref, y_ref, z_ref, once, again):
+    depth, width, length = once.shape
     half = depth // 2
-    xy_pass(lambda z: states[pl.ds(z, 8)], out, 0, depth, x_ref, y_ref, True)
-
-    def zz(i, carry):
-        halves = [[states[pl.ds(j * half, half), r] for r in tiles(i)] for j in range(2)]
-        for j, part in enumerate(z_part(*halves, z_ref)):
-            for k, r in enumerate(tiles(i)):
-                at = pl.ds(j * half, half)
-                out[at, r] = out[at, r] + cut(part, k, length)
-        return carry
-
-    lax.fori_loop(0, width // 16, zz, 0)
+
+    def z_pass(source, before, out):
+        def zz(i, carry):
+            halves = [[source[pl.ds(j * half, half), r] for r in tiles(i)] for j in range(2)]
+            for j, part in enumerate(z_part(*halves, z_ref)):
+                for k, r in enumerate(tiles(i)):
+                    at = pl.ds(j * half, half)
+                    out[at, r] = before[at, r] + cut(part, k, length)
+            return carry
+
+        lax.fori_loop(0, width // 16, zz, 0)
+
+    z_pass(states, partly, once)
+    xy_pass(lambda z: once[pl.ds(z, 8)], again, 0, depth, x_ref, y_ref, False)
+    z_pass(once, again, again)
 
 
 def box_rows(band, code, column):
@@ -166,12 +167,15 @@
     return [pl.ds(pl.multiple_of(i * column, column), column) for i in (at, 1 - at)]
 
 
-def line_loop(band, code, columns, use):
+CHUNKS = ((0, 0), (0, 1), (0, 3), (1, 0), (1, 1), (1, 3), (0, 2), (1, 2))
+
+
+def line_loop(band, code, columns, half, use):
     chip = band[0] >> 1
     for ref, rows in zip(columns, box_rows(band, code, columns[0].shape[2])):
         chunk = ref.shape[1]
-        for m in range(CHIPS):
-            start = ((chip - m) & (CHIPS - 1)) * chunk
+        for m, (slab, back) in enumerate(CHUNKS):
+            start = slab * half + ((chip - back) & (CHIPS - 1)) * chunk
 
             def line(i, carry, ref=ref, rows=rows, m=m, start=start):
                 use(rows, start + i, ref[m, i])
@@ -180,54 +184,29 @@
             lax.fori_loop(0, chunk, line, 0, unroll=2)
 
 
-def lower_half(band, code, states, kinetic, x_ref, y_ref, z_ref, own, other, pot, applied, again):
-    half, width, length = pot.shape
+def both_steps(band, code, states, kinetic, again, x_ref, y_ref, z_ref, own, other, *refs):
+    (keep0, give0, keep1, give1), (pot, forced, total_h, extra, twice) = refs[:4], refs[4:]
+    depth, width, length = pot.shape
+    half, column, double = depth // 2, width // 2, code[0, 0] & 1
+    chunk = half // CHIPS
 
     def use(rows, z, v):
         pot[z, rows] = v
-        applied[z, rows] = kinetic[z, rows] + v * states[z, rows]
-
-    line_loop(band, code, (own, other), use)
-    xy_pass(lambda z: applied[pl.ds(z, 8)], again, 0, half, x_ref, y_ref, False)
-    xy_pass(lambda z: kinetic[pl.ds(z, 8)], again, half, half, x_ref, y_ref, False)
-
-    def zz(i, carry):
-        lowers = [applied[:, r] for r in tiles(i)]
-        uppers = [kinetic[pl.ds(half, half), r] for r in tiles(i)]
-        for j, part in enumerate(z_part(lowers, uppers, z_ref)):
-            for k, r in enumerate(tiles(i)):
-                at = pl.ds(j * half, half)
-                again[at, r] = again[at, r] + cut(part, k, length)
-        return carry
-
-    lax.fori_loop(0, width // 16, zz, 0)
-
-
-def both_steps(band, code, states, kinetic, x_ref, y_ref, z_ref, pot, applied, again, own, other, *refs):
-    (keep0, give0, keep1, give1), (pot_up, forced, applied_up, extra, twice) = refs[:4], refs[4:]
-    half, width, length = pot.shape
-    chunk, column, double = half // CHIPS, width // 2, code[0, 0] & 1
-
-    def use(rows, z, v):
-        change = v * states[half + z, rows]
-        pot_up[z, rows] = v
-        forced[z, rows] = change
-        applied_up[z, rows] = kinetic[half + z, rows] + change
-
-    line_loop(band, code, (own, other), use)
-    xy_pass(lambda z: forced[pl.ds(z, 8)], extra, 0, half, x_ref, y_ref, False)
+        forced[z, rows] = v * states[z, rows]
+
+    line_loop(band, code, (own, other), half, use)
+    xy_pass(lambda z: forced[pl.ds(z, 8)], extra, 0, depth, x_ref, y_ref, False)
 
     def zz(i, sums):
-        low_part, high_part = z_part(None, [forced[:, r] for r in tiles(i)], z_ref)
+        places = [pl.ds(0, half), pl.ds(half, half)]
+        parts = z_part(*[[forced[at, r] for r in tiles(i)] for at in places], z_ref)
         for k, r in enumerate(tiles(i)):
-            low, high = pl.ds(0, half), pl.ds(half, half)
-            h, h_up = applied[:, r], applied_up[:, r]
-            w = again[low, r] + cut(low_part, k, length) + pot[:, r] * h
-            w_up = again[high, r] + extra[:, r] + cut(high_part, k, length) + pot_up[:, r] * h_up
-            twice[low, r] = w
-            twice[high, r] = w_up
             pairs = []
-            for s, h, w in ((states[low, r], h, w), (states[high, r], h_up, w_up)):
+            for at, part in zip(places, parts):
+                s, h = states[at, r], kinetic[at, r] + forced[at, r]
+                w = again[at, r] + extra[at, r] + cut(part, k, length) + pot[at, r] * h
+                total_h[at, r] = h
+                twice[at, r] = w
                 pairs.append((s * s, s * h, h * h, s * w, h * w, w * w))
             sums = tuple(v + fold(a + b) for v, a, b in zip(sums, *pairs))
         return sums
@@ -245,15 +224,14 @@
     sign = (2 * double - 1).astype(jnp.float32)
     factor = sign / 8.0 * square * cells / (square * weight + EPSILON)
     by_s, by_h, by_w = second * first, -STEP_LENGTH * (first + second), STEP_LENGTH * STEP_LENGTH
-    for slab, outs, source in ((1, (keep1, give1), applied_up), (0, (keep0, give0), applied)):
+    for slab, outs in ((1, (keep1, give1)), (0, (keep0, give0))):
         for out, rows in zip(outs, box_rows(band, code, column)):
             for k in range(CHIPS):
                 start = (((band[0] >> 1) + k) & (CHIPS - 1)) * chunk
 
-                def line(i, carry, out=out, rows=rows, start=start, k=k, slab=slab, source=source):
-                    z = start + i
-                    at = slab * half + z
-                    u = by_s * states[at, rows] + by_h * source[z, rows] + by_w * twice[at, rows]
+                def line(i, carry, out=out, rows=rows, start=start, k=k, slab=slab):
+                    at = slab * half + start + i
+                    u = by_s * states[at, rows] + by_h * total_h[at, rows] + by_w * twice[at, rows]
                     out[k, i] = factor * (u * u)
                     return carry
 
@@ -261,18 +239,17 @@
 
 
 def stack(after, *refs):
-    for i, block in enumerate(refs[:-1]):
-        refs[-1][i] = block[...]
+    out, at = refs[-1], 0
+    for block in refs[:-1]:
+        parts = [block[...]] if len(block.shape) < len(out.shape) else [block[i] for i in range(block.shape[0])]
+        for part in parts:
+            out[at] = part
+            at += 1
 
 
 def to_next_chip(block, k):
     m = 2 * CHIPS
     return lax.ppermute(block, "band", [(b, (b + 2 * k) % m) for b in range(m)])
-
-
-def exchange(blocks):
-    cores = [[2 * chip + core for chip in range(CHIPS)] for core in range(2)]
-    return lax.all_to_all(blocks, "band", 0, 0, axis_index_groups=cores)
 
 
 def around(blocks):
@@ -295,10 +272,21 @@
     return upper, ((low + upper) & (2 * CHIPS - 1)) >> 1
 
 
-def pick(band, code, code_before, after, pieces, below, here):
-    for out, order in ((below, code_before), (here, code)):
+def cut_chunks(band, potential, *outs):
+    for k, out in enumerate(outs):
+        at = (((band[0] >> 1) + k) & (CHIPS - 1)) * out.shape[0]
+        out[...] = potential[pl.ds(at, out.shape[0])]
+
+
+def pick(band, code, code_before, after, *refs):
+    for out, order in zip(refs[CHIPS:], (code_before, code)):
         _, owner = place(band[0] & 1, order[0, 0])
-        out[...] = pieces[owner]
+        source = ((band[0] >> 1) - owner) & (CHIPS - 1)
+        for k in range(CHIPS):
+
+            @pl.when(source == k)
+            def _(k=k, out=out):
+                out[...] = refs[k][...]
 
 
 def settle(band, *refs):
@@ -314,12 +302,11 @@
     band = lax.axis_index("band").astype(jnp.int32)
     core = band & 1
     order_before = to_group(fragment_order, 1)
-    pieces = exchange(potential.reshape(CHIPS, chunk, column, length))
 
     small = pltpu.CompilerParams(vmem_limit_bytes=4 * 1024 * 1024)
-    piece, quarter, half_box, box = (
+    piece, quarter, box = (
         jax.ShapeDtypeStruct(shape + (length,), jnp.float32)
-        for shape in ((chunk, column), (CHIPS, chunk, column), (depth // 2, width), (depth, width))
+        for shape in ((chunk, column), (CHIPS, chunk, column), (depth, width))
     )
     square = (4 * width, 4 * width)
     ops = [jax.ShapeDtypeStruct(lead + square, jnp.bfloat16) for lead in ((), (2,), (4,))]
@@ -336,26 +323,30 @@
             name=function.__name__,
         )
 
-    states, *ops = kernel(prepare, [box] + ops, [SMEM, ANY, VMEM, VMEM], MIDDLE)(
-        fragment_order, order_before, wave, operators(depth, width, length)
-    )
-    below, here = kernel(pick, [piece] * 2, [SMEM] * 3 + [ANY, VMEM], small)(
-        band[None], fragment_order, order_before, states, pieces
+    pieces = around(kernel(cut_chunks, [piece] * CHIPS, [SMEM, VMEM], small)(band[None], potential))
+    states, partly, *ops = kernel(prepare, [box] * 2 + ops, [SMEM, VMEM, VMEM], MIDDLE)(
+        fragment_order, wave, operators(depth, width, length)
+    )
+    below, here = kernel(pick, [piece] * 2, [SMEM] * 3 + [ANY] + [VMEM] * CHIPS, small)(
+        band[None], fragment_order, order_before, states, *pieces
     )
     below = to_group(below, -1)
-    lower, upper = around([here] * CHIPS), around([below] * CHIPS)
-    (kinetic,) = kernel(first_kinetic, [box], [ANY] + [VMEM] * 4, MIDDLE, flops=3_000_000_000)(below, states, *ops)
-
-    def two_columns(after, blocks):
-        (own,) = kernel(stack, [quarter], [ANY] + [VMEM] * CHIPS, small)(after, *blocks)
-        return own, to_other_core(own)
-
-    pot, applied, again = kernel(
-        lower_half, [half_box] * 2 + [box], [SMEM] * 2 + [VMEM] * 7, MIDDLE, flops=4_000_000_000
-    )(band[None], fragment_order, states, kinetic, *ops, *two_columns(kinetic, lower))
+
+    def stacked(after, *blocks):
+        count = sum(1 if block.ndim == 3 else block.shape[0] for block in blocks)
+        out = jax.ShapeDtypeStruct((count, chunk, column, length), jnp.float32)
+        return kernel(stack, [out], [ANY] + [VMEM] * len(blocks), small)(after, *blocks)[0]
+
+    near = [here] + [to_next_chip(here, k) for k in (1, 3)]
+    both = stacked(states, here, below)
+    far = [below] + [to_next_chip(below, k) for k in (1, 3)] + [to_next_chip(both, 2)]
+    kinetic, again = kernel(kinetics, [box] * 2, [ANY] + [VMEM] * 5, MIDDLE, flops=4_000_000_000)(
+        both, states, partly, *ops
+    )
+    own = stacked(again, *near, *far)
     keep0, give0, keep1, give1 = kernel(
-        both_steps, [quarter] * 4, [SMEM] * 2 + [VMEM] * 10, BIG, scratch=[half_box] * 4 + [box]
-    )(band[None], fragment_order, states, kinetic, *ops, pot, applied, again, *two_columns(again, upper))
+        both_steps, [quarter] * 4, [SMEM] * 2 + [VMEM] * 8, BIG, scratch=[box] * 5
+    )(band[None], fragment_order, states, kinetic, again, *ops, own, to_other_core(own))
 
     def reduce_chip(keep, give):
         result, *arrived = around(list(keep + to_other_core(give)))

time: 81.1 us -> 77.9 us (0.961)
  waiting for transfers between devices: 34.9 us -> 28.2 us
  starting transfers between devices: 25.8 us -> 27.2 us
  Pallas kernels: 16.2 us -> 17.3 us
  local copies, waits for them, and re-layouts: 2.19 us -> 3.22 us
    all_to_all x1 -> x0, starting transfers between devices: 5.4 us -> none  [exchange(): return lax.all_to_all(blocks, 'band', 0, 0, axis_index_groups=cores)]
    ppermute x3, waiting for transfers between devices: 12.1 us -> 7.91 us  [to_group(): lax.ppermute(block, 'frag', [(i, (i + distance) % n) for i in range(n)])]
    ppermute x15 -> x17, starting transfers between devices: 16.2 us -> 19.9 us  [to_next_chip(): return lax.ppermute(block, 'band', [(b, (b + 2 * k) % m) for b in range(m)])]
    ppermute x3, starting transfers between devices: 3.39 us -> 6.61 us  [to_group(): lax.ppermute(block, 'frag', [(i, (i + distance) % n) for i in range(n)])]
    ppermute x15 -> x17, waiting for transfers between devices: 19.4 us -> 16.2 us  [to_next_chip(): return lax.ppermute(block, 'band', [(b, (b + 2 * k) % m) for b in range(m)])]
    pallas_call x7, Pallas kernels: 15.4 us -> 16.5 us  [the longest x1 6.99 us: body(): kernel(both_steps, [quarter] * 4, [SMEM] * 2 + [VMEM] * 8, BIG, scratch=[...]
    unnamed x4 -> x6, local copies, waits for them, and re-layouts: 2.13 us -> 3.17 us
    ppermute x4 -> x3, waiting for transfers between devices: 3.29 us -> 4.05 us  [to_other_core(): return lax.ppermute(block, 'band', [(b, b ^ 1) for b in range(2 * CHIPS)])]
  transfers between devices with their start and end apart: 23 -> 23, of which waited for: 15 -> 14; matrix products, arithmetic and copies ran while one was open for 0% -> 0% of each run, Pallas kernels for 12% -> 11%
where the time goes in v4:
time: 77.9 us; the launch traced here: 77.7 us
  waiting for transfers between devices  28.2 us (36%)
  starting transfers between devices  27.2 us (35%)
  Pallas kernels  17.3 us (22%)
  local copies, waits for them, and re-layouts  3.22 us (4%)
  between operations  1.43 us (2%)
    ppermute x17, starting transfers between devices, to_next_chip(): return lax.ppermute(block, 'band', [(b, (b + 2 * k) % m) for b in range(m)])  19.9 us
    ppermute x17, waiting for transfers between devices, to_next_chip(): return lax.ppermute(block, 'band', [(b, (b + 2 * k) % m) for b in range(m)])  16.2 us
    ppermute x3, waiting for transfers between devices, to_group(): lax.ppermute(block, 'frag', [(i, (i + distance) % n) for i in range(n)])  7.91 us
    pallas_call x1, Pallas kernels, body(): kernel(both_steps, [quarter] * 4, [SMEM] * 2 + [VMEM] * 8, BIG, scratch=[...  6.99 us
    ppermute x3, starting transfers between devices, to_group(): lax.ppermute(block, 'frag', [(i, (i + distance) % n) for i in range(n)])  6.61 us
    pallas_call x1, Pallas kernels, body(): kernel(kinetics, [box] * 2, [ANY] + [VMEM] * 5, MIDDLE, flops=4000000000)  6 us
    ppermute x3, waiting for transfers between devices, to_other_core(): return lax.ppermute(block, 'band', [(b, b ^ 1) for b in range(2 * CHIPS)])  4.05 us
    unnamed x6, local copies, waits for them, and re-layouts  3.17 us
  transfers between devices with their start and end apart: 23, of which 14 were waited for; matrix products, arithmetic and copies ran while one was open for 0% of the time, Pallas kernels for 11%

profile of v4, /device:TPU:24, one launch (start us, length us, event | category | flops | bytes accessed | tf_op | source)
XLA Modules:
  0.0 77.7 jit_solution(7113950628446581819)
XLA Ops:
  0.0 1.0 %copy-done.1 = f32[32,32,128]{2,1,0:T(8,128)S(1)} copy-done((f32[32,32,128]{2,1,0:T(8,128)S(1)}, f32[32,32,128]{2,1,0:T(8,128)}, u32[]{:S(2)}) %copy-start.1) | copy-done | bytes 524312
  1.1 2.0 %collective-permute-start.1 = (f32[8,32,128]{2,1,0:T(8,128)S(1)}, f32[8,32,128]{2,1,0:T(8,128)S(1)}, u32[]{:S(2)}, u32[]{:S(2)}) collective-permute-start(f32[8,32,128]{2,1,0:T(8,128)S(1)} %get-tuple-element.24), channel_id=1, source_target_pairs={{0,2},{1,3},{2,4},{3,5},{4,6},{5,7},{6,0},{7,1},{8,10},{9,11},{10,... | collective-permute-start | bytes 393224 | tf_op jit(solution)/shard_map/ppermute | solution.py:252
  3.1 0.9 %collective-permute-start.2 = (f32[8,32,128]{2,1,0:T(8,128)S(1)}, f32[8,32,128]{2,1,0:T(8,128)S(1)}, u32[]{:S(2)}, u32[]{:S(2)}) collective-permute-start(f32[8,32,128]{2,1,0:T(8,128)S(1)} %get-tuple-element.25), channel_id=1, source_target_pairs={{0,4},{1,5},{2,6},{3,7},{4,0},{5,1},{6,2},{7,3},{8,12},{9,13},{10,... | collective-permute-start | bytes 393224 | tf_op jit(solution)/shard_map/ppermute | solution.py:252
  4.0 0.1 collective-permute-start.3
  4.1 1.4 %collective-permute-start = (s32[1,1]{1,0:T(1,128)}, s32[1,1]{1,0:T(1,128)}, u32[]{:S(2)}, u32[]{:S(2)}) collective-permute-start(s32[1,1]{1,0:T(1,128)} %param.10), channel_id=1, source_target_pairs={{0,8},{8,16},{16,24},{24,32},{32,40},{40,48},{48,56},{56,64},{64,7... | collective-permute-start | bytes 20 | tf_op jit(solution)/shard_map/ppermute | solution.py:266
  6.2 1.2 %copy-done = bf16[1,1,64,64,128]{4,3,2,1,0:T(8,128)(2,1)S(1)} copy-done((bf16[1,1,64,64,128]{4,3,2,1,0:T(8,128)(2,1)S(1)}, bf16[1,1,64,64,128]{4,3,2,1,0:T(8,128)(2,1)}, u32[]{:S(2)}) %copy-start) | copy-done | bytes 1048600
  7.4 0.9 %copy-done.2 = bf16[544,128]{1,0:T(8,128)(2,1)S(1)} copy-done((bf16[544,128]{1,0:T(8,128)(2,1)S(1)}, bf16[544,128]{1,0:T(8,128)(2,1)}, u32[]{:S(2)}) %copy-start.2) | copy-done | bytes 139288
  8.3 2.7 %prepare.1 = (f32[64,64,128]{2,1,0:T(8,128)S(1)}, f32[64,64,128]{2,1,0:T(8,128)S(1)}, bf16[256,256]{1,0:T(8,128)(2,1)S(1)}, bf16[2,256,256]{2,1,0:T(8,128)(2,1)S(1)}, bf16[4,256,256]{2,1,0:T(8,128)(2,1)S(1)}) custom-call(s32[1,1]{1,0:T(1,128)S(6)} %copy.9.code, bf16[64,64,128]{2,1,0:T(8,128)(2,1)S(1)} %bitcast.33, bf16[544,128]{1,0:T(8,128)(2,1)S(1)} %copy-done.2), custom_call_target="tpu_custom_call" | custom-call | tf_op jit(solution)/shard_map/prepare/pallas_call | solution.py:327
  11.0 2.8 %collective-permute-done.code_before = s32[1,1]{1,0:T(1,128)} collective-permute-done((s32[1,1]{1,0:T(1,128)}, s32[1,1]{1,0:T(1,128)}, u32[]{:S(2)}, u32[]{:S(2)}) %collective-permute-start) | collective-permute-done | bytes 36 | tf_op jit(solution)/shard_map/ppermute | solution.py:266
  13.8 0.6 pick.1
  14.4 5.1 %collective-permute-start.4 = (f32[8,32,128]{2,1,0:T(8,128)S(1)}, f32[8,32,128]{2,1,0:T(8,128)S(1)}, u32[]{:S(2)}, u32[]{:S(2)}) collective-permute-start(f32[8,32,128]{2,1,0:T(8,128)S(1)} %get-tuple-element.28), channel_id=1, source_target_pairs={{0,248},{8,0},{16,8},{24,16},{32,24},{40,32},{48,40},{56,48},{64,5... | collective-permute-start | bytes 393224 | tf_op jit(solution)/shard_map/ppermute | solution.py:266
  19.6 2.0 %collective-permute-start.5 = (f32[8,32,128]{2,1,0:T(8,128)S(1)}, f32[8,32,128]{2,1,0:T(8,128)S(1)}, u32[]{:S(2)}, u32[]{:S(2)}) collective-permute-start(f32[8,32,128]{2,1,0:T(8,128)S(1)} %get-tuple-element.27.refs_0_), channel_id=1, source_target_pairs={{0,2},{1,3},{2,4},{3,5},{4,6},{5,7},{6,0},{7,1},{8,10},{9,11},{10,... | collective-permute-start | bytes 393224 | tf_op jit(solution)/shard_map/ppermute | solution.py:252
  21.6 0.5 collective-permute-done.4.refs_1_.refs_3_
  22.1 2.2 %collective-permute-start.9 = (f32[2,8,32,128]{3,2,1,0:T(8,128)S(1)}, f32[2,8,32,128]{3,2,1,0:T(8,128)S(1)}, u32[]{:S(2)}, u32[]{:S(2)}) collective-permute-start(f32[2,8,32,128]{3,2,1,0:T(8,128)S(1)} %stack.2.after), channel_id=1, source_target_pairs={{0,4},{1,5},{2,6},{3,7},{4,0},{5,1},{6,2},{7,3},{8,12},{9,13},{10,... | collective-permute-start | bytes 786440 | tf_op jit(solution)/shard_map/ppermute | solution.py:252
  24.3 1.5 %collective-permute-start.7 = (f32[8,32,128]{2,1,0:T(8,128)S(1)}, f32[8,32,128]{2,1,0:T(8,128)S(1)}, u32[]{:S(2)}, u32[]{:S(2)}) collective-permute-start(f32[8,32,128]{2,1,0:T(8,128)S(1)} %collective-permute-done.4.refs_1_.refs_3_), channel_id=1, source_target_pairs={{0,2},{1,3},{2,4},{3,5},{4,6},{5,7},{6,0},{7,1},{8,10},{9,11},{10,... | collective-permute-start | bytes 393224 | tf_op jit(solution)/shard_map/ppermute | solution.py:252
  25.8 0.5 collective-permute-start.8
  26.3 6.0 %kinetics.1 = (f32[64,64,128]{2,1,0:T(8,128)S(1)}, f32[64,64,128]{2,1,0:T(8,128)S(1)}) custom-call(f32[2,8,32,128]{3,2,1,0:T(8,128)S(1)} %stack.2.after, f32[64,64,128]{2,1,0:T(8,128)S(1)} %get-tuple-element.22.after.states, f32[64,64,128]{2,1,0:T(8,128)S(1)} %get-tuple-element.29.partly, bf16[256,256]{1,0:T(8,128)(2,1)S(1)} %get-tuple-element.30.x_ref, ...), custom_call_target="tpu_custom_call" | custom-call | flops 4000000000 | bytes 4000000 | tf_op jit(solution)/shard_map/kinetics/pallas_call | solution.py:343
  32.4 1.1 %collective-permute-done.6.refs_2_ = f32[8,32,128]{2,1,0:T(8,128)S(1)} collective-permute-done((f32[8,32,128]{2,1,0:T(8,128)S(1)}, f32[8,32,128]{2,1,0:T(8,128)S(1)}, u32[]{:S(2)}, u32[]{:S(2)}) %collective-permute-start.6) | collective-permute-done | bytes 131104 | tf_op jit(solution)/shard_map/ppermute | solution.py:252
  33.5 1.6 %collective-permute-done.8.refs_5_ = f32[8,32,128]{2,1,0:T(8,128)S(1)} collective-permute-done((f32[8,32,128]{2,1,0:T(8,128)S(1)}, f32[8,32,128]{2,1,0:T(8,128)S(1)}, u32[]{:S(2)}, u32[]{:S(2)}) %collective-permute-start.8) | collective-permute-done | bytes 131104 | tf_op jit(solution)/shard_map/ppermute | solution.py:252
  35.1 0.1 stack.3.own
  35.2 0.1 collective-permute-start.10
  35.3 2.6 %collective-permute-done.10.other = f32[8,8,32,128]{3,2,1,0:T(8,128)S(1)} collective-permute-done((f32[8,8,32,128]{3,2,1,0:T(8,128)S(1)}, f32[8,8,32,128]{3,2,1,0:T(8,128)S(1)}, u32[]{:S(2)}, u32[]{:S(2)}) %collective-permute-start.10) | collective-permute-done | bytes 1048608 | tf_op jit(solution)/shard_map/ppermute | solution.py:261
  37.9 7.0 %both_steps.1 = (f32[4,8,32,128]{3,2,1,0:T(8,128)S(1)}, f32[4,8,32,128]{3,2,1,0:T(8,128)S(1)}, f32[4,8,32,128]{3,2,1,0:T(8,128)S(1)}, f32[4,8,32,128]{3,2,1,0:T(8,128)S(1)}) custom-call(s32[1]{0:T(128)} %bitcast.band, s32[1,1]{1,0:T(1,128)S(6)} %copy.9.code, f32[64,64,128]{2,1,0:T(8,128)S(1)} %get-tuple-element.22.after.states, ...), custom_call_target="tpu_custom_call" | custom-call | tf_op jit(solution)/shard_map/both_steps/pallas_call | solution.py:347
  44.9 0.2 collective-permute-start.15
  45.1 0.4 collective-permute-start.11
  45.5 1.4 %collective-permute-done.15 = f32[4,8,32,128]{3,2,1,0:T(8,128)S(1)} collective-permute-done((f32[4,8,32,128]{3,2,1,0:T(8,128)S(1)}, f32[4,8,32,128]{3,2,1,0:T(8,128)S(1)}, u32[]{:S(2)}, u32[]{:S(2)}) %collective-permute-start.15) | collective-permute-done | bytes 524320 | tf_op jit(solution)/shard_map/ppermute | solution.py:261
  46.9 0.1 add.65
  47.0 1.4 %collective-permute-start.16 = (f32[8,32,128]{2,1,0:T(8,128)S(1)}, f32[8,32,128]{2,1,0:T(8,128)S(1)}, u32[]{:S(2)}, u32[]{:S(2)}) collective-permute-start(f32[8,32,128]{2,1,0:T(8,128)S(1)} %get-tuple-element.44), channel_id=1, source_target_pairs={{0,2},{1,3},{2,4},{3,5},{4,6},{5,7},{6,0},{7,1},{8,10},{9,11},{10,... | collective-permute-start | bytes 393224 | tf_op jit(solution)/shard_map/ppermute | solution.py:252
  48.4 0.8 collective-permute-start.17
  49.1 0.5 collective-permute-start.18
  49.6 0.1 add.59
  49.7 2.8 %collective-permute-start.12 = (f32[8,32,128]{2,1,0:T(8,128)S(1)}, f32[8,32,128]{2,1,0:T(8,128)S(1)}, u32[]{:S(2)}, u32[]{:S(2)}) collective-permute-start(f32[8,32,128]{2,1,0:T(8,128)S(1)} %get-tuple-element.41), channel_id=1, source_target_pairs={{0,2},{1,3},{2,4},{3,5},{4,6},{5,7},{6,0},{7,1},{8,10},{9,11},{10,... | collective-permute-start | bytes 393224 | tf_op jit(solution)/shard_map/ppermute | solution.py:252
  52.6 1.6 %collective-permute-start.13 = (f32[8,32,128]{2,1,0:T(8,128)S(1)}, f32[8,32,128]{2,1,0:T(8,128)S(1)}, u32[]{:S(2)}, u32[]{:S(2)}) collective-permute-start(f32[8,32,128]{2,1,0:T(8,128)S(1)} %get-tuple-element.43), channel_id=1, source_target_pairs={{0,4},{1,5},{2,6},{3,7},{4,0},{5,1},{6,2},{7,3},{8,12},{9,13},{10,... | collective-permute-start | bytes 393224 | tf_op jit(solution)/shard_map/ppermute | solution.py:252
  54.1 0.9 %collective-permute-start.14 = (f32[8,32,128]{2,1,0:T(8,128)S(1)}, f32[8,32,128]{2,1,0:T(8,128)S(1)}, u32[]{:S(2)}, u32[]{:S(2)}) collective-permute-start(f32[8,32,128]{2,1,0:T(8,128)S(1)} %get-tuple-element.42), channel_id=1, source_target_pairs={{0,6},{1,7},{2,0},{3,1},{4,2},{5,3},{6,4},{7,5},{8,14},{9,15},{10,... | collective-permute-start | bytes 393224 | tf_op jit(solution)/shard_map/ppermute | solution.py:252
  55.1 1.2 %collective-permute-done.17 = f32[8,32,128]{2,1,0:T(8,128)S(1)} collective-permute-done((f32[8,32,128]{2,1,0:T(8,128)S(1)}, f32[8,32,128]{2,1,0:T(8,128)S(1)}, u32[]{:S(2)}, u32[]{:S(2)}) %collective-permute-start.17) | collective-permute-done | bytes 131104 | tf_op jit(solution)/shard_map/ppermute | solution.py:252
  56.3 3.6 %collective-permute-done.18 = f32[8,32,128]{2,1,0:T(8,128)S(1)} collective-permute-done((f32[8,32,128]{2,1,0:T(8,128)S(1)}, f32[8,32,128]{2,1,0:T(8,128)S(1)}, u32[]{:S(2)}, u32[]{:S(2)}) %collective-permute-start.18) | collective-permute-done | bytes 131104 | tf_op jit(solution)/shard_map/ppermute | solution.py:252
  59.9 0.1 collective-permute-start.19
  60.6 1.3 %collective-permute-done.13 = f32[8,32,128]{2,1,0:T(8,128)S(1)} collective-permute-done((f32[8,32,128]{2,1,0:T(8,128)S(1)}, f32[8,32,128]{2,1,0:T(8,128)S(1)}, u32[]{:S(2)}, u32[]{:S(2)}) %collective-permute-start.13) | collective-permute-done | bytes 131104 | tf_op jit(solution)/shard_map/ppermute | solution.py:252
  61.9 1.7 %collective-permute-done.14 = f32[8,32,128]{2,1,0:T(8,128)S(1)} collective-permute-done((f32[8,32,128]{2,1,0:T(8,128)S(1)}, f32[8,32,128]{2,1,0:T(8,128)S(1)}, u32[]{:S(2)}, u32[]{:S(2)}) %collective-permute-start.14) | collective-permute-done | bytes 131104 | tf_op jit(solution)/shard_map/ppermute | solution.py:252
  63.6 4.7 %collective-permute-done.19 = f32[8,32,128]{2,1,0:T(8,128)S(1)} collective-permute-done((f32[8,32,128]{2,1,0:T(8,128)S(1)}, f32[8,32,128]{2,1,0:T(8,128)S(1)}, u32[]{:S(2)}, u32[]{:S(2)}) %collective-permute-start.19) | collective-permute-done | bytes 131104 | tf_op jit(solution)/shard_map/ppermute | solution.py:266
  68.3 0.1 select_add_fusion.1
  68.3 0.1 collective-permute-start.20
  68.4 1.3 %collective-permute-start.21 = (f32[8,32,128]{2,1,0:T(8,128)S(1)}, f32[8,32,128]{2,1,0:T(8,128)S(1)}, u32[]{:S(2)}, u32[]{:S(2)}) collective-permute-start(f32[8,32,128]{2,1,0:T(8,128)S(1)} %get-tuple-element.47), channel_id=1, source_target_pairs={{0,4},{1,5},{2,6},{3,7},{4,0},{5,1},{6,2},{7,3},{8,12},{9,13},{10,... | collective-permute-start | bytes 393224 | tf_op jit(solution)/shard_map/ppermute | solution.py:252
  69.8 1.3 %collective-permute-start.22 = (f32[8,32,128]{2,1,0:T(8,128)S(1)}, f32[8,32,128]{2,1,0:T(8,128)S(1)}, u32[]{:S(2)}, u32[]{:S(2)}) collective-permute-start(f32[8,32,128]{2,1,0:T(8,128)S(1)} %get-tuple-element.39), channel_id=1, source_target_pairs={{0,6},{1,7},{2,0},{3,1},{4,2},{5,3},{6,4},{7,5},{8,14},{9,15},{10,... | collective-permute-start | bytes 393224 | tf_op jit(solution)/shard_map/ppermute | solution.py:252
  71.1 2.3 %collective-permute-done.20.refs_1_ = f32[8,32,128]{2,1,0:T(8,128)S(1)} collective-permute-done((f32[8,32,128]{2,1,0:T(8,128)S(1)}, f32[8,32,128]{2,1,0:T(8,128)S(1)}, u32[]{:S(2)}, u32[]{:S(2)}) %collective-permute-start.20) | collective-permute-done | bytes 131104 | tf_op jit(solution)/shard_map/ppermute | solution.py:252
  73.4 2.1 %collective-permute-done.21.refs_2_ = f32[8,32,128]{2,1,0:T(8,128)S(1)} collective-permute-done((f32[8,32,128]{2,1,0:T(8,128)S(1)}, f32[8,32,128]{2,1,0:T(8,128)S(1)}, u32[]{:S(2)}, u32[]{:S(2)}) %collective-permute-start.21) | collective-permute-done | bytes 131104 | tf_op jit(solution)/shard_map/ppermute | solution.py:252
  75.5 1.3 %collective-permute-done.22.refs_3_ = f32[8,32,128]{2,1,0:T(8,128)S(1)} collective-permute-done((f32[8,32,128]{2,1,0:T(8,128)S(1)}, f32[8,32,128]{2,1,0:T(8,128)S(1)}, u32[]{:S(2)}, u32[]{:S(2)}) %collective-permute-start.22) | collective-permute-done | bytes 131104 | tf_op jit(solution)/shard_map/ppermute | solution.py:252
  76.8 0.8 %settle.1 = f32[32,32,128]{2,1,0:T(8,128)} custom-call(s32[1]{0:T(128)} %bitcast.band, f32[8,32,128]{2,1,0:T(8,128)S(1)} %get-tuple-element.49.refs_0_, f32[8,32,128]{2,1,0:T(8,128)S(1)} %collective-permute-done.20.refs_1_, f32[8,32,128]{2,1,0:T(8,128)S(1)} %collective-permute-done.21.refs_2_, f32[8,32,128]{2,1,0:T(8,128)S(1)} %collective-permute-done.22.refs_3_), custom_call_target="tpu_custom_call" | custom-call | tf_op jit(solution)/shard_map/settle/pallas_call | solution.py:364
  (19 shorter events, 0.2 us)
Async XLA Ops:
  0.0 1.0 %copy-start.1 = (f32[32,32,128]{2,1,0:T(8,128)S(1)}, f32[32,32,128]{2,1,0:T(8,128)}, u32[]{:S(2)}) copy-start(f32[32,32,128]{2,1,0:T(8,128)} %potential.1) | copy-start | bytes 1572868
  1.1 12.7 %collective-permute-start.1 = (f32[8,32,128]{2,1,0:T(8,128)S(1)}, f32[8,32,128]{2,1,0:T(8,128)S(1)}, u32[]{:S(2)}, u32[]{:S(2)}) collective-permute-start(f32[8,32,128]{2,1,0:T(8,128)S(1)} %get-tuple-element.24), channel_id=1, source_target_pairs={{0,2},{1,3},{2,4},{3,5},{4,6},{5,7},{6,0},{7,1},{8,10},{9,11},{10,... | collective-permute-start | bytes 393224 | tf_op jit(solution)/shard_map/ppermute | solution.py:252
  3.1 10.7 %collective-permute-start.2 = (f32[8,32,128]{2,1,0:T(8,128)S(1)}, f32[8,32,128]{2,1,0:T(8,128)S(1)}, u32[]{:S(2)}, u32[]{:S(2)}) collective-permute-start(f32[8,32,128]{2,1,0:T(8,128)S(1)} %get-tuple-element.25), channel_id=1, source_target_pairs={{0,4},{1,5},{2,6},{3,7},{4,0},{5,1},{6,2},{7,3},{8,12},{9,13},{10,... | collective-permute-start | bytes 393224 | tf_op jit(solution)/shard_map/ppermute | solution.py:252
  4.0 9.8 %collective-permute-start.3 = (f32[8,32,128]{2,1,0:T(8,128)S(1)}, f32[8,32,128]{2,1,0:T(8,128)S(1)}, u32[]{:S(2)}, u32[]{:S(2)}) collective-permute-start(f32[8,32,128]{2,1,0:T(8,128)S(1)} %get-tuple-element.26), channel_id=1, source_target_pairs={{0,6},{1,7},{2,0},{3,1},{4,2},{5,3},{6,4},{7,5},{8,14},{9,15},{10,... | collective-permute-start | bytes 393224 | tf_op jit(solution)/shard_map/ppermute | solution.py:252
  4.1 9.7 %collective-permute-start = (s32[1,1]{1,0:T(1,128)}, s32[1,1]{1,0:T(1,128)}, u32[]{:S(2)}, u32[]{:S(2)}) collective-permute-start(s32[1,1]{1,0:T(1,128)} %param.10), channel_id=1, source_target_pairs={{0,8},{8,16},{16,24},{24,32},{32,40},{40,48},{48,56},{56,64},{64,7... | collective-permute-start | bytes 20 | tf_op jit(solution)/shard_map/ppermute | solution.py:266
  6.2 1.2 %copy-start = (bf16[1,1,64,64,128]{4,3,2,1,0:T(8,128)(2,1)S(1)}, bf16[1,1,64,64,128]{4,3,2,1,0:T(8,128)(2,1)}, u32[]{:S(2)}) copy-start(bf16[1,1,64,64,128]{4,3,2,1,0:T(8,128)(2,1)} %param.8) | copy-start | bytes 3145732
  7.4 0.9 %copy-start.2 = (bf16[544,128]{1,0:T(8,128)(2,1)S(1)}, bf16[544,128]{1,0:T(8,128)(2,1)}, u32[]{:S(2)}) copy-start(bf16[544,128]{1,0:T(8,128)(2,1)} %constant.59.consts) | copy-start | bytes 417796
  14.4 7.7 %collective-permute-start.4 = (f32[8,32,128]{2,1,0:T(8,128)S(1)}, f32[8,32,128]{2,1,0:T(8,128)S(1)}, u32[]{:S(2)}, u32[]{:S(2)}) collective-permute-start(f32[8,32,128]{2,1,0:T(8,128)S(1)} %get-tuple-element.28), channel_id=1, source_target_pairs={{0,248},{8,0},{16,8},{24,16},{32,24},{40,32},{48,40},{56,48},{64,5... | collective-permute-start | bytes 393224 | tf_op jit(solution)/shard_map/ppermute | solution.py:266
  19.6 12.8 %collective-permute-start.5 = (f32[8,32,128]{2,1,0:T(8,128)S(1)}, f32[8,32,128]{2,1,0:T(8,128)S(1)}, u32[]{:S(2)}, u32[]{:S(2)}) collective-permute-start(f32[8,32,128]{2,1,0:T(8,128)S(1)} %get-tuple-element.27.refs_0_), channel_id=1, source_target_pairs={{0,2},{1,3},{2,4},{3,5},{4,6},{5,7},{6,0},{7,1},{8,10},{9,11},{10,... | collective-permute-start | bytes 393224 | tf_op jit(solution)/shard_map/ppermute | solution.py:252
  21.6 11.9 %collective-permute-start.6 = (f32[8,32,128]{2,1,0:T(8,128)S(1)}, f32[8,32,128]{2,1,0:T(8,128)S(1)}, u32[]{:S(2)}, u32[]{:S(2)}) collective-permute-start(f32[8,32,128]{2,1,0:T(8,128)S(1)} %get-tuple-element.27.refs_0_), channel_id=1, source_target_pairs={{0,6},{1,7},{2,0},{3,1},{4,2},{5,3},{6,4},{7,5},{8,14},{9,15},{10,... | collective-permute-start | bytes 393224 | tf_op jit(solution)/shard_map/ppermute | solution.py:252
  22.1 13.0 %collective-permute-start.9 = (f32[2,8,32,128]{3,2,1,0:T(8,128)S(1)}, f32[2,8,32,128]{3,2,1,0:T(8,128)S(1)}, u32[]{:S(2)}, u32[]{:S(2)}) collective-permute-start(f32[2,8,32,128]{3,2,1,0:T(8,128)S(1)} %stack.2.after), channel_id=1, source_target_pairs={{0,4},{1,5},{2,6},{3,7},{4,0},{5,1},{6,2},{7,3},{8,12},{9,13},{10,... | collective-permute-start | bytes 786440 | tf_op jit(solution)/shard_map/ppermute | solution.py:252
  24.3 9.2 %collective-permute-start.7 = (f32[8,32,128]{2,1,0:T(8,128)S(1)}, f32[8,32,128]{2,1,0:T(8,128)S(1)}, u32[]{:S(2)}, u32[]{:S(2)}) collective-permute-start(f32[8,32,128]{2,1,0:T(8,128)S(1)} %collective-permute-done.4.refs_1_.refs_3_), channel_id=1, source_target_pairs={{0,2},{1,3},{2,4},{3,5},{4,6},{5,7},{6,0},{7,1},{8,10},{9,11},{10,... | collective-permute-start | bytes 393224 | tf_op jit(solution)/shard_map/ppermute | solution.py:252
  25.8 9.2 %collective-permute-start.8 = (f32[8,32,128]{2,1,0:T(8,128)S(1)}, f32[8,32,128]{2,1,0:T(8,128)S(1)}, u32[]{:S(2)}, u32[]{:S(2)}) collective-permute-start(f32[8,32,128]{2,1,0:T(8,128)S(1)} %collective-permute-done.4.refs_1_.refs_3_), channel_id=1, source_target_pairs={{0,6},{1,7},{2,0},{3,1},{4,2},{5,3},{6,4},{7,5},{8,14},{9,15},{10,... | collective-permute-start | bytes 393224 | tf_op jit(solution)/shard_map/ppermute | solution.py:252
  35.2 2.7 %collective-permute-start.10 = (f32[8,8,32,128]{3,2,1,0:T(8,128)S(1)}, f32[8,8,32,128]{3,2,1,0:T(8,128)S(1)}, u32[]{:S(2)}, u32[]{:S(2)}) collective-permute-start(f32[8,8,32,128]{3,2,1,0:T(8,128)S(1)} %stack.3.own), channel_id=1, source_target_pairs={{0,1},{1,0},{2,3},{3,2},{4,5},{5,4},{6,7},{7,6},{8,9},{9,8},{10,11... | collective-permute-start | bytes 3145736 | tf_op jit(solution)/shard_map/ppermute | solution.py:261
  44.9 2.0 %collective-permute-start.15 = (f32[4,8,32,128]{3,2,1,0:T(8,128)S(1)}, f32[4,8,32,128]{3,2,1,0:T(8,128)S(1)}, u32[]{:S(2)}, u32[]{:S(2)}) collective-permute-start(f32[4,8,32,128]{3,2,1,0:T(8,128)S(1)} %get-tuple-element.38), channel_id=1, source_target_pairs={{0,1},{1,0},{2,3},{3,2},{4,5},{5,4},{6,7},{7,6},{8,9},{9,8},{10,11... | collective-permute-start | bytes 1572872 | tf_op jit(solution)/shard_map/ppermute | solution.py:261
  45.1 4.5 %collective-permute-start.11 = (f32[4,8,32,128]{3,2,1,0:T(8,128)S(1)}, f32[4,8,32,128]{3,2,1,0:T(8,128)S(1)}, u32[]{:S(2)}, u32[]{:S(2)}) collective-permute-start(f32[4,8,32,128]{3,2,1,0:T(8,128)S(1)} %get-tuple-element.36), channel_id=1, source_target_pairs={{0,1},{1,0},{2,3},{3,2},{4,5},{5,4},{6,7},{7,6},{8,9},{9,8},{10,11... | collective-permute-start | bytes 1572872 | tf_op jit(solution)/shard_map/ppermute | solution.py:261
  47.0 7.1 %collective-permute-start.16 = (f32[8,32,128]{2,1,0:T(8,128)S(1)}, f32[8,32,128]{2,1,0:T(8,128)S(1)}, u32[]{:S(2)}, u32[]{:S(2)}) collective-permute-start(f32[8,32,128]{2,1,0:T(8,128)S(1)} %get-tuple-element.44), channel_id=1, source_target_pairs={{0,2},{1,3},{2,4},{3,5},{4,6},{5,7},{6,0},{7,1},{8,10},{9,11},{10,... | collective-permute-start | bytes 393224 | tf_op jit(solution)/shard_map/ppermute | solution.py:252
  48.4 7.9 %collective-permute-start.17 = (f32[8,32,128]{2,1,0:T(8,128)S(1)}, f32[8,32,128]{2,1,0:T(8,128)S(1)}, u32[]{:S(2)}, u32[]{:S(2)}) collective-permute-start(f32[8,32,128]{2,1,0:T(8,128)S(1)} %get-tuple-element.46), channel_id=1, source_target_pairs={{0,4},{1,5},{2,6},{3,7},{4,0},{5,1},{6,2},{7,3},{8,12},{9,13},{10,... | collective-permute-start | bytes 393224 | tf_op jit(solution)/shard_map/ppermute | solution.py:252
  49.1 10.7 %collective-permute-start.18 = (f32[8,32,128]{2,1,0:T(8,128)S(1)}, f32[8,32,128]{2,1,0:T(8,128)S(1)}, u32[]{:S(2)}, u32[]{:S(2)}) collective-permute-start(f32[8,32,128]{2,1,0:T(8,128)S(1)} %get-tuple-element.45), channel_id=1, source_target_pairs={{0,6},{1,7},{2,0},{3,1},{4,2},{5,3},{6,4},{7,5},{8,14},{9,15},{10,... | collective-permute-start | bytes 393224 | tf_op jit(solution)/shard_map/ppermute | solution.py:252
  49.7 10.8 %collective-permute-start.12 = (f32[8,32,128]{2,1,0:T(8,128)S(1)}, f32[8,32,128]{2,1,0:T(8,128)S(1)}, u32[]{:S(2)}, u32[]{:S(2)}) collective-permute-start(f32[8,32,128]{2,1,0:T(8,128)S(1)} %get-tuple-element.41), channel_id=1, source_target_pairs={{0,2},{1,3},{2,4},{3,5},{4,6},{5,7},{6,0},{7,1},{8,10},{9,11},{10,... | collective-permute-start | bytes 393224 | tf_op jit(solution)/shard_map/ppermute | solution.py:252
  52.6 9.3 %collective-permute-start.13 = (f32[8,32,128]{2,1,0:T(8,128)S(1)}, f32[8,32,128]{2,1,0:T(8,128)S(1)}, u32[]{:S(2)}, u32[]{:S(2)}) collective-permute-start(f32[8,32,128]{2,1,0:T(8,128)S(1)} %get-tuple-element.43), channel_id=1, source_target_pairs={{0,4},{1,5},{2,6},{3,7},{4,0},{5,1},{6,2},{7,3},{8,12},{9,13},{10,... | collective-permute-start | bytes 393224 | tf_op jit(solution)/shard_map/ppermute | solution.py:252
  54.1 9.4 %collective-permute-start.14 = (f32[8,32,128]{2,1,0:T(8,128)S(1)}, f32[8,32,128]{2,1,0:T(8,128)S(1)}, u32[]{:S(2)}, u32[]{:S(2)}) collective-permute-start(f32[8,32,128]{2,1,0:T(8,128)S(1)} %get-tuple-element.42), channel_id=1, source_target_pairs={{0,6},{1,7},{2,0},{3,1},{4,2},{5,3},{6,4},{7,5},{8,14},{9,15},{10,... | collective-permute-start | bytes 393224 | tf_op jit(solution)/shard_map/ppermute | solution.py:252
  59.9 8.4 %collective-permute-start.19 = (f32[8,32,128]{2,1,0:T(8,128)S(1)}, f32[8,32,128]{2,1,0:T(8,128)S(1)}, u32[]{:S(2)}, u32[]{:S(2)}) collective-permute-start(f32[8,32,128]{2,1,0:T(8,128)S(1)} %fusion.2), channel_id=1, source_target_pairs={{0,8},{8,16},{16,24},{24,32},{32,40},{40,48},{48,56},{56,64},{64,7... | collective-permute-start | bytes 393224 | tf_op jit(solution)/shard_map/ppermute | solution.py:266
  68.3 5.0 %collective-permute-start.20 = (f32[8,32,128]{2,1,0:T(8,128)S(1)}, f32[8,32,128]{2,1,0:T(8,128)S(1)}, u32[]{:S(2)}, u32[]{:S(2)}) collective-permute-start(f32[8,32,128]{2,1,0:T(8,128)S(1)} %get-tuple-element.48), channel_id=1, source_target_pairs={{0,2},{1,3},{2,4},{3,5},{4,6},{5,7},{6,0},{7,1},{8,10},{9,11},{10,... | collective-permute-start | bytes 393224 | tf_op jit(solution)/shard_map/ppermute | solution.py:252
  68.4 7.1 %collective-permute-start.21 = (f32[8,32,128]{2,1,0:T(8,128)S(1)}, f32[8,32,128]{2,1,0:T(8,128)S(1)}, u32[]{:S(2)}, u32[]{:S(2)}) collective-permute-start(f32[8,32,128]{2,1,0:T(8,128)S(1)} %get-tuple-element.47), channel_id=1, source_target_pairs={{0,4},{1,5},{2,6},{3,7},{4,0},{5,1},{6,2},{7,3},{8,12},{9,13},{10,... | collective-permute-start | bytes 393224 | tf_op jit(solution)/shard_map/ppermute | solution.py:252
  69.8 7.0 %collective-permute-start.22 = (f32[8,32,128]{2,1,0:T(8,128)S(1)}, f32[8,32,128]{2,1,0:T(8,128)S(1)}, u32[]{:S(2)}, u32[]{:S(2)}) collective-permute-start(f32[8,32,128]{2,1,0:T(8,128)S(1)} %get-tuple-element.39), channel_id=1, source_target_pairs={{0,6},{1,7},{2,0},{3,1},{4,2},{5,3},{6,4},{7,5},{8,14},{9,15},{10,... | collective-permute-start | bytes 393224 | tf_op jit(solution)/shard_map/ppermute | solution.py:252

commit v5 on v4

--- a/solution.py
+++ b/solution.py
@@ -170,18 +170,12 @@
 CHUNKS = ((0, 0), (0, 1), (0, 3), (1, 0), (1, 1), (1, 3), (0, 2), (1, 2))
 
 
-def line_loop(band, code, columns, half, use):
+def chunk_loop(band, code, columns, half, use):
     chip = band[0] >> 1
     for ref, rows in zip(columns, box_rows(band, code, columns[0].shape[2])):
         chunk = ref.shape[1]
         for m, (slab, back) in enumerate(CHUNKS):
-            start = slab * half + ((chip - back) & (CHIPS - 1)) * chunk
-
-            def line(i, carry, ref=ref, rows=rows, m=m, start=start):
-                use(rows, start + i, ref[m, i])
-                return carry
-
-            lax.fori_loop(0, chunk, line, 0, unroll=2)
+            use(pl.ds(slab * half + ((chip - back) & (CHIPS - 1)) * chunk, chunk), rows, ref[m])
 
 
 def both_steps(band, code, states, kinetic, again, x_ref, y_ref, z_ref, own, other, *refs):
@@ -190,11 +184,11 @@
     half, column, double = depth // 2, width // 2, code[0, 0] & 1
     chunk = half // CHIPS
 
-    def use(rows, z, v):
-        pot[z, rows] = v
-        forced[z, rows] = v * states[z, rows]
-
-    line_loop(band, code, (own, other), half, use)
+    def use(lines, rows, v):
+        pot[lines, rows] = v
+        forced[lines, rows] = v * states[lines, rows]
+
+    chunk_loop(band, code, (own, other), half, use)
     xy_pass(lambda z: forced[pl.ds(z, 8)], extra, 0, depth, x_ref, y_ref, False)
 
     def zz(i, sums):
@@ -223,19 +217,15 @@
     weight = second * second * tt - 2.0 * STEP_LENGTH * second * th + STEP_LENGTH * STEP_LENGTH * hh
     sign = (2 * double - 1).astype(jnp.float32)
     factor = sign / 8.0 * square * cells / (square * weight + EPSILON)
-    by_s, by_h, by_w = second * first, -STEP_LENGTH * (first + second), STEP_LENGTH * STEP_LENGTH
+    factor = factor.reshape(1, 1, 1)
+    by_s, by_h = ((second * first).reshape(1, 1, 1), (-STEP_LENGTH * (first + second)).reshape(1, 1, 1))
+    by_w = STEP_LENGTH * STEP_LENGTH
     for slab, outs in ((1, (keep1, give1)), (0, (keep0, give0))):
         for out, rows in zip(outs, box_rows(band, code, column)):
             for k in range(CHIPS):
-                start = (((band[0] >> 1) + k) & (CHIPS - 1)) * chunk
-
-                def line(i, carry, out=out, rows=rows, start=start, k=k, slab=slab):
-                    at = slab * half + start + i
-                    u = by_s * states[at, rows] + by_h * total_h[at, rows] + by_w * twice[at, rows]
-                    out[k, i] = factor * (u * u)
-                    return carry
-
-                lax.fori_loop(0, chunk, line, 0, unroll=2)
+                at = pl.ds(slab * half + (((band[0] >> 1) + k) & (CHIPS - 1)) * chunk, chunk)
+                u = by_s * states[at, rows] + by_h * total_h[at, rows] + by_w * twice[at, rows]
+                out[k] = factor * (u * u)
 
 
 def stack(after, *refs):

time: 77.9 us -> 77.1 us (0.990)
  no operation moved by 1% of the time
where the time goes in v5:
time: 77.1 us; the launch traced here: 76.9 us
  waiting for transfers between devices  28.2 us (37%)
  starting transfers between devices  27.1 us (35%)
  Pallas kernels  16.8 us (22%)
  local copies, waits for them, and re-layouts  3.22 us (4%)
  between operations  1.43 us (2%)
    ppermute x17, starting transfers between devices, to_next_chip(): return lax.ppermute(block, 'band', [(b, (b + 2 * k) % m) for b in range(m)])  19.7 us
    ppermute x17, waiting for transfers between devices, to_next_chip(): return lax.ppermute(block, 'band', [(b, (b + 2 * k) % m) for b in range(m)])  16.2 us
    ppermute x3, waiting for transfers between devices, to_group(): lax.ppermute(block, 'frag', [(i, (i + distance) % n) for i in range(n)])  7.9 us
    ppermute x3, starting transfers between devices, to_group(): lax.ppermute(block, 'frag', [(i, (i + distance) % n) for i in range(n)])  6.61 us
    pallas_call x1, Pallas kernels, body(): kernel(both_steps, [quarter] * 4, [SMEM] * 2 + [VMEM] * 8, BIG, scratch=[...  6.46 us
    pallas_call x1, Pallas kernels, body(): kernel(kinetics, [box] * 2, [ANY] + [VMEM] * 5, MIDDLE, flops=4000000000)  6 us
    ppermute x3, waiting for transfers between devices, to_other_core(): return lax.ppermute(block, 'band', [(b, b ^ 1) for b in range(2 * CHIPS)])  4.05 us
    unnamed x6, local copies, waits for them, and re-layouts  3.17 us
  transfers between devices with their start and end apart: 23, of which 14 were waited for; matrix products, arithmetic and copies ran while one was open for 0% of the time, Pallas kernels for 11%

profile of v5, /device:TPU:24, one launch (start us, length us, event | category | flops | bytes accessed | tf_op | source)
XLA Modules:
  0.0 76.9 jit_solution(13314798172765030465)
XLA Ops:
  0.0 1.0 %copy-done.1 = f32[32,32,128]{2,1,0:T(8,128)S(1)} copy-done((f32[32,32,128]{2,1,0:T(8,128)S(1)}, f32[32,32,128]{2,1,0:T(8,128)}, u32[]{:S(2)}) %copy-start.1) | copy-done | bytes 524312
  1.1 2.0 %collective-permute-start.1 = (f32[8,32,128]{2,1,0:T(8,128)S(1)}, f32[8,32,128]{2,1,0:T(8,128)S(1)}, u32[]{:S(2)}, u32[]{:S(2)}) collective-permute-start(f32[8,32,128]{2,1,0:T(8,128)S(1)} %get-tuple-element.24), channel_id=1, source_target_pairs={{0,2},{1,3},{2,4},{3,5},{4,6},{5,7},{6,0},{7,1},{8,10},{9,11},{10,... | collective-permute-start | bytes 393224 | tf_op jit(solution)/shard_map/ppermute | solution.py:242
  3.1 0.9 %collective-permute-start.2 = (f32[8,32,128]{2,1,0:T(8,128)S(1)}, f32[8,32,128]{2,1,0:T(8,128)S(1)}, u32[]{:S(2)}, u32[]{:S(2)}) collective-permute-start(f32[8,32,128]{2,1,0:T(8,128)S(1)} %get-tuple-element.25), channel_id=1, source_target_pairs={{0,4},{1,5},{2,6},{3,7},{4,0},{5,1},{6,2},{7,3},{8,12},{9,13},{10,... | collective-permute-start | bytes 393224 | tf_op jit(solution)/shard_map/ppermute | solution.py:242
  4.0 0.1 collective-permute-start.3
  4.1 1.4 %collective-permute-start = (s32[1,1]{1,0:T(1,128)}, s32[1,1]{1,0:T(1,128)}, u32[]{:S(2)}, u32[]{:S(2)}) collective-permute-start(s32[1,1]{1,0:T(1,128)} %param.10), channel_id=1, source_target_pairs={{0,8},{8,16},{16,24},{24,32},{32,40},{40,48},{48,56},{56,64},{64,7... | collective-permute-start | bytes 20 | tf_op jit(solution)/shard_map/ppermute | solution.py:256
  6.2 1.2 %copy-done = bf16[1,1,64,64,128]{4,3,2,1,0:T(8,128)(2,1)S(1)} copy-done((bf16[1,1,64,64,128]{4,3,2,1,0:T(8,128)(2,1)S(1)}, bf16[1,1,64,64,128]{4,3,2,1,0:T(8,128)(2,1)}, u32[]{:S(2)}) %copy-start) | copy-done | bytes 1048600
  7.4 0.9 %copy-done.2 = bf16[544,128]{1,0:T(8,128)(2,1)S(1)} copy-done((bf16[544,128]{1,0:T(8,128)(2,1)S(1)}, bf16[544,128]{1,0:T(8,128)(2,1)}, u32[]{:S(2)}) %copy-start.2) | copy-done | bytes 139288
  8.3 2.7 %prepare.1 = (f32[64,64,128]{2,1,0:T(8,128)S(1)}, f32[64,64,128]{2,1,0:T(8,128)S(1)}, bf16[256,256]{1,0:T(8,128)(2,1)S(1)}, bf16[2,256,256]{2,1,0:T(8,128)(2,1)S(1)}, bf16[4,256,256]{2,1,0:T(8,128)(2,1)S(1)}) custom-call(s32[1,1]{1,0:T(1,128)S(6)} %copy.9.code, bf16[64,64,128]{2,1,0:T(8,128)(2,1)S(1)} %bitcast.33, bf16[544,128]{1,0:T(8,128)(2,1)S(1)} %copy-done.2), custom_call_target="tpu_custom_call" | custom-call | tf_op jit(solution)/shard_map/prepare/pallas_call | solution.py:317
  11.0 2.8 %collective-permute-done.code_before = s32[1,1]{1,0:T(1,128)} collective-permute-done((s32[1,1]{1,0:T(1,128)}, s32[1,1]{1,0:T(1,128)}, u32[]{:S(2)}, u32[]{:S(2)}) %collective-permute-start) | collective-permute-done | bytes 36 | tf_op jit(solution)/shard_map/ppermute | solution.py:256
  13.8 0.6 pick.1
  14.4 5.1 %collective-permute-start.4 = (f32[8,32,128]{2,1,0:T(8,128)S(1)}, f32[8,32,128]{2,1,0:T(8,128)S(1)}, u32[]{:S(2)}, u32[]{:S(2)}) collective-permute-start(f32[8,32,128]{2,1,0:T(8,128)S(1)} %get-tuple-element.28), channel_id=1, source_target_pairs={{0,248},{8,0},{16,8},{24,16},{32,24},{40,32},{48,40},{56,48},{64,5... | collective-permute-start | bytes 393224 | tf_op jit(solution)/shard_map/ppermute | solution.py:256
  19.6 2.0 %collective-permute-start.5 = (f32[8,32,128]{2,1,0:T(8,128)S(1)}, f32[8,32,128]{2,1,0:T(8,128)S(1)}, u32[]{:S(2)}, u32[]{:S(2)}) collective-permute-start(f32[8,32,128]{2,1,0:T(8,128)S(1)} %get-tuple-element.27.refs_0_), channel_id=1, source_target_pairs={{0,2},{1,3},{2,4},{3,5},{4,6},{5,7},{6,0},{7,1},{8,10},{9,11},{10,... | collective-permute-start | bytes 393224 | tf_op jit(solution)/shard_map/ppermute | solution.py:242
  21.6 0.5 collective-permute-done.4.refs_1_.refs_3_
  22.1 2.2 %collective-permute-start.9 = (f32[2,8,32,128]{3,2,1,0:T(8,128)S(1)}, f32[2,8,32,128]{3,2,1,0:T(8,128)S(1)}, u32[]{:S(2)}, u32[]{:S(2)}) collective-permute-start(f32[2,8,32,128]{3,2,1,0:T(8,128)S(1)} %stack.2.after), channel_id=1, source_target_pairs={{0,4},{1,5},{2,6},{3,7},{4,0},{5,1},{6,2},{7,3},{8,12},{9,13},{10,... | collective-permute-start | bytes 786440 | tf_op jit(solution)/shard_map/ppermute | solution.py:242
  24.3 1.5 %collective-permute-start.7 = (f32[8,32,128]{2,1,0:T(8,128)S(1)}, f32[8,32,128]{2,1,0:T(8,128)S(1)}, u32[]{:S(2)}, u32[]{:S(2)}) collective-permute-start(f32[8,32,128]{2,1,0:T(8,128)S(1)} %collective-permute-done.4.refs_1_.refs_3_), channel_id=1, source_target_pairs={{0,2},{1,3},{2,4},{3,5},{4,6},{5,7},{6,0},{7,1},{8,10},{9,11},{10,... | collective-permute-start | bytes 393224 | tf_op jit(solution)/shard_map/ppermute | solution.py:242
  25.8 0.5 collective-permute-start.8
  26.3 6.0 %kinetics.1 = (f32[64,64,128]{2,1,0:T(8,128)S(1)}, f32[64,64,128]{2,1,0:T(8,128)S(1)}) custom-call(f32[2,8,32,128]{3,2,1,0:T(8,128)S(1)} %stack.2.after, f32[64,64,128]{2,1,0:T(8,128)S(1)} %get-tuple-element.22.after.states, f32[64,64,128]{2,1,0:T(8,128)S(1)} %get-tuple-element.29.partly, bf16[256,256]{1,0:T(8,128)(2,1)S(1)} %get-tuple-element.30.x_ref, ...), custom_call_target="tpu_custom_call" | custom-call | flops 4000000000 | bytes 4000000 | tf_op jit(solution)/shard_map/kinetics/pallas_call | solution.py:333
  32.4 1.1 %collective-permute-done.6.refs_2_ = f32[8,32,128]{2,1,0:T(8,128)S(1)} collective-permute-done((f32[8,32,128]{2,1,0:T(8,128)S(1)}, f32[8,32,128]{2,1,0:T(8,128)S(1)}, u32[]{:S(2)}, u32[]{:S(2)}) %collective-permute-start.6) | collective-permute-done | bytes 131104 | tf_op jit(solution)/shard_map/ppermute | solution.py:242
  33.5 1.6 %collective-permute-done.8.refs_5_ = f32[8,32,128]{2,1,0:T(8,128)S(1)} collective-permute-done((f32[8,32,128]{2,1,0:T(8,128)S(1)}, f32[8,32,128]{2,1,0:T(8,128)S(1)}, u32[]{:S(2)}, u32[]{:S(2)}) %collective-permute-start.8) | collective-permute-done | bytes 131104 | tf_op jit(solution)/shard_map/ppermute | solution.py:242
  35.1 0.1 stack.3.own
  35.2 0.1 collective-permute-start.10
  35.3 2.6 %collective-permute-done.10.other = f32[8,8,32,128]{3,2,1,0:T(8,128)S(1)} collective-permute-done((f32[8,8,32,128]{3,2,1,0:T(8,128)S(1)}, f32[8,8,32,128]{3,2,1,0:T(8,128)S(1)}, u32[]{:S(2)}, u32[]{:S(2)}) %collective-permute-start.10) | collective-permute-done | bytes 1048608 | tf_op jit(solution)/shard_map/ppermute | solution.py:251
  37.9 6.5 %both_steps.1 = (f32[4,8,32,128]{3,2,1,0:T(8,128)S(1)}, f32[4,8,32,128]{3,2,1,0:T(8,128)S(1)}, f32[4,8,32,128]{3,2,1,0:T(8,128)S(1)}, f32[4,8,32,128]{3,2,1,0:T(8,128)S(1)}) custom-call(s32[1]{0:T(128)} %bitcast.band, s32[1,1]{1,0:T(1,128)S(6)} %copy.9.code, f32[64,64,128]{2,1,0:T(8,128)S(1)} %get-tuple-element.22.after.states, ...), custom_call_target="tpu_custom_call" | custom-call | tf_op jit(solution)/shard_map/both_steps/pallas_call | solution.py:337
  44.4 0.2 collective-permute-start.15
  44.6 0.4 collective-permute-start.11
  45.0 1.4 %collective-permute-done.15 = f32[4,8,32,128]{3,2,1,0:T(8,128)S(1)} collective-permute-done((f32[4,8,32,128]{3,2,1,0:T(8,128)S(1)}, f32[4,8,32,128]{3,2,1,0:T(8,128)S(1)}, u32[]{:S(2)}, u32[]{:S(2)}) %collective-permute-start.15) | collective-permute-done | bytes 524320 | tf_op jit(solution)/shard_map/ppermute | solution.py:251
  46.4 0.1 add.65
  46.5 1.2 %collective-permute-start.16 = (f32[8,32,128]{2,1,0:T(8,128)S(1)}, f32[8,32,128]{2,1,0:T(8,128)S(1)}, u32[]{:S(2)}, u32[]{:S(2)}) collective-permute-start(f32[8,32,128]{2,1,0:T(8,128)S(1)} %get-tuple-element.44), channel_id=1, source_target_pairs={{0,2},{1,3},{2,4},{3,5},{4,6},{5,7},{6,0},{7,1},{8,10},{9,11},{10,... | collective-permute-start | bytes 393224 | tf_op jit(solution)/shard_map/ppermute | solution.py:242
  47.7 0.8 %collective-permute-start.17 = (f32[8,32,128]{2,1,0:T(8,128)S(1)}, f32[8,32,128]{2,1,0:T(8,128)S(1)}, u32[]{:S(2)}, u32[]{:S(2)}) collective-permute-start(f32[8,32,128]{2,1,0:T(8,128)S(1)} %get-tuple-element.46), channel_id=1, source_target_pairs={{0,4},{1,5},{2,6},{3,7},{4,0},{5,1},{6,2},{7,3},{8,12},{9,13},{10,... | collective-permute-start | bytes 393224 | tf_op jit(solution)/shard_map/ppermute | solution.py:242
  48.4 0.5 collective-permute-start.18
  48.9 0.1 add.59
  49.0 2.8 %collective-permute-start.12 = (f32[8,32,128]{2,1,0:T(8,128)S(1)}, f32[8,32,128]{2,1,0:T(8,128)S(1)}, u32[]{:S(2)}, u32[]{:S(2)}) collective-permute-start(f32[8,32,128]{2,1,0:T(8,128)S(1)} %get-tuple-element.41), channel_id=1, source_target_pairs={{0,2},{1,3},{2,4},{3,5},{4,6},{5,7},{6,0},{7,1},{8,10},{9,11},{10,... | collective-permute-start | bytes 393224 | tf_op jit(solution)/shard_map/ppermute | solution.py:242
  51.9 1.5 %collective-permute-start.13 = (f32[8,32,128]{2,1,0:T(8,128)S(1)}, f32[8,32,128]{2,1,0:T(8,128)S(1)}, u32[]{:S(2)}, u32[]{:S(2)}) collective-permute-start(f32[8,32,128]{2,1,0:T(8,128)S(1)} %get-tuple-element.43), channel_id=1, source_target_pairs={{0,4},{1,5},{2,6},{3,7},{4,0},{5,1},{6,2},{7,3},{8,12},{9,13},{10,... | collective-permute-start | bytes 393224 | tf_op jit(solution)/shard_map/ppermute | solution.py:242
  53.4 0.9 %collective-permute-start.14 = (f32[8,32,128]{2,1,0:T(8,128)S(1)}, f32[8,32,128]{2,1,0:T(8,128)S(1)}, u32[]{:S(2)}, u32[]{:S(2)}) collective-permute-start(f32[8,32,128]{2,1,0:T(8,128)S(1)} %get-tuple-element.42), channel_id=1, source_target_pairs={{0,6},{1,7},{2,0},{3,1},{4,2},{5,3},{6,4},{7,5},{8,14},{9,15},{10,... | collective-permute-start | bytes 393224 | tf_op jit(solution)/shard_map/ppermute | solution.py:242
  54.4 1.2 %collective-permute-done.17 = f32[8,32,128]{2,1,0:T(8,128)S(1)} collective-permute-done((f32[8,32,128]{2,1,0:T(8,128)S(1)}, f32[8,32,128]{2,1,0:T(8,128)S(1)}, u32[]{:S(2)}, u32[]{:S(2)}) %collective-permute-start.17) | collective-permute-done | bytes 131104 | tf_op jit(solution)/shard_map/ppermute | solution.py:242
  55.5 3.5 %collective-permute-done.18 = f32[8,32,128]{2,1,0:T(8,128)S(1)} collective-permute-done((f32[8,32,128]{2,1,0:T(8,128)S(1)}, f32[8,32,128]{2,1,0:T(8,128)S(1)}, u32[]{:S(2)}, u32[]{:S(2)}) %collective-permute-start.18) | collective-permute-done | bytes 131104 | tf_op jit(solution)/shard_map/ppermute | solution.py:242
  59.1 0.1 collective-permute-start.19
  59.8 1.3 %collective-permute-done.13 = f32[8,32,128]{2,1,0:T(8,128)S(1)} collective-permute-done((f32[8,32,128]{2,1,0:T(8,128)S(1)}, f32[8,32,128]{2,1,0:T(8,128)S(1)}, u32[]{:S(2)}, u32[]{:S(2)}) %collective-permute-start.13) | collective-permute-done | bytes 131104 | tf_op jit(solution)/shard_map/ppermute | solution.py:242
  61.2 1.7 %collective-permute-done.14 = f32[8,32,128]{2,1,0:T(8,128)S(1)} collective-permute-done((f32[8,32,128]{2,1,0:T(8,128)S(1)}, f32[8,32,128]{2,1,0:T(8,128)S(1)}, u32[]{:S(2)}, u32[]{:S(2)}) %collective-permute-start.14) | collective-permute-done | bytes 131104 | tf_op jit(solution)/shard_map/ppermute | solution.py:242
  62.8 4.7 %collective-permute-done.19 = f32[8,32,128]{2,1,0:T(8,128)S(1)} collective-permute-done((f32[8,32,128]{2,1,0:T(8,128)S(1)}, f32[8,32,128]{2,1,0:T(8,128)S(1)}, u32[]{:S(2)}, u32[]{:S(2)}) %collective-permute-start.19) | collective-permute-done | bytes 131104 | tf_op jit(solution)/shard_map/ppermute | solution.py:256
  67.6 0.1 select_add_fusion.1
  67.6 0.1 collective-permute-start.20
  67.7 1.4 %collective-permute-start.21 = (f32[8,32,128]{2,1,0:T(8,128)S(1)}, f32[8,32,128]{2,1,0:T(8,128)S(1)}, u32[]{:S(2)}, u32[]{:S(2)}) collective-permute-start(f32[8,32,128]{2,1,0:T(8,128)S(1)} %get-tuple-element.47), channel_id=1, source_target_pairs={{0,4},{1,5},{2,6},{3,7},{4,0},{5,1},{6,2},{7,3},{8,12},{9,13},{10,... | collective-permute-start | bytes 393224 | tf_op jit(solution)/shard_map/ppermute | solution.py:242
  69.1 1.3 %collective-permute-start.22 = (f32[8,32,128]{2,1,0:T(8,128)S(1)}, f32[8,32,128]{2,1,0:T(8,128)S(1)}, u32[]{:S(2)}, u32[]{:S(2)}) collective-permute-start(f32[8,32,128]{2,1,0:T(8,128)S(1)} %get-tuple-element.39), channel_id=1, source_target_pairs={{0,6},{1,7},{2,0},{3,1},{4,2},{5,3},{6,4},{7,5},{8,14},{9,15},{10,... | collective-permute-start | bytes 393224 | tf_op jit(solution)/shard_map/ppermute | solution.py:242
  70.4 2.3 %collective-permute-done.20.refs_1_ = f32[8,32,128]{2,1,0:T(8,128)S(1)} collective-permute-done((f32[8,32,128]{2,1,0:T(8,128)S(1)}, f32[8,32,128]{2,1,0:T(8,128)S(1)}, u32[]{:S(2)}, u32[]{:S(2)}) %collective-permute-start.20) | collective-permute-done | bytes 131104 | tf_op jit(solution)/shard_map/ppermute | solution.py:242
  72.7 2.1 %collective-permute-done.21.refs_2_ = f32[8,32,128]{2,1,0:T(8,128)S(1)} collective-permute-done((f32[8,32,128]{2,1,0:T(8,128)S(1)}, f32[8,32,128]{2,1,0:T(8,128)S(1)}, u32[]{:S(2)}, u32[]{:S(2)}) %collective-permute-start.21) | collective-permute-done | bytes 131104 | tf_op jit(solution)/shard_map/ppermute | solution.py:242
  74.8 1.3 %collective-permute-done.22.refs_3_ = f32[8,32,128]{2,1,0:T(8,128)S(1)} collective-permute-done((f32[8,32,128]{2,1,0:T(8,128)S(1)}, f32[8,32,128]{2,1,0:T(8,128)S(1)}, u32[]{:S(2)}, u32[]{:S(2)}) %collective-permute-start.22) | collective-permute-done | bytes 131104 | tf_op jit(solution)/shard_map/ppermute | solution.py:242
  76.1 0.8 %settle.1 = f32[32,32,128]{2,1,0:T(8,128)} custom-call(s32[1]{0:T(128)} %bitcast.band, f32[8,32,128]{2,1,0:T(8,128)S(1)} %get-tuple-element.49.refs_0_, f32[8,32,128]{2,1,0:T(8,128)S(1)} %collective-permute-done.20.refs_1_, f32[8,32,128]{2,1,0:T(8,128)S(1)} %collective-permute-done.21.refs_2_, f32[8,32,128]{2,1,0:T(8,128)S(1)} %collective-permute-done.22.refs_3_), custom_call_target="tpu_custom_call" | custom-call | tf_op jit(solution)/shard_map/settle/pallas_call | solution.py:354
  (19 shorter events, 0.2 us)
Async XLA Ops:
  0.0 1.0 %copy-start.1 = (f32[32,32,128]{2,1,0:T(8,128)S(1)}, f32[32,32,128]{2,1,0:T(8,128)}, u32[]{:S(2)}) copy-start(f32[32,32,128]{2,1,0:T(8,128)} %potential.1) | copy-start | bytes 1572868
  1.1 12.7 %collective-permute-start.1 = (f32[8,32,128]{2,1,0:T(8,128)S(1)}, f32[8,32,128]{2,1,0:T(8,128)S(1)}, u32[]{:S(2)}, u32[]{:S(2)}) collective-permute-start(f32[8,32,128]{2,1,0:T(8,128)S(1)} %get-tuple-element.24), channel_id=1, source_target_pairs={{0,2},{1,3},{2,4},{3,5},{4,6},{5,7},{6,0},{7,1},{8,10},{9,11},{10,... | collective-permute-start | bytes 393224 | tf_op jit(solution)/shard_map/ppermute | solution.py:242
  3.1 10.7 %collective-permute-start.2 = (f32[8,32,128]{2,1,0:T(8,128)S(1)}, f32[8,32,128]{2,1,0:T(8,128)S(1)}, u32[]{:S(2)}, u32[]{:S(2)}) collective-permute-start(f32[8,32,128]{2,1,0:T(8,128)S(1)} %get-tuple-element.25), channel_id=1, source_target_pairs={{0,4},{1,5},{2,6},{3,7},{4,0},{5,1},{6,2},{7,3},{8,12},{9,13},{10,... | collective-permute-start | bytes 393224 | tf_op jit(solution)/shard_map/ppermute | solution.py:242
  4.0 9.8 %collective-permute-start.3 = (f32[8,32,128]{2,1,0:T(8,128)S(1)}, f32[8,32,128]{2,1,0:T(8,128)S(1)}, u32[]{:S(2)}, u32[]{:S(2)}) collective-permute-start(f32[8,32,128]{2,1,0:T(8,128)S(1)} %get-tuple-element.26), channel_id=1, source_target_pairs={{0,6},{1,7},{2,0},{3,1},{4,2},{5,3},{6,4},{7,5},{8,14},{9,15},{10,... | collective-permute-start | bytes 393224 | tf_op jit(solution)/shard_map/ppermute | solution.py:242
  4.1 9.7 %collective-permute-start = (s32[1,1]{1,0:T(1,128)}, s32[1,1]{1,0:T(1,128)}, u32[]{:S(2)}, u32[]{:S(2)}) collective-permute-start(s32[1,1]{1,0:T(1,128)} %param.10), channel_id=1, source_target_pairs={{0,8},{8,16},{16,24},{24,32},{32,40},{40,48},{48,56},{56,64},{64,7... | collective-permute-start | bytes 20 | tf_op jit(solution)/shard_map/ppermute | solution.py:256
  6.2 1.2 %copy-start = (bf16[1,1,64,64,128]{4,3,2,1,0:T(8,128)(2,1)S(1)}, bf16[1,1,64,64,128]{4,3,2,1,0:T(8,128)(2,1)}, u32[]{:S(2)}) copy-start(bf16[1,1,64,64,128]{4,3,2,1,0:T(8,128)(2,1)} %param.8) | copy-start | bytes 3145732
  7.4 0.9 %copy-start.2 = (bf16[544,128]{1,0:T(8,128)(2,1)S(1)}, bf16[544,128]{1,0:T(8,128)(2,1)}, u32[]{:S(2)}) copy-start(bf16[544,128]{1,0:T(8,128)(2,1)} %constant.59.consts) | copy-start | bytes 417796
  14.4 7.7 %collective-permute-start.4 = (f32[8,32,128]{2,1,0:T(8,128)S(1)}, f32[8,32,128]{2,1,0:T(8,128)S(1)}, u32[]{:S(2)}, u32[]{:S(2)}) collective-permute-start(f32[8,32,128]{2,1,0:T(8,128)S(1)} %get-tuple-element.28), channel_id=1, source_target_pairs={{0,248},{8,0},{16,8},{24,16},{32,24},{40,32},{48,40},{56,48},{64,5... | collective-permute-start | bytes 393224 | tf_op jit(solution)/shard_map/ppermute | solution.py:256
  19.6 12.8 %collective-permute-start.5 = (f32[8,32,128]{2,1,0:T(8,128)S(1)}, f32[8,32,128]{2,1,0:T(8,128)S(1)}, u32[]{:S(2)}, u32[]{:S(2)}) collective-permute-start(f32[8,32,128]{2,1,0:T(8,128)S(1)} %get-tuple-element.27.refs_0_), channel_id=1, source_target_pairs={{0,2},{1,3},{2,4},{3,5},{4,6},{5,7},{6,0},{7,1},{8,10},{9,11},{10,... | collective-permute-start | bytes 393224 | tf_op jit(solution)/shard_map/ppermute | solution.py:242
  21.6 11.9 %collective-permute-start.6 = (f32[8,32,128]{2,1,0:T(8,128)S(1)}, f32[8,32,128]{2,1,0:T(8,128)S(1)}, u32[]{:S(2)}, u32[]{:S(2)}) collective-permute-start(f32[8,32,128]{2,1,0:T(8,128)S(1)} %get-tuple-element.27.refs_0_), channel_id=1, source_target_pairs={{0,6},{1,7},{2,0},{3,1},{4,2},{5,3},{6,4},{7,5},{8,14},{9,15},{10,... | collective-permute-start | bytes 393224 | tf_op jit(solution)/shard_map/ppermute | solution.py:242
  22.1 13.0 %collective-permute-start.9 = (f32[2,8,32,128]{3,2,1,0:T(8,128)S(1)}, f32[2,8,32,128]{3,2,1,0:T(8,128)S(1)}, u32[]{:S(2)}, u32[]{:S(2)}) collective-permute-start(f32[2,8,32,128]{3,2,1,0:T(8,128)S(1)} %stack.2.after), channel_id=1, source_target_pairs={{0,4},{1,5},{2,6},{3,7},{4,0},{5,1},{6,2},{7,3},{8,12},{9,13},{10,... | collective-permute-start | bytes 786440 | tf_op jit(solution)/shard_map/ppermute | solution.py:242
  24.3 9.2 %collective-permute-start.7 = (f32[8,32,128]{2,1,0:T(8,128)S(1)}, f32[8,32,128]{2,1,0:T(8,128)S(1)}, u32[]{:S(2)}, u32[]{:S(2)}) collective-permute-start(f32[8,32,128]{2,1,0:T(8,128)S(1)} %collective-permute-done.4.refs_1_.refs_3_), channel_id=1, source_target_pairs={{0,2},{1,3},{2,4},{3,5},{4,6},{5,7},{6,0},{7,1},{8,10},{9,11},{10,... | collective-permute-start | bytes 393224 | tf_op jit(solution)/shard_map/ppermute | solution.py:242
  25.8 9.2 %collective-permute-start.8 = (f32[8,32,128]{2,1,0:T(8,128)S(1)}, f32[8,32,128]{2,1,0:T(8,128)S(1)}, u32[]{:S(2)}, u32[]{:S(2)}) collective-permute-start(f32[8,32,128]{2,1,0:T(8,128)S(1)} %collective-permute-done.4.refs_1_.refs_3_), channel_id=1, source_target_pairs={{0,6},{1,7},{2,0},{3,1},{4,2},{5,3},{6,4},{7,5},{8,14},{9,15},{10,... | collective-permute-start | bytes 393224 | tf_op jit(solution)/shard_map/ppermute | solution.py:242
  35.2 2.7 %collective-permute-start.10 = (f32[8,8,32,128]{3,2,1,0:T(8,128)S(1)}, f32[8,8,32,128]{3,2,1,0:T(8,128)S(1)}, u32[]{:S(2)}, u32[]{:S(2)}) collective-permute-start(f32[8,8,32,128]{3,2,1,0:T(8,128)S(1)} %stack.3.own), channel_id=1, source_target_pairs={{0,1},{1,0},{2,3},{3,2},{4,5},{5,4},{6,7},{7,6},{8,9},{9,8},{10,11... | collective-permute-start | bytes 3145736 | tf_op jit(solution)/shard_map/ppermute | solution.py:251
  44.4 2.0 %collective-permute-start.15 = (f32[4,8,32,128]{3,2,1,0:T(8,128)S(1)}, f32[4,8,32,128]{3,2,1,0:T(8,128)S(1)}, u32[]{:S(2)}, u32[]{:S(2)}) collective-permute-start(f32[4,8,32,128]{3,2,1,0:T(8,128)S(1)} %get-tuple-element.38), channel_id=1, source_target_pairs={{0,1},{1,0},{2,3},{3,2},{4,5},{5,4},{6,7},{7,6},{8,9},{9,8},{10,11... | collective-permute-start | bytes 1572872 | tf_op jit(solution)/shard_map/ppermute | solution.py:251
  44.6 4.3 %collective-permute-start.11 = (f32[4,8,32,128]{3,2,1,0:T(8,128)S(1)}, f32[4,8,32,128]{3,2,1,0:T(8,128)S(1)}, u32[]{:S(2)}, u32[]{:S(2)}) collective-permute-start(f32[4,8,32,128]{3,2,1,0:T(8,128)S(1)} %get-tuple-element.36), channel_id=1, source_target_pairs={{0,1},{1,0},{2,3},{3,2},{4,5},{5,4},{6,7},{7,6},{8,9},{9,8},{10,11... | collective-permute-start | bytes 1572872 | tf_op jit(solution)/shard_map/ppermute | solution.py:251
  46.5 6.9 %collective-permute-start.16 = (f32[8,32,128]{2,1,0:T(8,128)S(1)}, f32[8,32,128]{2,1,0:T(8,128)S(1)}, u32[]{:S(2)}, u32[]{:S(2)}) collective-permute-start(f32[8,32,128]{2,1,0:T(8,128)S(1)} %get-tuple-element.44), channel_id=1, source_target_pairs={{0,2},{1,3},{2,4},{3,5},{4,6},{5,7},{6,0},{7,1},{8,10},{9,11},{10,... | collective-permute-start | bytes 393224 | tf_op jit(solution)/shard_map/ppermute | solution.py:242
  47.7 7.9 %collective-permute-start.17 = (f32[8,32,128]{2,1,0:T(8,128)S(1)}, f32[8,32,128]{2,1,0:T(8,128)S(1)}, u32[]{:S(2)}, u32[]{:S(2)}) collective-permute-start(f32[8,32,128]{2,1,0:T(8,128)S(1)} %get-tuple-element.46), channel_id=1, source_target_pairs={{0,4},{1,5},{2,6},{3,7},{4,0},{5,1},{6,2},{7,3},{8,12},{9,13},{10,... | collective-permute-start | bytes 393224 | tf_op jit(solution)/shard_map/ppermute | solution.py:242
  48.4 10.7 %collective-permute-start.18 = (f32[8,32,128]{2,1,0:T(8,128)S(1)}, f32[8,32,128]{2,1,0:T(8,128)S(1)}, u32[]{:S(2)}, u32[]{:S(2)}) collective-permute-start(f32[8,32,128]{2,1,0:T(8,128)S(1)} %get-tuple-element.45), channel_id=1, source_target_pairs={{0,6},{1,7},{2,0},{3,1},{4,2},{5,3},{6,4},{7,5},{8,14},{9,15},{10,... | collective-permute-start | bytes 393224 | tf_op jit(solution)/shard_map/ppermute | solution.py:242
  49.0 10.8 %collective-permute-start.12 = (f32[8,32,128]{2,1,0:T(8,128)S(1)}, f32[8,32,128]{2,1,0:T(8,128)S(1)}, u32[]{:S(2)}, u32[]{:S(2)}) collective-permute-start(f32[8,32,128]{2,1,0:T(8,128)S(1)} %get-tuple-element.41), channel_id=1, source_target_pairs={{0,2},{1,3},{2,4},{3,5},{4,6},{5,7},{6,0},{7,1},{8,10},{9,11},{10,... | collective-permute-start | bytes 393224 | tf_op jit(solution)/shard_map/ppermute | solution.py:242
  51.9 9.3 %collective-permute-start.13 = (f32[8,32,128]{2,1,0:T(8,128)S(1)}, f32[8,32,128]{2,1,0:T(8,128)S(1)}, u32[]{:S(2)}, u32[]{:S(2)}) collective-permute-start(f32[8,32,128]{2,1,0:T(8,128)S(1)} %get-tuple-element.43), channel_id=1, source_target_pairs={{0,4},{1,5},{2,6},{3,7},{4,0},{5,1},{6,2},{7,3},{8,12},{9,13},{10,... | collective-permute-start | bytes 393224 | tf_op jit(solution)/shard_map/ppermute | solution.py:242
  53.4 9.4 %collective-permute-start.14 = (f32[8,32,128]{2,1,0:T(8,128)S(1)}, f32[8,32,128]{2,1,0:T(8,128)S(1)}, u32[]{:S(2)}, u32[]{:S(2)}) collective-permute-start(f32[8,32,128]{2,1,0:T(8,128)S(1)} %get-tuple-element.42), channel_id=1, source_target_pairs={{0,6},{1,7},{2,0},{3,1},{4,2},{5,3},{6,4},{7,5},{8,14},{9,15},{10,... | collective-permute-start | bytes 393224 | tf_op jit(solution)/shard_map/ppermute | solution.py:242
  59.1 8.4 %collective-permute-start.19 = (f32[8,32,128]{2,1,0:T(8,128)S(1)}, f32[8,32,128]{2,1,0:T(8,128)S(1)}, u32[]{:S(2)}, u32[]{:S(2)}) collective-permute-start(f32[8,32,128]{2,1,0:T(8,128)S(1)} %fusion.2), channel_id=1, source_target_pairs={{0,8},{8,16},{16,24},{24,32},{32,40},{40,48},{48,56},{56,64},{64,7... | collective-permute-start | bytes 393224 | tf_op jit(solution)/shard_map/ppermute | solution.py:256
  67.6 5.0 %collective-permute-start.20 = (f32[8,32,128]{2,1,0:T(8,128)S(1)}, f32[8,32,128]{2,1,0:T(8,128)S(1)}, u32[]{:S(2)}, u32[]{:S(2)}) collective-permute-start(f32[8,32,128]{2,1,0:T(8,128)S(1)} %get-tuple-element.48), channel_id=1, source_target_pairs={{0,2},{1,3},{2,4},{3,5},{4,6},{5,7},{6,0},{7,1},{8,10},{9,11},{10,... | collective-permute-start | bytes 393224 | tf_op jit(solution)/shard_map/ppermute | solution.py:242
  67.7 7.1 %collective-permute-start.21 = (f32[8,32,128]{2,1,0:T(8,128)S(1)}, f32[8,32,128]{2,1,0:T(8,128)S(1)}, u32[]{:S(2)}, u32[]{:S(2)}) collective-permute-start(f32[8,32,128]{2,1,0:T(8,128)S(1)} %get-tuple-element.47), channel_id=1, source_target_pairs={{0,4},{1,5},{2,6},{3,7},{4,0},{5,1},{6,2},{7,3},{8,12},{9,13},{10,... | collective-permute-start | bytes 393224 | tf_op jit(solution)/shard_map/ppermute | solution.py:242
  69.1 7.0 %collective-permute-start.22 = (f32[8,32,128]{2,1,0:T(8,128)S(1)}, f32[8,32,128]{2,1,0:T(8,128)S(1)}, u32[]{:S(2)}, u32[]{:S(2)}) collective-permute-start(f32[8,32,128]{2,1,0:T(8,128)S(1)} %get-tuple-element.39), channel_id=1, source_target_pairs={{0,6},{1,7},{2,0},{3,1},{4,2},{5,3},{6,4},{7,5},{8,14},{9,15},{10,... | collective-permute-start | bytes 393224 | tf_op jit(solution)/shard_map/ppermute | solution.py:242

commit v6 on v5

--- a/solution.py
+++ b/solution.py
@@ -142,24 +142,19 @@
     lax.fori_loop(0, lines // 8, step, 0)
 
 
-def kinetics(after, states, partly, x_ref, y_ref, z_ref, once, again):
-    depth, width, length = once.shape
+def kinetics(after, states, partly, z_ref, out):
+    depth, width, length = out.shape
     half = depth // 2
 
-    def z_pass(source, before, out):
-        def zz(i, carry):
-            halves = [[source[pl.ds(j * half, half), r] for r in tiles(i)] for j in range(2)]
-            for j, part in enumerate(z_part(*halves, z_ref)):
-                for k, r in enumerate(tiles(i)):
-                    at = pl.ds(j * half, half)
-                    out[at, r] = before[at, r] + cut(part, k, length)
-            return carry
-
-        lax.fori_loop(0, width // 16, zz, 0)
-
-    z_pass(states, partly, once)
-    xy_pass(lambda z: once[pl.ds(z, 8)], again, 0, depth, x_ref, y_ref, False)
-    z_pass(once, again, again)
+    def zz(i, carry):
+        halves = [[states[pl.ds(j * half, half), r] for r in tiles(i)] for j in range(2)]
+        for j, part in enumerate(z_part(*halves, z_ref)):
+            for k, r in enumerate(tiles(i)):
+                at = pl.ds(j * half, half)
+                out[at, r] = partly[at, r] + cut(part, k, length)
+        return carry
+
+    lax.fori_loop(0, width // 16, zz, 0)
 
 
 def box_rows(band, code, column):
@@ -178,28 +173,27 @@
             use(pl.ds(slab * half + ((chip - back) & (CHIPS - 1)) * chunk, chunk), rows, ref[m])
 
 
-def both_steps(band, code, states, kinetic, again, x_ref, y_ref, z_ref, own, other, *refs):
-    (keep0, give0, keep1, give1), (pot, forced, total_h, extra, twice) = refs[:4], refs[4:]
+def both_steps(band, code, states, kinetic, x_ref, y_ref, z_ref, own, other, *refs):
+    (keep0, give0, keep1, give1), (pot, once, extra, twice) = refs[:4], refs[4:]
     depth, width, length = pot.shape
     half, column, double = depth // 2, width // 2, code[0, 0] & 1
     chunk = half // CHIPS
 
     def use(lines, rows, v):
         pot[lines, rows] = v
-        forced[lines, rows] = v * states[lines, rows]
+        once[lines, rows] = kinetic[lines, rows] + v * states[lines, rows]
 
     chunk_loop(band, code, (own, other), half, use)
-    xy_pass(lambda z: forced[pl.ds(z, 8)], extra, 0, depth, x_ref, y_ref, False)
+    xy_pass(lambda z: once[pl.ds(z, 8)], extra, 0, depth, x_ref, y_ref, False)
 
     def zz(i, sums):
         places = [pl.ds(0, half), pl.ds(half, half)]
-        parts = z_part(*[[forced[at, r] for r in tiles(i)] for at in places], z_ref)
+        parts = z_part(*[[once[at, r] for r in tiles(i)] for at in places], z_ref)
         for k, r in enumerate(tiles(i)):
             pairs = []
             for at, part in zip(places, parts):
-                s, h = states[at, r], kinetic[at, r] + forced[at, r]
-                w = again[at, r] + extra[at, r] + cut(part, k, length) + pot[at, r] * h
-                total_h[at, r] = h
+                s, h = states[at, r], once[at, r]
+                w = extra[at, r] + cut(part, k, length) + pot[at, r] * h
                 twice[at, r] = w
                 pairs.append((s * s, s * h, h * h, s * w, h * w, w * w))
             sums = tuple(v + fold(a + b) for v, a, b in zip(sums, *pairs))
@@ -224,7 +218,7 @@
         for out, rows in zip(outs, box_rows(band, code, column)):
             for k in range(CHIPS):
                 at = pl.ds(slab * half + (((band[0] >> 1) + k) & (CHIPS - 1)) * chunk, chunk)
-                u = by_s * states[at, rows] + by_h * total_h[at, rows] + by_w * twice[at, rows]
+                u = by_s * states[at, rows] + by_h * once[at, rows] + by_w * twice[at, rows]
                 out[k] = factor * (u * u)
 
 
@@ -330,13 +324,11 @@
     near = [here] + [to_next_chip(here, k) for k in (1, 3)]
     both = stacked(states, here, below)
     far = [below] + [to_next_chip(below, k) for k in (1, 3)] + [to_next_chip(both, 2)]
-    kinetic, again = kernel(kinetics, [box] * 2, [ANY] + [VMEM] * 5, MIDDLE, flops=4_000_000_000)(
-        both, states, partly, *ops
-    )
-    own = stacked(again, *near, *far)
+    (kinetic,) = kernel(kinetics, [box], [ANY] + [VMEM] * 3, MIDDLE, flops=4_000_000_000)(both, states, partly, ops[2])
+    own = stacked(kinetic, *near, *far)
     keep0, give0, keep1, give1 = kernel(
-        both_steps, [quarter] * 4, [SMEM] * 2 + [VMEM] * 8, BIG, scratch=[box] * 5
-    )(band[None], fragment_order, states, kinetic, again, *ops, own, to_other_core(own))
+        both_steps, [quarter] * 4, [SMEM] * 2 + [VMEM] * 7, BIG, scratch=[box] * 4
+    )(band[None], fragment_order, states, kinetic, *ops, own, to_other_core(own))
 
     def reduce_chip(keep, give):
         result, *arrived = around(list(keep + to_other_core(give)))

time: 77.1 us -> 77.1 us (level)
  Pallas kernels: 16.8 us -> 12.2 us
  waiting for transfers between devices: 28.2 us -> 32.4 us
    pallas_call x2, Pallas kernels: 12.5 us -> 7.83 us  [the longest x1 6.23 us: body(): kernel(both_steps, [quarter] * 4, [SMEM] * 2 + [VMEM] * 7, BIG, scratch=[...]
    ppermute x17, waiting for transfers between devices: 16.2 us -> 20.6 us  [to_next_chip(): return lax.ppermute(block, 'band', [(b, (b + 2 * k) % m) for b in range(m)])]
  transfers between devices with their start and end apart: 23 -> 23, of which waited for: 14 -> 15; matrix products, arithmetic and copies ran while one was open for 0% -> 0% of each run, Pallas kernels for 11% -> 6%
where the time goes in v6:
time: 77.1 us; the launch traced here: 76.9 us
  waiting for transfers between devices  32.4 us (42%)
  starting transfers between devices  27.4 us (36%)
  Pallas kernels  12.2 us (16%)
  local copies, waits for them, and re-layouts  3.22 us (4%)
  between operations  1.47 us (2%)
    ppermute x17, waiting for transfers between devices, to_next_chip(): return lax.ppermute(block, 'band', [(b, (b + 2 * k) % m) for b in range(m)])  20.6 us
    ppermute x17, starting transfers between devices, to_next_chip(): return lax.ppermute(block, 'band', [(b, (b + 2 * k) % m) for b in range(m)])  19.9 us
    ppermute x3, waiting for transfers between devices, to_group(): lax.ppermute(block, 'frag', [(i, (i + distance) % n) for i in range(n)])  7.76 us
    ppermute x3, starting transfers between devices, to_group(): lax.ppermute(block, 'frag', [(i, (i + distance) % n) for i in range(n)])  6.77 us
    pallas_call x1, Pallas kernels, body(): kernel(both_steps, [quarter] * 4, [SMEM] * 2 + [VMEM] * 7, BIG, scratch=[...  6.23 us
    ppermute x3, waiting for transfers between devices, to_other_core(): return lax.ppermute(block, 'band', [(b, b ^ 1) for b in range(2 * CHIPS)])  4.05 us
    unnamed x6, local copies, waits for them, and re-layouts  3.17 us
    pallas_call x1, Pallas kernels, body(): kernel(prepare, [box] * 2 + ops, [SMEM, VMEM, VMEM], MIDDLE)  2.73 us
  transfers between devices with their start and end apart: 23, of which 15 were waited for; matrix products, arithmetic and copies ran while one was open for 0% of the time, Pallas kernels for 6%

profile of v6, /device:TPU:24, one launch (start us, length us, event | category | flops | bytes accessed | tf_op | source)
XLA Modules:
  0.0 76.9 jit_solution(18009469358659859145)
XLA Ops:
  0.0 1.0 %copy-done.1 = f32[32,32,128]{2,1,0:T(8,128)S(1)} copy-done((f32[32,32,128]{2,1,0:T(8,128)S(1)}, f32[32,32,128]{2,1,0:T(8,128)}, u32[]{:S(2)}) %copy-start.1) | copy-done | bytes 524312
  1.1 2.0 %collective-permute-start.1 = (f32[8,32,128]{2,1,0:T(8,128)S(1)}, f32[8,32,128]{2,1,0:T(8,128)S(1)}, u32[]{:S(2)}, u32[]{:S(2)}) collective-permute-start(f32[8,32,128]{2,1,0:T(8,128)S(1)} %get-tuple-element.22), channel_id=1, source_target_pairs={{0,2},{1,3},{2,4},{3,5},{4,6},{5,7},{6,0},{7,1},{8,10},{9,11},{10,... | collective-permute-start | bytes 393224 | tf_op jit(solution)/shard_map/ppermute | solution.py:236
  3.1 0.9 %collective-permute-start.2 = (f32[8,32,128]{2,1,0:T(8,128)S(1)}, f32[8,32,128]{2,1,0:T(8,128)S(1)}, u32[]{:S(2)}, u32[]{:S(2)}) collective-permute-start(f32[8,32,128]{2,1,0:T(8,128)S(1)} %get-tuple-element.23), channel_id=1, source_target_pairs={{0,4},{1,5},{2,6},{3,7},{4,0},{5,1},{6,2},{7,3},{8,12},{9,13},{10,... | collective-permute-start | bytes 393224 | tf_op jit(solution)/shard_map/ppermute | solution.py:236
  4.0 0.1 collective-permute-start.3
  4.1 1.4 %collective-permute-start = (s32[1,1]{1,0:T(1,128)}, s32[1,1]{1,0:T(1,128)}, u32[]{:S(2)}, u32[]{:S(2)}) collective-permute-start(s32[1,1]{1,0:T(1,128)} %param.10), channel_id=1, source_target_pairs={{0,8},{8,16},{16,24},{24,32},{32,40},{40,48},{48,56},{56,64},{64,7... | collective-permute-start | bytes 20 | tf_op jit(solution)/shard_map/ppermute | solution.py:250
  6.2 1.2 %copy-done = bf16[1,1,64,64,128]{4,3,2,1,0:T(8,128)(2,1)S(1)} copy-done((bf16[1,1,64,64,128]{4,3,2,1,0:T(8,128)(2,1)S(1)}, bf16[1,1,64,64,128]{4,3,2,1,0:T(8,128)(2,1)}, u32[]{:S(2)}) %copy-start) | copy-done | bytes 1048600
  7.4 0.9 %copy-done.2 = bf16[544,128]{1,0:T(8,128)(2,1)S(1)} copy-done((bf16[544,128]{1,0:T(8,128)(2,1)S(1)}, bf16[544,128]{1,0:T(8,128)(2,1)}, u32[]{:S(2)}) %copy-start.2) | copy-done | bytes 139288
  8.3 2.7 %prepare.1 = (f32[64,64,128]{2,1,0:T(8,128)S(1)}, f32[64,64,128]{2,1,0:T(8,128)S(1)}, bf16[256,256]{1,0:T(8,128)(2,1)S(1)}, bf16[2,256,256]{2,1,0:T(8,128)(2,1)S(1)}, bf16[4,256,256]{2,1,0:T(8,128)(2,1)S(1)}) custom-call(s32[1,1]{1,0:T(1,128)S(6)} %copy.9.code, bf16[64,64,128]{2,1,0:T(8,128)(2,1)S(1)} %bitcast.33, bf16[544,128]{1,0:T(8,128)(2,1)S(1)} %copy-done.2), custom_call_target="tpu_custom_call" | custom-call | tf_op jit(solution)/shard_map/prepare/pallas_call | solution.py:311
  11.0 2.6 %collective-permute-done.code_before = s32[1,1]{1,0:T(1,128)} collective-permute-done((s32[1,1]{1,0:T(1,128)}, s32[1,1]{1,0:T(1,128)}, u32[]{:S(2)}, u32[]{:S(2)}) %collective-permute-start) | collective-permute-done | bytes 36 | tf_op jit(solution)/shard_map/ppermute | solution.py:250
  13.6 0.7 pick.1
  14.3 5.3 %collective-permute-start.4 = (f32[8,32,128]{2,1,0:T(8,128)S(1)}, f32[8,32,128]{2,1,0:T(8,128)S(1)}, u32[]{:S(2)}, u32[]{:S(2)}) collective-permute-start(f32[8,32,128]{2,1,0:T(8,128)S(1)} %get-tuple-element.26), channel_id=1, source_target_pairs={{0,248},{8,0},{16,8},{24,16},{32,24},{40,32},{48,40},{56,48},{64,5... | collective-permute-start | bytes 393224 | tf_op jit(solution)/shard_map/ppermute | solution.py:250
  19.6 2.0 %collective-permute-start.5 = (f32[8,32,128]{2,1,0:T(8,128)S(1)}, f32[8,32,128]{2,1,0:T(8,128)S(1)}, u32[]{:S(2)}, u32[]{:S(2)}) collective-permute-start(f32[8,32,128]{2,1,0:T(8,128)S(1)} %get-tuple-element.25.refs_0_), channel_id=1, source_target_pairs={{0,2},{1,3},{2,4},{3,5},{4,6},{5,7},{6,0},{7,1},{8,10},{9,11},{10,... | collective-permute-start | bytes 393224 | tf_op jit(solution)/shard_map/ppermute | solution.py:236
  21.6 0.5 collective-permute-done.4.refs_1_.refs_3_
  22.2 2.2 %collective-permute-start.9 = (f32[2,8,32,128]{3,2,1,0:T(8,128)S(1)}, f32[2,8,32,128]{3,2,1,0:T(8,128)S(1)}, u32[]{:S(2)}, u32[]{:S(2)}) collective-permute-start(f32[2,8,32,128]{3,2,1,0:T(8,128)S(1)} %stack.2.after), channel_id=1, source_target_pairs={{0,4},{1,5},{2,6},{3,7},{4,0},{5,1},{6,2},{7,3},{8,12},{9,13},{10,... | collective-permute-start | bytes 786440 | tf_op jit(solution)/shard_map/ppermute | solution.py:236
  24.4 1.5 %collective-permute-start.7 = (f32[8,32,128]{2,1,0:T(8,128)S(1)}, f32[8,32,128]{2,1,0:T(8,128)S(1)}, u32[]{:S(2)}, u32[]{:S(2)}) collective-permute-start(f32[8,32,128]{2,1,0:T(8,128)S(1)} %collective-permute-done.4.refs_1_.refs_3_), channel_id=1, source_target_pairs={{0,2},{1,3},{2,4},{3,5},{4,6},{5,7},{6,0},{7,1},{8,10},{9,11},{10,... | collective-permute-start | bytes 393224 | tf_op jit(solution)/shard_map/ppermute | solution.py:236
  25.9 0.5 collective-permute-start.8
  26.4 1.6 %kinetics.1.after.kinetic = f32[64,64,128]{2,1,0:T(8,128)S(1)} custom-call(f32[2,8,32,128]{3,2,1,0:T(8,128)S(1)} %stack.2.after, f32[64,64,128]{2,1,0:T(8,128)S(1)} %get-tuple-element.20.after.states, f32[64,64,128]{2,1,0:T(8,128)S(1)} %get-tuple-element.27.partly, bf16[4,256,256]{2,1,0:T(8,128)(2,1)S(1)} %get-tuple-element.28.z_ref), custom_call_target="tpu_custom_call" | custom-call | flops 4000000000 | bytes 4000000 | tf_op jit(solution)/shard_map/kinetics/pallas_call | solution.py:327
  28.0 0.6 collective-permute-done.5.refs_1_
  28.6 5.0 %collective-permute-done.6.refs_2_ = f32[8,32,128]{2,1,0:T(8,128)S(1)} collective-permute-done((f32[8,32,128]{2,1,0:T(8,128)S(1)}, f32[8,32,128]{2,1,0:T(8,128)S(1)}, u32[]{:S(2)}, u32[]{:S(2)}) %collective-permute-start.6) | collective-permute-done | bytes 131104 | tf_op jit(solution)/shard_map/ppermute | solution.py:236
  33.6 1.6 %collective-permute-done.8.refs_5_ = f32[8,32,128]{2,1,0:T(8,128)S(1)} collective-permute-done((f32[8,32,128]{2,1,0:T(8,128)S(1)}, f32[8,32,128]{2,1,0:T(8,128)S(1)}, u32[]{:S(2)}, u32[]{:S(2)}) %collective-permute-start.8) | collective-permute-done | bytes 131104 | tf_op jit(solution)/shard_map/ppermute | solution.py:236
  35.1 0.1 stack.3.own
  35.2 0.1 collective-permute-start.10
  35.3 2.6 %collective-permute-done.10.other = f32[8,8,32,128]{3,2,1,0:T(8,128)S(1)} collective-permute-done((f32[8,8,32,128]{3,2,1,0:T(8,128)S(1)}, f32[8,8,32,128]{3,2,1,0:T(8,128)S(1)}, u32[]{:S(2)}, u32[]{:S(2)}) %collective-permute-start.10) | collective-permute-done | bytes 1048608 | tf_op jit(solution)/shard_map/ppermute | solution.py:245
  38.0 6.2 %both_steps.1 = (f32[4,8,32,128]{3,2,1,0:T(8,128)S(1)}, f32[4,8,32,128]{3,2,1,0:T(8,128)S(1)}, f32[4,8,32,128]{3,2,1,0:T(8,128)S(1)}, f32[4,8,32,128]{3,2,1,0:T(8,128)S(1)}) custom-call(s32[1]{0:T(128)} %bitcast.band, s32[1,1]{1,0:T(1,128)S(6)} %copy.9.code, f32[64,64,128]{2,1,0:T(8,128)S(1)} %get-tuple-element.20.after.states, ...), custom_call_target="tpu_custom_call" | custom-call | tf_op jit(solution)/shard_map/both_steps/pallas_call | solution.py:329
  44.2 0.2 collective-permute-start.15
  44.4 0.4 collective-permute-start.11
  44.8 1.4 %collective-permute-done.15 = f32[4,8,32,128]{3,2,1,0:T(8,128)S(1)} collective-permute-done((f32[4,8,32,128]{3,2,1,0:T(8,128)S(1)}, f32[4,8,32,128]{3,2,1,0:T(8,128)S(1)}, u32[]{:S(2)}, u32[]{:S(2)}) %collective-permute-start.15) | collective-permute-done | bytes 524320 | tf_op jit(solution)/shard_map/ppermute | solution.py:245
  46.2 0.1 add.65
  46.3 1.4 %collective-permute-start.16 = (f32[8,32,128]{2,1,0:T(8,128)S(1)}, f32[8,32,128]{2,1,0:T(8,128)S(1)}, u32[]{:S(2)}, u32[]{:S(2)}) collective-permute-start(f32[8,32,128]{2,1,0:T(8,128)S(1)} %get-tuple-element.40), channel_id=1, source_target_pairs={{0,2},{1,3},{2,4},{3,5},{4,6},{5,7},{6,0},{7,1},{8,10},{9,11},{10,... | collective-permute-start | bytes 393224 | tf_op jit(solution)/shard_map/ppermute | solution.py:236
  47.7 0.8 %collective-permute-start.17 = (f32[8,32,128]{2,1,0:T(8,128)S(1)}, f32[8,32,128]{2,1,0:T(8,128)S(1)}, u32[]{:S(2)}, u32[]{:S(2)}) collective-permute-start(f32[8,32,128]{2,1,0:T(8,128)S(1)} %get-tuple-element.42), channel_id=1, source_target_pairs={{0,4},{1,5},{2,6},{3,7},{4,0},{5,1},{6,2},{7,3},{8,12},{9,13},{10,... | collective-permute-start | bytes 393224 | tf_op jit(solution)/shard_map/ppermute | solution.py:236
  48.4 0.5 collective-permute-start.18
  48.9 0.1 add.59
  49.0 2.8 %collective-permute-start.12 = (f32[8,32,128]{2,1,0:T(8,128)S(1)}, f32[8,32,128]{2,1,0:T(8,128)S(1)}, u32[]{:S(2)}, u32[]{:S(2)}) collective-permute-start(f32[8,32,128]{2,1,0:T(8,128)S(1)} %get-tuple-element.37), channel_id=1, source_target_pairs={{0,2},{1,3},{2,4},{3,5},{4,6},{5,7},{6,0},{7,1},{8,10},{9,11},{10,... | collective-permute-start | bytes 393224 | tf_op jit(solution)/shard_map/ppermute | solution.py:236
  51.9 1.5 %collective-permute-start.13 = (f32[8,32,128]{2,1,0:T(8,128)S(1)}, f32[8,32,128]{2,1,0:T(8,128)S(1)}, u32[]{:S(2)}, u32[]{:S(2)}) collective-permute-start(f32[8,32,128]{2,1,0:T(8,128)S(1)} %get-tuple-element.39), channel_id=1, source_target_pairs={{0,4},{1,5},{2,6},{3,7},{4,0},{5,1},{6,2},{7,3},{8,12},{9,13},{10,... | collective-permute-start | bytes 393224 | tf_op jit(solution)/shard_map/ppermute | solution.py:236
  53.4 0.9 %collective-permute-start.14 = (f32[8,32,128]{2,1,0:T(8,128)S(1)}, f32[8,32,128]{2,1,0:T(8,128)S(1)}, u32[]{:S(2)}, u32[]{:S(2)}) collective-permute-start(f32[8,32,128]{2,1,0:T(8,128)S(1)} %get-tuple-element.38), channel_id=1, source_target_pairs={{0,6},{1,7},{2,0},{3,1},{4,2},{5,3},{6,4},{7,5},{8,14},{9,15},{10,... | collective-permute-start | bytes 393224 | tf_op jit(solution)/shard_map/ppermute | solution.py:236
  54.3 1.2 %collective-permute-done.17 = f32[8,32,128]{2,1,0:T(8,128)S(1)} collective-permute-done((f32[8,32,128]{2,1,0:T(8,128)S(1)}, f32[8,32,128]{2,1,0:T(8,128)S(1)}, u32[]{:S(2)}, u32[]{:S(2)}) %collective-permute-start.17) | collective-permute-done | bytes 131104 | tf_op jit(solution)/shard_map/ppermute | solution.py:236
  55.5 3.6 %collective-permute-done.18 = f32[8,32,128]{2,1,0:T(8,128)S(1)} collective-permute-done((f32[8,32,128]{2,1,0:T(8,128)S(1)}, f32[8,32,128]{2,1,0:T(8,128)S(1)}, u32[]{:S(2)}, u32[]{:S(2)}) %collective-permute-start.18) | collective-permute-done | bytes 131104 | tf_op jit(solution)/shard_map/ppermute | solution.py:236
  59.1 0.1 collective-permute-start.19
  59.9 1.3 %collective-permute-done.13 = f32[8,32,128]{2,1,0:T(8,128)S(1)} collective-permute-done((f32[8,32,128]{2,1,0:T(8,128)S(1)}, f32[8,32,128]{2,1,0:T(8,128)S(1)}, u32[]{:S(2)}, u32[]{:S(2)}) %collective-permute-start.13) | collective-permute-done | bytes 131104 | tf_op jit(solution)/shard_map/ppermute | solution.py:236
  61.2 1.7 %collective-permute-done.14 = f32[8,32,128]{2,1,0:T(8,128)S(1)} collective-permute-done((f32[8,32,128]{2,1,0:T(8,128)S(1)}, f32[8,32,128]{2,1,0:T(8,128)S(1)}, u32[]{:S(2)}, u32[]{:S(2)}) %collective-permute-start.14) | collective-permute-done | bytes 131104 | tf_op jit(solution)/shard_map/ppermute | solution.py:236
  62.8 4.7 %collective-permute-done.19 = f32[8,32,128]{2,1,0:T(8,128)S(1)} collective-permute-done((f32[8,32,128]{2,1,0:T(8,128)S(1)}, f32[8,32,128]{2,1,0:T(8,128)S(1)}, u32[]{:S(2)}, u32[]{:S(2)}) %collective-permute-start.19) | collective-permute-done | bytes 131104 | tf_op jit(solution)/shard_map/ppermute | solution.py:250
  67.6 0.1 collective-permute-start.20
  67.7 1.3 %collective-permute-start.21 = (f32[8,32,128]{2,1,0:T(8,128)S(1)}, f32[8,32,128]{2,1,0:T(8,128)S(1)}, u32[]{:S(2)}, u32[]{:S(2)}) collective-permute-start(f32[8,32,128]{2,1,0:T(8,128)S(1)} %get-tuple-element.43), channel_id=1, source_target_pairs={{0,4},{1,5},{2,6},{3,7},{4,0},{5,1},{6,2},{7,3},{8,12},{9,13},{10,... | collective-permute-start | bytes 393224 | tf_op jit(solution)/shard_map/ppermute | solution.py:236
  69.1 1.3 %collective-permute-start.22 = (f32[8,32,128]{2,1,0:T(8,128)S(1)}, f32[8,32,128]{2,1,0:T(8,128)S(1)}, u32[]{:S(2)}, u32[]{:S(2)}) collective-permute-start(f32[8,32,128]{2,1,0:T(8,128)S(1)} %get-tuple-element.35), channel_id=1, source_target_pairs={{0,6},{1,7},{2,0},{3,1},{4,2},{5,3},{6,4},{7,5},{8,14},{9,15},{10,... | collective-permute-start | bytes 393224 | tf_op jit(solution)/shard_map/ppermute | solution.py:236
  70.4 2.3 %collective-permute-done.20.refs_1_ = f32[8,32,128]{2,1,0:T(8,128)S(1)} collective-permute-done((f32[8,32,128]{2,1,0:T(8,128)S(1)}, f32[8,32,128]{2,1,0:T(8,128)S(1)}, u32[]{:S(2)}, u32[]{:S(2)}) %collective-permute-start.20) | collective-permute-done | bytes 131104 | tf_op jit(solution)/shard_map/ppermute | solution.py:236
  72.7 2.1 %collective-permute-done.21.refs_2_ = f32[8,32,128]{2,1,0:T(8,128)S(1)} collective-permute-done((f32[8,32,128]{2,1,0:T(8,128)S(1)}, f32[8,32,128]{2,1,0:T(8,128)S(1)}, u32[]{:S(2)}, u32[]{:S(2)}) %collective-permute-start.21) | collective-permute-done | bytes 131104 | tf_op jit(solution)/shard_map/ppermute | solution.py:236
  74.8 1.3 %collective-permute-done.22.refs_3_ = f32[8,32,128]{2,1,0:T(8,128)S(1)} collective-permute-done((f32[8,32,128]{2,1,0:T(8,128)S(1)}, f32[8,32,128]{2,1,0:T(8,128)S(1)}, u32[]{:S(2)}, u32[]{:S(2)}) %collective-permute-start.22) | collective-permute-done | bytes 131104 | tf_op jit(solution)/shard_map/ppermute | solution.py:236
  76.1 0.8 %settle.1 = f32[32,32,128]{2,1,0:T(8,128)} custom-call(s32[1]{0:T(128)} %bitcast.band, f32[8,32,128]{2,1,0:T(8,128)S(1)} %get-tuple-element.45.refs_0_, f32[8,32,128]{2,1,0:T(8,128)S(1)} %collective-permute-done.20.refs_1_, f32[8,32,128]{2,1,0:T(8,128)S(1)} %collective-permute-done.21.refs_2_, f32[8,32,128]{2,1,0:T(8,128)S(1)} %collective-permute-done.22.refs_3_), custom_call_target="tpu_custom_call" | custom-call | tf_op jit(solution)/shard_map/settle/pallas_call | solution.py:346
  (19 shorter events, 0.3 us)
Async XLA Ops:
  0.0 1.0 %copy-start.1 = (f32[32,32,128]{2,1,0:T(8,128)S(1)}, f32[32,32,128]{2,1,0:T(8,128)}, u32[]{:S(2)}) copy-start(f32[32,32,128]{2,1,0:T(8,128)} %potential.1) | copy-start | bytes 1572868
  1.1 12.6 %collective-permute-start.1 = (f32[8,32,128]{2,1,0:T(8,128)S(1)}, f32[8,32,128]{2,1,0:T(8,128)S(1)}, u32[]{:S(2)}, u32[]{:S(2)}) collective-permute-start(f32[8,32,128]{2,1,0:T(8,128)S(1)} %get-tuple-element.22), channel_id=1, source_target_pairs={{0,2},{1,3},{2,4},{3,5},{4,6},{5,7},{6,0},{7,1},{8,10},{9,11},{10,... | collective-permute-start | bytes 393224 | tf_op jit(solution)/shard_map/ppermute | solution.py:236
  3.1 10.5 %collective-permute-start.2 = (f32[8,32,128]{2,1,0:T(8,128)S(1)}, f32[8,32,128]{2,1,0:T(8,128)S(1)}, u32[]{:S(2)}, u32[]{:S(2)}) collective-permute-start(f32[8,32,128]{2,1,0:T(8,128)S(1)} %get-tuple-element.23), channel_id=1, source_target_pairs={{0,4},{1,5},{2,6},{3,7},{4,0},{5,1},{6,2},{7,3},{8,12},{9,13},{10,... | collective-permute-start | bytes 393224 | tf_op jit(solution)/shard_map/ppermute | solution.py:236
  4.0 9.7 %collective-permute-start.3 = (f32[8,32,128]{2,1,0:T(8,128)S(1)}, f32[8,32,128]{2,1,0:T(8,128)S(1)}, u32[]{:S(2)}, u32[]{:S(2)}) collective-permute-start(f32[8,32,128]{2,1,0:T(8,128)S(1)} %get-tuple-element.24), channel_id=1, source_target_pairs={{0,6},{1,7},{2,0},{3,1},{4,2},{5,3},{6,4},{7,5},{8,14},{9,15},{10,... | collective-permute-start | bytes 393224 | tf_op jit(solution)/shard_map/ppermute | solution.py:236
  4.1 9.6 %collective-permute-start = (s32[1,1]{1,0:T(1,128)}, s32[1,1]{1,0:T(1,128)}, u32[]{:S(2)}, u32[]{:S(2)}) collective-permute-start(s32[1,1]{1,0:T(1,128)} %param.10), channel_id=1, source_target_pairs={{0,8},{8,16},{16,24},{24,32},{32,40},{40,48},{48,56},{56,64},{64,7... | collective-permute-start | bytes 20 | tf_op jit(solution)/shard_map/ppermute | solution.py:250
  6.2 1.2 %copy-start = (bf16[1,1,64,64,128]{4,3,2,1,0:T(8,128)(2,1)S(1)}, bf16[1,1,64,64,128]{4,3,2,1,0:T(8,128)(2,1)}, u32[]{:S(2)}) copy-start(bf16[1,1,64,64,128]{4,3,2,1,0:T(8,128)(2,1)} %param.8) | copy-start | bytes 3145732
  7.4 0.9 %copy-start.2 = (bf16[544,128]{1,0:T(8,128)(2,1)S(1)}, bf16[544,128]{1,0:T(8,128)(2,1)}, u32[]{:S(2)}) copy-start(bf16[544,128]{1,0:T(8,128)(2,1)} %constant.59.consts) | copy-start | bytes 417796
  14.3 7.8 %collective-permute-start.4 = (f32[8,32,128]{2,1,0:T(8,128)S(1)}, f32[8,32,128]{2,1,0:T(8,128)S(1)}, u32[]{:S(2)}, u32[]{:S(2)}) collective-permute-start(f32[8,32,128]{2,1,0:T(8,128)S(1)} %get-tuple-element.26), channel_id=1, source_target_pairs={{0,248},{8,0},{16,8},{24,16},{32,24},{40,32},{48,40},{56,48},{64,5... | collective-permute-start | bytes 393224 | tf_op jit(solution)/shard_map/ppermute | solution.py:250
  19.6 9.0 %collective-permute-start.5 = (f32[8,32,128]{2,1,0:T(8,128)S(1)}, f32[8,32,128]{2,1,0:T(8,128)S(1)}, u32[]{:S(2)}, u32[]{:S(2)}) collective-permute-start(f32[8,32,128]{2,1,0:T(8,128)S(1)} %get-tuple-element.25.refs_0_), channel_id=1, source_target_pairs={{0,2},{1,3},{2,4},{3,5},{4,6},{5,7},{6,0},{7,1},{8,10},{9,11},{10,... | collective-permute-start | bytes 393224 | tf_op jit(solution)/shard_map/ppermute | solution.py:236
  21.6 11.9 %collective-permute-start.6 = (f32[8,32,128]{2,1,0:T(8,128)S(1)}, f32[8,32,128]{2,1,0:T(8,128)S(1)}, u32[]{:S(2)}, u32[]{:S(2)}) collective-permute-start(f32[8,32,128]{2,1,0:T(8,128)S(1)} %get-tuple-element.25.refs_0_), channel_id=1, source_target_pairs={{0,6},{1,7},{2,0},{3,1},{4,2},{5,3},{6,4},{7,5},{8,14},{9,15},{10,... | collective-permute-start | bytes 393224 | tf_op jit(solution)/shard_map/ppermute | solution.py:236
  22.2 13.0 %collective-permute-start.9 = (f32[2,8,32,128]{3,2,1,0:T(8,128)S(1)}, f32[2,8,32,128]{3,2,1,0:T(8,128)S(1)}, u32[]{:S(2)}, u32[]{:S(2)}) collective-permute-start(f32[2,8,32,128]{3,2,1,0:T(8,128)S(1)} %stack.2.after), channel_id=1, source_target_pairs={{0,4},{1,5},{2,6},{3,7},{4,0},{5,1},{6,2},{7,3},{8,12},{9,13},{10,... | collective-permute-start | bytes 786440 | tf_op jit(solution)/shard_map/ppermute | solution.py:236
  24.4 9.2 %collective-permute-start.7 = (f32[8,32,128]{2,1,0:T(8,128)S(1)}, f32[8,32,128]{2,1,0:T(8,128)S(1)}, u32[]{:S(2)}, u32[]{:S(2)}) collective-permute-start(f32[8,32,128]{2,1,0:T(8,128)S(1)} %collective-permute-done.4.refs_1_.refs_3_), channel_id=1, source_target_pairs={{0,2},{1,3},{2,4},{3,5},{4,6},{5,7},{6,0},{7,1},{8,10},{9,11},{10,... | collective-permute-start | bytes 393224 | tf_op jit(solution)/shard_map/ppermute | solution.py:236
  25.9 9.2 %collective-permute-start.8 = (f32[8,32,128]{2,1,0:T(8,128)S(1)}, f32[8,32,128]{2,1,0:T(8,128)S(1)}, u32[]{:S(2)}, u32[]{:S(2)}) collective-permute-start(f32[8,32,128]{2,1,0:T(8,128)S(1)} %collective-permute-done.4.refs_1_.refs_3_), channel_id=1, source_target_pairs={{0,6},{1,7},{2,0},{3,1},{4,2},{5,3},{6,4},{7,5},{8,14},{9,15},{10,... | collective-permute-start | bytes 393224 | tf_op jit(solution)/shard_map/ppermute | solution.py:236
  35.2 2.7 %collective-permute-start.10 = (f32[8,8,32,128]{3,2,1,0:T(8,128)S(1)}, f32[8,8,32,128]{3,2,1,0:T(8,128)S(1)}, u32[]{:S(2)}, u32[]{:S(2)}) collective-permute-start(f32[8,8,32,128]{3,2,1,0:T(8,128)S(1)} %stack.3.own), channel_id=1, source_target_pairs={{0,1},{1,0},{2,3},{3,2},{4,5},{5,4},{6,7},{7,6},{8,9},{9,8},{10,11... | collective-permute-start | bytes 3145736 | tf_op jit(solution)/shard_map/ppermute | solution.py:245
  44.2 2.0 %collective-permute-start.15 = (f32[4,8,32,128]{3,2,1,0:T(8,128)S(1)}, f32[4,8,32,128]{3,2,1,0:T(8,128)S(1)}, u32[]{:S(2)}, u32[]{:S(2)}) collective-permute-start(f32[4,8,32,128]{3,2,1,0:T(8,128)S(1)} %get-tuple-element.34), channel_id=1, source_target_pairs={{0,1},{1,0},{2,3},{3,2},{4,5},{5,4},{6,7},{7,6},{8,9},{9,8},{10,11... | collective-permute-start | bytes 1572872 | tf_op jit(solution)/shard_map/ppermute | solution.py:245
  44.4 4.5 %collective-permute-start.11 = (f32[4,8,32,128]{3,2,1,0:T(8,128)S(1)}, f32[4,8,32,128]{3,2,1,0:T(8,128)S(1)}, u32[]{:S(2)}, u32[]{:S(2)}) collective-permute-start(f32[4,8,32,128]{3,2,1,0:T(8,128)S(1)} %get-tuple-element.32), channel_id=1, source_target_pairs={{0,1},{1,0},{2,3},{3,2},{4,5},{5,4},{6,7},{7,6},{8,9},{9,8},{10,11... | collective-permute-start | bytes 1572872 | tf_op jit(solution)/shard_map/ppermute | solution.py:245
  46.3 7.1 %collective-permute-start.16 = (f32[8,32,128]{2,1,0:T(8,128)S(1)}, f32[8,32,128]{2,1,0:T(8,128)S(1)}, u32[]{:S(2)}, u32[]{:S(2)}) collective-permute-start(f32[8,32,128]{2,1,0:T(8,128)S(1)} %get-tuple-element.40), channel_id=1, source_target_pairs={{0,2},{1,3},{2,4},{3,5},{4,6},{5,7},{6,0},{7,1},{8,10},{9,11},{10,... | collective-permute-start | bytes 393224 | tf_op jit(solution)/shard_map/ppermute | solution.py:236
  47.7 7.9 %collective-permute-start.17 = (f32[8,32,128]{2,1,0:T(8,128)S(1)}, f32[8,32,128]{2,1,0:T(8,128)S(1)}, u32[]{:S(2)}, u32[]{:S(2)}) collective-permute-start(f32[8,32,128]{2,1,0:T(8,128)S(1)} %get-tuple-element.42), channel_id=1, source_target_pairs={{0,4},{1,5},{2,6},{3,7},{4,0},{5,1},{6,2},{7,3},{8,12},{9,13},{10,... | collective-permute-start | bytes 393224 | tf_op jit(solution)/shard_map/ppermute | solution.py:236
  48.4 10.7 %collective-permute-start.18 = (f32[8,32,128]{2,1,0:T(8,128)S(1)}, f32[8,32,128]{2,1,0:T(8,128)S(1)}, u32[]{:S(2)}, u32[]{:S(2)}) collective-permute-start(f32[8,32,128]{2,1,0:T(8,128)S(1)} %get-tuple-element.41), channel_id=1, source_target_pairs={{0,6},{1,7},{2,0},{3,1},{4,2},{5,3},{6,4},{7,5},{8,14},{9,15},{10,... | collective-permute-start | bytes 393224 | tf_op jit(solution)/shard_map/ppermute | solution.py:236
  49.0 10.9 %collective-permute-start.12 = (f32[8,32,128]{2,1,0:T(8,128)S(1)}, f32[8,32,128]{2,1,0:T(8,128)S(1)}, u32[]{:S(2)}, u32[]{:S(2)}) collective-permute-start(f32[8,32,128]{2,1,0:T(8,128)S(1)} %get-tuple-element.37), channel_id=1, source_target_pairs={{0,2},{1,3},{2,4},{3,5},{4,6},{5,7},{6,0},{7,1},{8,10},{9,11},{10,... | collective-permute-start | bytes 393224 | tf_op jit(solution)/shard_map/ppermute | solution.py:236
  51.9 9.3 %collective-permute-start.13 = (f32[8,32,128]{2,1,0:T(8,128)S(1)}, f32[8,32,128]{2,1,0:T(8,128)S(1)}, u32[]{:S(2)}, u32[]{:S(2)}) collective-permute-start(f32[8,32,128]{2,1,0:T(8,128)S(1)} %get-tuple-element.39), channel_id=1, source_target_pairs={{0,4},{1,5},{2,6},{3,7},{4,0},{5,1},{6,2},{7,3},{8,12},{9,13},{10,... | collective-permute-start | bytes 393224 | tf_op jit(solution)/shard_map/ppermute | solution.py:236
  53.4 9.4 %collective-permute-start.14 = (f32[8,32,128]{2,1,0:T(8,128)S(1)}, f32[8,32,128]{2,1,0:T(8,128)S(1)}, u32[]{:S(2)}, u32[]{:S(2)}) collective-permute-start(f32[8,32,128]{2,1,0:T(8,128)S(1)} %get-tuple-element.38), channel_id=1, source_target_pairs={{0,6},{1,7},{2,0},{3,1},{4,2},{5,3},{6,4},{7,5},{8,14},{9,15},{10,... | collective-permute-start | bytes 393224 | tf_op jit(solution)/shard_map/ppermute | solution.py:236
  59.1 8.4 %collective-permute-start.19 = (f32[8,32,128]{2,1,0:T(8,128)S(1)}, f32[8,32,128]{2,1,0:T(8,128)S(1)}, u32[]{:S(2)}, u32[]{:S(2)}) collective-permute-start(f32[8,32,128]{2,1,0:T(8,128)S(1)} %fusion.2), channel_id=1, source_target_pairs={{0,8},{8,16},{16,24},{24,32},{32,40},{40,48},{48,56},{56,64},{64,7... | collective-permute-start | bytes 393224 | tf_op jit(solution)/shard_map/ppermute | solution.py:250
  67.6 5.0 %collective-permute-start.20 = (f32[8,32,128]{2,1,0:T(8,128)S(1)}, f32[8,32,128]{2,1,0:T(8,128)S(1)}, u32[]{:S(2)}, u32[]{:S(2)}) collective-permute-start(f32[8,32,128]{2,1,0:T(8,128)S(1)} %get-tuple-element.44), channel_id=1, source_target_pairs={{0,2},{1,3},{2,4},{3,5},{4,6},{5,7},{6,0},{7,1},{8,10},{9,11},{10,... | collective-permute-start | bytes 393224 | tf_op jit(solution)/shard_map/ppermute | solution.py:236
  67.7 7.1 %collective-permute-start.21 = (f32[8,32,128]{2,1,0:T(8,128)S(1)}, f32[8,32,128]{2,1,0:T(8,128)S(1)}, u32[]{:S(2)}, u32[]{:S(2)}) collective-permute-start(f32[8,32,128]{2,1,0:T(8,128)S(1)} %get-tuple-element.43), channel_id=1, source_target_pairs={{0,4},{1,5},{2,6},{3,7},{4,0},{5,1},{6,2},{7,3},{8,12},{9,13},{10,... | collective-permute-start | bytes 393224 | tf_op jit(solution)/shard_map/ppermute | solution.py:236
  69.1 7.0 %collective-permute-start.22 = (f32[8,32,128]{2,1,0:T(8,128)S(1)}, f32[8,32,128]{2,1,0:T(8,128)S(1)}, u32[]{:S(2)}, u32[]{:S(2)}) collective-permute-start(f32[8,32,128]{2,1,0:T(8,128)S(1)} %get-tuple-element.35), channel_id=1, source_target_pairs={{0,6},{1,7},{2,0},{3,1},{4,2},{5,3},{6,4},{7,5},{8,14},{9,15},{10,... | collective-permute-start | bytes 393224 | tf_op jit(solution)/shard_map/ppermute | solution.py:236

commit v7 on v6

--- a/solution.py
+++ b/solution.py
@@ -139,7 +139,7 @@
         out[pl.ds(z + 4, 4)] = upper.reshape(4, width, length)
         return carry
 
-    lax.fori_loop(0, lines // 8, step, 0)
+    lax.fori_loop(0, lines // 8, step, 0, unroll=2)
 
 
 def kinetics(after, states, partly, z_ref, out):
@@ -200,7 +200,7 @@
         return sums
 
     zero = jnp.zeros((8, length), jnp.float32)
-    ss, sh, hh, sw, hw, ww = (total(v) for v in lax.fori_loop(0, width // 16, zz, (zero,) * 6))
+    ss, sh, hh, sw, hw, ww = (total(v) for v in lax.fori_loop(0, width // 16, zz, (zero,) * 6, unroll=2))
     cells = (2 * half * column * length * (1 + double)).astype(jnp.float32)
     first = 1.0 + STEP_LENGTH * sh / (ss + EPSILON)
     tt = first * first * ss - 2.0 * STEP_LENGTH * first * sh + STEP_LENGTH * STEP_LENGTH * hh

time: 77.1 us -> 75.4 us (0.978)
  Pallas kernels: 12.2 us -> 10.6 us
    pallas_call x1, Pallas kernels: 6.23 us -> 5.3 us  [body(): kernel(both_steps, [quarter] * 4, [SMEM] * 2 + [VMEM] * 7, BIG, scratch=[...]
  transfers between devices with their start and end apart: 23 -> 23, of which waited for: 15 -> 15; matrix products, arithmetic and copies ran while one was open for 0% -> 0% of each run, Pallas kernels for 6% -> 5%
where the time goes in v7:
time: 75.4 us; the launch traced here: 75.2 us
  waiting for transfers between devices  32.8 us (44%)
  starting transfers between devices  26.8 us (36%)
  Pallas kernels  10.6 us (14%)
  local copies, waits for them, and re-layouts  3.22 us (4%)
  between operations  1.48 us (2%)
    ppermute x17, waiting for transfers between devices, to_next_chip(): return lax.ppermute(block, 'band', [(b, (b + 2 * k) % m) for b in range(m)])  20.3 us
    ppermute x17, starting transfers between devices, to_next_chip(): return lax.ppermute(block, 'band', [(b, (b + 2 * k) % m) for b in range(m)])  19.3 us
    ppermute x3, waiting for transfers between devices, to_group(): lax.ppermute(block, 'frag', [(i, (i + distance) % n) for i in range(n)])  8.41 us
    ppermute x3, starting transfers between devices, to_group(): lax.ppermute(block, 'frag', [(i, (i + distance) % n) for i in range(n)])  6.77 us
    pallas_call x1, Pallas kernels, body(): kernel(both_steps, [quarter] * 4, [SMEM] * 2 + [VMEM] * 7, BIG, scratch=[...  5.3 us
    ppermute x3, waiting for transfers between devices, to_other_core(): return lax.ppermute(block, 'band', [(b, b ^ 1) for b in range(2 * CHIPS)])  4.05 us
    unnamed x6, local copies, waits for them, and re-layouts  3.17 us
    pallas_call x1, Pallas kernels, body(): kernel(prepare, [box] * 2 + ops, [SMEM, VMEM, VMEM], MIDDLE)  2.12 us
  transfers between devices with their start and end apart: 23, of which 15 were waited for; matrix products, arithmetic and copies ran while one was open for 0% of the time, Pallas kernels for 5%

profile of v7, /device:TPU:24, one launch (start us, length us, event | category | flops | bytes accessed | tf_op | source)
XLA Modules:
  0.0 75.2 jit_solution(11796419990357422908)
XLA Ops:
  0.0 1.0 %copy-done.1 = f32[32,32,128]{2,1,0:T(8,128)S(1)} copy-done((f32[32,32,128]{2,1,0:T(8,128)S(1)}, f32[32,32,128]{2,1,0:T(8,128)}, u32[]{:S(2)}) %copy-start.1) | copy-done | bytes 524312
  1.1 2.0 %collective-permute-start.1 = (f32[8,32,128]{2,1,0:T(8,128)S(1)}, f32[8,32,128]{2,1,0:T(8,128)S(1)}, u32[]{:S(2)}, u32[]{:S(2)}) collective-permute-start(f32[8,32,128]{2,1,0:T(8,128)S(1)} %get-tuple-element.22), channel_id=1, source_target_pairs={{0,2},{1,3},{2,4},{3,5},{4,6},{5,7},{6,0},{7,1},{8,10},{9,11},{10,... | collective-permute-start | bytes 393224 | tf_op jit(solution)/shard_map/ppermute | solution.py:236
  3.1 0.9 %collective-permute-start.2 = (f32[8,32,128]{2,1,0:T(8,128)S(1)}, f32[8,32,128]{2,1,0:T(8,128)S(1)}, u32[]{:S(2)}, u32[]{:S(2)}) collective-permute-start(f32[8,32,128]{2,1,0:T(8,128)S(1)} %get-tuple-element.23), channel_id=1, source_target_pairs={{0,4},{1,5},{2,6},{3,7},{4,0},{5,1},{6,2},{7,3},{8,12},{9,13},{10,... | collective-permute-start | bytes 393224 | tf_op jit(solution)/shard_map/ppermute | solution.py:236
  4.0 0.1 collective-permute-start.3
  4.1 1.4 %collective-permute-start = (s32[1,1]{1,0:T(1,128)}, s32[1,1]{1,0:T(1,128)}, u32[]{:S(2)}, u32[]{:S(2)}) collective-permute-start(s32[1,1]{1,0:T(1,128)} %param.10), channel_id=1, source_target_pairs={{0,8},{8,16},{16,24},{24,32},{32,40},{40,48},{48,56},{56,64},{64,7... | collective-permute-start | bytes 20 | tf_op jit(solution)/shard_map/ppermute | solution.py:250
  6.2 1.2 %copy-done = bf16[1,1,64,64,128]{4,3,2,1,0:T(8,128)(2,1)S(1)} copy-done((bf16[1,1,64,64,128]{4,3,2,1,0:T(8,128)(2,1)S(1)}, bf16[1,1,64,64,128]{4,3,2,1,0:T(8,128)(2,1)}, u32[]{:S(2)}) %copy-start) | copy-done | bytes 1048600
  7.4 0.9 %copy-done.2 = bf16[544,128]{1,0:T(8,128)(2,1)S(1)} copy-done((bf16[544,128]{1,0:T(8,128)(2,1)S(1)}, bf16[544,128]{1,0:T(8,128)(2,1)}, u32[]{:S(2)}) %copy-start.2) | copy-done | bytes 139288
  8.3 2.1 %prepare.1 = (f32[64,64,128]{2,1,0:T(8,128)S(1)}, f32[64,64,128]{2,1,0:T(8,128)S(1)}, bf16[256,256]{1,0:T(8,128)(2,1)S(1)}, bf16[2,256,256]{2,1,0:T(8,128)(2,1)S(1)}, bf16[4,256,256]{2,1,0:T(8,128)(2,1)S(1)}) custom-call(s32[1,1]{1,0:T(1,128)S(6)} %copy.9.code, bf16[64,64,128]{2,1,0:T(8,128)(2,1)S(1)} %bitcast.33, bf16[544,128]{1,0:T(8,128)(2,1)S(1)} %copy-done.2), custom_call_target="tpu_custom_call" | custom-call | tf_op jit(solution)/shard_map/prepare/pallas_call | solution.py:311
  10.4 3.2 %collective-permute-done.code_before = s32[1,1]{1,0:T(1,128)} collective-permute-done((s32[1,1]{1,0:T(1,128)}, s32[1,1]{1,0:T(1,128)}, u32[]{:S(2)}, u32[]{:S(2)}) %collective-permute-start) | collective-permute-done | bytes 36 | tf_op jit(solution)/shard_map/ppermute | solution.py:250
  13.6 0.7 pick.1
  14.3 5.3 %collective-permute-start.4 = (f32[8,32,128]{2,1,0:T(8,128)S(1)}, f32[8,32,128]{2,1,0:T(8,128)S(1)}, u32[]{:S(2)}, u32[]{:S(2)}) collective-permute-start(f32[8,32,128]{2,1,0:T(8,128)S(1)} %get-tuple-element.26), channel_id=1, source_target_pairs={{0,248},{8,0},{16,8},{24,16},{32,24},{40,32},{48,40},{56,48},{64,5... | collective-permute-start | bytes 393224 | tf_op jit(solution)/shard_map/ppermute | solution.py:250
  19.6 1.4 %collective-permute-start.5 = (f32[8,32,128]{2,1,0:T(8,128)S(1)}, f32[8,32,128]{2,1,0:T(8,128)S(1)}, u32[]{:S(2)}, u32[]{:S(2)}) collective-permute-start(f32[8,32,128]{2,1,0:T(8,128)S(1)} %get-tuple-element.25.refs_0_), channel_id=1, source_target_pairs={{0,2},{1,3},{2,4},{3,5},{4,6},{5,7},{6,0},{7,1},{8,10},{9,11},{10,... | collective-permute-start | bytes 393224 | tf_op jit(solution)/shard_map/ppermute | solution.py:236
  21.0 0.6 collective-permute-start.6
  21.6 0.5 collective-permute-done.4.refs_1_.refs_3_
  22.2 1.8 %collective-permute-start.9 = (f32[2,8,32,128]{3,2,1,0:T(8,128)S(1)}, f32[2,8,32,128]{3,2,1,0:T(8,128)S(1)}, u32[]{:S(2)}, u32[]{:S(2)}) collective-permute-start(f32[2,8,32,128]{3,2,1,0:T(8,128)S(1)} %stack.2.after), channel_id=1, source_target_pairs={{0,4},{1,5},{2,6},{3,7},{4,0},{5,1},{6,2},{7,3},{8,12},{9,13},{10,... | collective-permute-start | bytes 786440 | tf_op jit(solution)/shard_map/ppermute | solution.py:236
  24.0 1.9 %collective-permute-start.7 = (f32[8,32,128]{2,1,0:T(8,128)S(1)}, f32[8,32,128]{2,1,0:T(8,128)S(1)}, u32[]{:S(2)}, u32[]{:S(2)}) collective-permute-start(f32[8,32,128]{2,1,0:T(8,128)S(1)} %collective-permute-done.4.refs_1_.refs_3_), channel_id=1, source_target_pairs={{0,2},{1,3},{2,4},{3,5},{4,6},{5,7},{6,0},{7,1},{8,10},{9,11},{10,... | collective-permute-start | bytes 393224 | tf_op jit(solution)/shard_map/ppermute | solution.py:236
  25.9 0.1 collective-permute-start.8
  26.0 1.6 %kinetics.1.after.kinetic = f32[64,64,128]{2,1,0:T(8,128)S(1)} custom-call(f32[2,8,32,128]{3,2,1,0:T(8,128)S(1)} %stack.2.after, f32[64,64,128]{2,1,0:T(8,128)S(1)} %get-tuple-element.20.after.states, f32[64,64,128]{2,1,0:T(8,128)S(1)} %get-tuple-element.27.partly, bf16[4,256,256]{2,1,0:T(8,128)(2,1)S(1)} %get-tuple-element.28.z_ref), custom_call_target="tpu_custom_call" | custom-call | flops 4000000000 | bytes 4000000 | tf_op jit(solution)/shard_map/kinetics/pallas_call | solution.py:327
  27.6 5.3 %collective-permute-done.6.refs_2_ = f32[8,32,128]{2,1,0:T(8,128)S(1)} collective-permute-done((f32[8,32,128]{2,1,0:T(8,128)S(1)}, f32[8,32,128]{2,1,0:T(8,128)S(1)}, u32[]{:S(2)}, u32[]{:S(2)}) %collective-permute-start.6) | collective-permute-done | bytes 131104 | tf_op jit(solution)/shard_map/ppermute | solution.py:236
  32.9 0.1 collective-permute-done.7.refs_4_
  33.0 2.0 %collective-permute-done.8.refs_5_ = f32[8,32,128]{2,1,0:T(8,128)S(1)} collective-permute-done((f32[8,32,128]{2,1,0:T(8,128)S(1)}, f32[8,32,128]{2,1,0:T(8,128)S(1)}, u32[]{:S(2)}, u32[]{:S(2)}) %collective-permute-start.8) | collective-permute-done | bytes 131104 | tf_op jit(solution)/shard_map/ppermute | solution.py:236
  35.1 0.1 collective-permute-start.10
  35.2 2.6 %collective-permute-done.10.other = f32[8,8,32,128]{3,2,1,0:T(8,128)S(1)} collective-permute-done((f32[8,8,32,128]{3,2,1,0:T(8,128)S(1)}, f32[8,8,32,128]{3,2,1,0:T(8,128)S(1)}, u32[]{:S(2)}, u32[]{:S(2)}) %collective-permute-start.10) | collective-permute-done | bytes 1048608 | tf_op jit(solution)/shard_map/ppermute | solution.py:245
  37.8 5.3 %both_steps.1 = (f32[4,8,32,128]{3,2,1,0:T(8,128)S(1)}, f32[4,8,32,128]{3,2,1,0:T(8,128)S(1)}, f32[4,8,32,128]{3,2,1,0:T(8,128)S(1)}, f32[4,8,32,128]{3,2,1,0:T(8,128)S(1)}) custom-call(s32[1]{0:T(128)} %bitcast.band, s32[1,1]{1,0:T(1,128)S(6)} %copy.9.code, f32[64,64,128]{2,1,0:T(8,128)S(1)} %get-tuple-element.20.after.states, ...), custom_call_target="tpu_custom_call" | custom-call | tf_op jit(solution)/shard_map/both_steps/pallas_call | solution.py:329
  43.1 0.2 collective-permute-start.15
  43.3 0.4 collective-permute-start.11
  43.7 1.4 %collective-permute-done.15 = f32[4,8,32,128]{3,2,1,0:T(8,128)S(1)} collective-permute-done((f32[4,8,32,128]{3,2,1,0:T(8,128)S(1)}, f32[4,8,32,128]{3,2,1,0:T(8,128)S(1)}, u32[]{:S(2)}, u32[]{:S(2)}) %collective-permute-start.15) | collective-permute-done | bytes 524320 | tf_op jit(solution)/shard_map/ppermute | solution.py:245
  45.1 0.1 add.65
  45.2 0.7 collective-permute-start.16
  45.9 1.1 %collective-permute-start.17 = (f32[8,32,128]{2,1,0:T(8,128)S(1)}, f32[8,32,128]{2,1,0:T(8,128)S(1)}, u32[]{:S(2)}, u32[]{:S(2)}) collective-permute-start(f32[8,32,128]{2,1,0:T(8,128)S(1)} %get-tuple-element.42), channel_id=1, source_target_pairs={{0,4},{1,5},{2,6},{3,7},{4,0},{5,1},{6,2},{7,3},{8,12},{9,13},{10,... | collective-permute-start | bytes 393224 | tf_op jit(solution)/shard_map/ppermute | solution.py:236
  47.0 0.8 %collective-permute-start.18 = (f32[8,32,128]{2,1,0:T(8,128)S(1)}, f32[8,32,128]{2,1,0:T(8,128)S(1)}, u32[]{:S(2)}, u32[]{:S(2)}) collective-permute-start(f32[8,32,128]{2,1,0:T(8,128)S(1)} %get-tuple-element.41), channel_id=1, source_target_pairs={{0,6},{1,7},{2,0},{3,1},{4,2},{5,3},{6,4},{7,5},{8,14},{9,15},{10,... | collective-permute-start | bytes 393224 | tf_op jit(solution)/shard_map/ppermute | solution.py:236
  47.8 0.1 add.59
  47.9 2.5 %collective-permute-start.12 = (f32[8,32,128]{2,1,0:T(8,128)S(1)}, f32[8,32,128]{2,1,0:T(8,128)S(1)}, u32[]{:S(2)}, u32[]{:S(2)}) collective-permute-start(f32[8,32,128]{2,1,0:T(8,128)S(1)} %get-tuple-element.37), channel_id=1, source_target_pairs={{0,2},{1,3},{2,4},{3,5},{4,6},{5,7},{6,0},{7,1},{8,10},{9,11},{10,... | collective-permute-start | bytes 393224 | tf_op jit(solution)/shard_map/ppermute | solution.py:236
  50.5 1.3 %collective-permute-start.13 = (f32[8,32,128]{2,1,0:T(8,128)S(1)}, f32[8,32,128]{2,1,0:T(8,128)S(1)}, u32[]{:S(2)}, u32[]{:S(2)}) collective-permute-start(f32[8,32,128]{2,1,0:T(8,128)S(1)} %get-tuple-element.39), channel_id=1, source_target_pairs={{0,4},{1,5},{2,6},{3,7},{4,0},{5,1},{6,2},{7,3},{8,12},{9,13},{10,... | collective-permute-start | bytes 393224 | tf_op jit(solution)/shard_map/ppermute | solution.py:236
  51.8 1.3 %collective-permute-start.14 = (f32[8,32,128]{2,1,0:T(8,128)S(1)}, f32[8,32,128]{2,1,0:T(8,128)S(1)}, u32[]{:S(2)}, u32[]{:S(2)}) collective-permute-start(f32[8,32,128]{2,1,0:T(8,128)S(1)} %get-tuple-element.38), channel_id=1, source_target_pairs={{0,6},{1,7},{2,0},{3,1},{4,2},{5,3},{6,4},{7,5},{8,14},{9,15},{10,... | collective-permute-start | bytes 393224 | tf_op jit(solution)/shard_map/ppermute | solution.py:236
  53.1 0.7 collective-permute-done.17
  53.8 3.6 %collective-permute-done.18 = f32[8,32,128]{2,1,0:T(8,128)S(1)} collective-permute-done((f32[8,32,128]{2,1,0:T(8,128)S(1)}, f32[8,32,128]{2,1,0:T(8,128)S(1)}, u32[]{:S(2)}, u32[]{:S(2)}) %collective-permute-start.18) | collective-permute-done | bytes 131104 | tf_op jit(solution)/shard_map/ppermute | solution.py:236
  57.5 0.1 collective-permute-start.19
  58.2 1.2 %collective-permute-done.13 = f32[8,32,128]{2,1,0:T(8,128)S(1)} collective-permute-done((f32[8,32,128]{2,1,0:T(8,128)S(1)}, f32[8,32,128]{2,1,0:T(8,128)S(1)}, u32[]{:S(2)}, u32[]{:S(2)}) %collective-permute-start.13) | collective-permute-done | bytes 131104 | tf_op jit(solution)/shard_map/ppermute | solution.py:236
  59.4 1.7 %collective-permute-done.14 = f32[8,32,128]{2,1,0:T(8,128)S(1)} collective-permute-done((f32[8,32,128]{2,1,0:T(8,128)S(1)}, f32[8,32,128]{2,1,0:T(8,128)S(1)}, u32[]{:S(2)}, u32[]{:S(2)}) %collective-permute-start.14) | collective-permute-done | bytes 131104 | tf_op jit(solution)/shard_map/ppermute | solution.py:236
  61.1 4.7 %collective-permute-done.19 = f32[8,32,128]{2,1,0:T(8,128)S(1)} collective-permute-done((f32[8,32,128]{2,1,0:T(8,128)S(1)}, f32[8,32,128]{2,1,0:T(8,128)S(1)}, u32[]{:S(2)}, u32[]{:S(2)}) %collective-permute-start.19) | collective-permute-done | bytes 131104 | tf_op jit(solution)/shard_map/ppermute | solution.py:250
  66.0 0.1 collective-permute-start.20
  66.0 1.3 %collective-permute-start.21 = (f32[8,32,128]{2,1,0:T(8,128)S(1)}, f32[8,32,128]{2,1,0:T(8,128)S(1)}, u32[]{:S(2)}, u32[]{:S(2)}) collective-permute-start(f32[8,32,128]{2,1,0:T(8,128)S(1)} %get-tuple-element.43), channel_id=1, source_target_pairs={{0,4},{1,5},{2,6},{3,7},{4,0},{5,1},{6,2},{7,3},{8,12},{9,13},{10,... | collective-permute-start | bytes 393224 | tf_op jit(solution)/shard_map/ppermute | solution.py:236
  67.3 1.3 %collective-permute-start.22 = (f32[8,32,128]{2,1,0:T(8,128)S(1)}, f32[8,32,128]{2,1,0:T(8,128)S(1)}, u32[]{:S(2)}, u32[]{:S(2)}) collective-permute-start(f32[8,32,128]{2,1,0:T(8,128)S(1)} %get-tuple-element.35), channel_id=1, source_target_pairs={{0,6},{1,7},{2,0},{3,1},{4,2},{5,3},{6,4},{7,5},{8,14},{9,15},{10,... | collective-permute-start | bytes 393224 | tf_op jit(solution)/shard_map/ppermute | solution.py:236
  68.7 2.3 %collective-permute-done.20.refs_1_ = f32[8,32,128]{2,1,0:T(8,128)S(1)} collective-permute-done((f32[8,32,128]{2,1,0:T(8,128)S(1)}, f32[8,32,128]{2,1,0:T(8,128)S(1)}, u32[]{:S(2)}, u32[]{:S(2)}) %collective-permute-start.20) | collective-permute-done | bytes 131104 | tf_op jit(solution)/shard_map/ppermute | solution.py:236
  71.0 2.0 %collective-permute-done.21.refs_2_ = f32[8,32,128]{2,1,0:T(8,128)S(1)} collective-permute-done((f32[8,32,128]{2,1,0:T(8,128)S(1)}, f32[8,32,128]{2,1,0:T(8,128)S(1)}, u32[]{:S(2)}, u32[]{:S(2)}) %collective-permute-start.21) | collective-permute-done | bytes 131104 | tf_op jit(solution)/shard_map/ppermute | solution.py:236
  73.0 1.3 %collective-permute-done.22.refs_3_ = f32[8,32,128]{2,1,0:T(8,128)S(1)} collective-permute-done((f32[8,32,128]{2,1,0:T(8,128)S(1)}, f32[8,32,128]{2,1,0:T(8,128)S(1)}, u32[]{:S(2)}, u32[]{:S(2)}) %collective-permute-start.22) | collective-permute-done | bytes 131104 | tf_op jit(solution)/shard_map/ppermute | solution.py:236
  74.3 0.8 %settle.1 = f32[32,32,128]{2,1,0:T(8,128)} custom-call(s32[1]{0:T(128)} %bitcast.band, f32[8,32,128]{2,1,0:T(8,128)S(1)} %get-tuple-element.45.refs_0_, f32[8,32,128]{2,1,0:T(8,128)S(1)} %collective-permute-done.20.refs_1_, f32[8,32,128]{2,1,0:T(8,128)S(1)} %collective-permute-done.21.refs_2_, f32[8,32,128]{2,1,0:T(8,128)S(1)} %collective-permute-done.22.refs_3_), custom_call_target="tpu_custom_call" | custom-call | tf_op jit(solution)/shard_map/settle/pallas_call | solution.py:346
  (19 shorter events, 0.4 us)
Async XLA Ops:
  0.0 1.0 %copy-start.1 = (f32[32,32,128]{2,1,0:T(8,128)S(1)}, f32[32,32,128]{2,1,0:T(8,128)}, u32[]{:S(2)}) copy-start(f32[32,32,128]{2,1,0:T(8,128)} %potential.1) | copy-start | bytes 1572868
  1.1 12.6 %collective-permute-start.1 = (f32[8,32,128]{2,1,0:T(8,128)S(1)}, f32[8,32,128]{2,1,0:T(8,128)S(1)}, u32[]{:S(2)}, u32[]{:S(2)}) collective-permute-start(f32[8,32,128]{2,1,0:T(8,128)S(1)} %get-tuple-element.22), channel_id=1, source_target_pairs={{0,2},{1,3},{2,4},{3,5},{4,6},{5,7},{6,0},{7,1},{8,10},{9,11},{10,... | collective-permute-start | bytes 393224 | tf_op jit(solution)/shard_map/ppermute | solution.py:236
  3.1 10.5 %collective-permute-start.2 = (f32[8,32,128]{2,1,0:T(8,128)S(1)}, f32[8,32,128]{2,1,0:T(8,128)S(1)}, u32[]{:S(2)}, u32[]{:S(2)}) collective-permute-start(f32[8,32,128]{2,1,0:T(8,128)S(1)} %get-tuple-element.23), channel_id=1, source_target_pairs={{0,4},{1,5},{2,6},{3,7},{4,0},{5,1},{6,2},{7,3},{8,12},{9,13},{10,... | collective-permute-start | bytes 393224 | tf_op jit(solution)/shard_map/ppermute | solution.py:236
  4.0 9.7 %collective-permute-start.3 = (f32[8,32,128]{2,1,0:T(8,128)S(1)}, f32[8,32,128]{2,1,0:T(8,128)S(1)}, u32[]{:S(2)}, u32[]{:S(2)}) collective-permute-start(f32[8,32,128]{2,1,0:T(8,128)S(1)} %get-tuple-element.24), channel_id=1, source_target_pairs={{0,6},{1,7},{2,0},{3,1},{4,2},{5,3},{6,4},{7,5},{8,14},{9,15},{10,... | collective-permute-start | bytes 393224 | tf_op jit(solution)/shard_map/ppermute | solution.py:236
  4.1 9.6 %collective-permute-start = (s32[1,1]{1,0:T(1,128)}, s32[1,1]{1,0:T(1,128)}, u32[]{:S(2)}, u32[]{:S(2)}) collective-permute-start(s32[1,1]{1,0:T(1,128)} %param.10), channel_id=1, source_target_pairs={{0,8},{8,16},{16,24},{24,32},{32,40},{40,48},{48,56},{56,64},{64,7... | collective-permute-start | bytes 20 | tf_op jit(solution)/shard_map/ppermute | solution.py:250
  6.2 1.2 %copy-start = (bf16[1,1,64,64,128]{4,3,2,1,0:T(8,128)(2,1)S(1)}, bf16[1,1,64,64,128]{4,3,2,1,0:T(8,128)(2,1)}, u32[]{:S(2)}) copy-start(bf16[1,1,64,64,128]{4,3,2,1,0:T(8,128)(2,1)} %param.8) | copy-start | bytes 3145732
  7.4 0.9 %copy-start.2 = (bf16[544,128]{1,0:T(8,128)(2,1)S(1)}, bf16[544,128]{1,0:T(8,128)(2,1)}, u32[]{:S(2)}) copy-start(bf16[544,128]{1,0:T(8,128)(2,1)} %constant.59.consts) | copy-start | bytes 417796
  14.3 7.8 %collective-permute-start.4 = (f32[8,32,128]{2,1,0:T(8,128)S(1)}, f32[8,32,128]{2,1,0:T(8,128)S(1)}, u32[]{:S(2)}, u32[]{:S(2)}) collective-permute-start(f32[8,32,128]{2,1,0:T(8,128)S(1)} %get-tuple-element.26), channel_id=1, source_target_pairs={{0,248},{8,0},{16,8},{24,16},{32,24},{40,32},{48,40},{56,48},{64,5... | collective-permute-start | bytes 393224 | tf_op jit(solution)/shard_map/ppermute | solution.py:250
  19.6 8.0 %collective-permute-start.5 = (f32[8,32,128]{2,1,0:T(8,128)S(1)}, f32[8,32,128]{2,1,0:T(8,128)S(1)}, u32[]{:S(2)}, u32[]{:S(2)}) collective-permute-start(f32[8,32,128]{2,1,0:T(8,128)S(1)} %get-tuple-element.25.refs_0_), channel_id=1, source_target_pairs={{0,2},{1,3},{2,4},{3,5},{4,6},{5,7},{6,0},{7,1},{8,10},{9,11},{10,... | collective-permute-start | bytes 393224 | tf_op jit(solution)/shard_map/ppermute | solution.py:236
  21.0 11.9 %collective-permute-start.6 = (f32[8,32,128]{2,1,0:T(8,128)S(1)}, f32[8,32,128]{2,1,0:T(8,128)S(1)}, u32[]{:S(2)}, u32[]{:S(2)}) collective-permute-start(f32[8,32,128]{2,1,0:T(8,128)S(1)} %get-tuple-element.25.refs_0_), channel_id=1, source_target_pairs={{0,6},{1,7},{2,0},{3,1},{4,2},{5,3},{6,4},{7,5},{8,14},{9,15},{10,... | collective-permute-start | bytes 393224 | tf_op jit(solution)/shard_map/ppermute | solution.py:236
  22.2 12.8 %collective-permute-start.9 = (f32[2,8,32,128]{3,2,1,0:T(8,128)S(1)}, f32[2,8,32,128]{3,2,1,0:T(8,128)S(1)}, u32[]{:S(2)}, u32[]{:S(2)}) collective-permute-start(f32[2,8,32,128]{3,2,1,0:T(8,128)S(1)} %stack.2.after), channel_id=1, source_target_pairs={{0,4},{1,5},{2,6},{3,7},{4,0},{5,1},{6,2},{7,3},{8,12},{9,13},{10,... | collective-permute-start | bytes 786440 | tf_op jit(solution)/shard_map/ppermute | solution.py:236
  24.0 9.0 %collective-permute-start.7 = (f32[8,32,128]{2,1,0:T(8,128)S(1)}, f32[8,32,128]{2,1,0:T(8,128)S(1)}, u32[]{:S(2)}, u32[]{:S(2)}) collective-permute-start(f32[8,32,128]{2,1,0:T(8,128)S(1)} %collective-permute-done.4.refs_1_.refs_3_), channel_id=1, source_target_pairs={{0,2},{1,3},{2,4},{3,5},{4,6},{5,7},{6,0},{7,1},{8,10},{9,11},{10,... | collective-permute-start | bytes 393224 | tf_op jit(solution)/shard_map/ppermute | solution.py:236
  25.9 9.1 %collective-permute-start.8 = (f32[8,32,128]{2,1,0:T(8,128)S(1)}, f32[8,32,128]{2,1,0:T(8,128)S(1)}, u32[]{:S(2)}, u32[]{:S(2)}) collective-permute-start(f32[8,32,128]{2,1,0:T(8,128)S(1)} %collective-permute-done.4.refs_1_.refs_3_), channel_id=1, source_target_pairs={{0,6},{1,7},{2,0},{3,1},{4,2},{5,3},{6,4},{7,5},{8,14},{9,15},{10,... | collective-permute-start | bytes 393224 | tf_op jit(solution)/shard_map/ppermute | solution.py:236
  35.1 2.7 %collective-permute-start.10 = (f32[8,8,32,128]{3,2,1,0:T(8,128)S(1)}, f32[8,8,32,128]{3,2,1,0:T(8,128)S(1)}, u32[]{:S(2)}, u32[]{:S(2)}) collective-permute-start(f32[8,8,32,128]{3,2,1,0:T(8,128)S(1)} %stack.3.own), channel_id=1, source_target_pairs={{0,1},{1,0},{2,3},{3,2},{4,5},{5,4},{6,7},{7,6},{8,9},{9,8},{10,11... | collective-permute-start | bytes 3145736 | tf_op jit(solution)/shard_map/ppermute | solution.py:245
  43.1 2.0 %collective-permute-start.15 = (f32[4,8,32,128]{3,2,1,0:T(8,128)S(1)}, f32[4,8,32,128]{3,2,1,0:T(8,128)S(1)}, u32[]{:S(2)}, u32[]{:S(2)}) collective-permute-start(f32[4,8,32,128]{3,2,1,0:T(8,128)S(1)} %get-tuple-element.34), channel_id=1, source_target_pairs={{0,1},{1,0},{2,3},{3,2},{4,5},{5,4},{6,7},{7,6},{8,9},{9,8},{10,11... | collective-permute-start | bytes 1572872 | tf_op jit(solution)/shard_map/ppermute | solution.py:245
  43.3 4.5 %collective-permute-start.11 = (f32[4,8,32,128]{3,2,1,0:T(8,128)S(1)}, f32[4,8,32,128]{3,2,1,0:T(8,128)S(1)}, u32[]{:S(2)}, u32[]{:S(2)}) collective-permute-start(f32[4,8,32,128]{3,2,1,0:T(8,128)S(1)} %get-tuple-element.32), channel_id=1, source_target_pairs={{0,1},{1,0},{2,3},{3,2},{4,5},{5,4},{6,7},{7,6},{8,9},{9,8},{10,11... | collective-permute-start | bytes 1572872 | tf_op jit(solution)/shard_map/ppermute | solution.py:245
  45.2 6.5 %collective-permute-start.16 = (f32[8,32,128]{2,1,0:T(8,128)S(1)}, f32[8,32,128]{2,1,0:T(8,128)S(1)}, u32[]{:S(2)}, u32[]{:S(2)}) collective-permute-start(f32[8,32,128]{2,1,0:T(8,128)S(1)} %get-tuple-element.40), channel_id=1, source_target_pairs={{0,2},{1,3},{2,4},{3,5},{4,6},{5,7},{6,0},{7,1},{8,10},{9,11},{10,... | collective-permute-start | bytes 393224 | tf_op jit(solution)/shard_map/ppermute | solution.py:236
  45.9 7.9 %collective-permute-start.17 = (f32[8,32,128]{2,1,0:T(8,128)S(1)}, f32[8,32,128]{2,1,0:T(8,128)S(1)}, u32[]{:S(2)}, u32[]{:S(2)}) collective-permute-start(f32[8,32,128]{2,1,0:T(8,128)S(1)} %get-tuple-element.42), channel_id=1, source_target_pairs={{0,4},{1,5},{2,6},{3,7},{4,0},{5,1},{6,2},{7,3},{8,12},{9,13},{10,... | collective-permute-start | bytes 393224 | tf_op jit(solution)/shard_map/ppermute | solution.py:236
  47.0 10.4 %collective-permute-start.18 = (f32[8,32,128]{2,1,0:T(8,128)S(1)}, f32[8,32,128]{2,1,0:T(8,128)S(1)}, u32[]{:S(2)}, u32[]{:S(2)}) collective-permute-start(f32[8,32,128]{2,1,0:T(8,128)S(1)} %get-tuple-element.41), channel_id=1, source_target_pairs={{0,6},{1,7},{2,0},{3,1},{4,2},{5,3},{6,4},{7,5},{8,14},{9,15},{10,... | collective-permute-start | bytes 393224 | tf_op jit(solution)/shard_map/ppermute | solution.py:236
  47.9 10.3 %collective-permute-start.12 = (f32[8,32,128]{2,1,0:T(8,128)S(1)}, f32[8,32,128]{2,1,0:T(8,128)S(1)}, u32[]{:S(2)}, u32[]{:S(2)}) collective-permute-start(f32[8,32,128]{2,1,0:T(8,128)S(1)} %get-tuple-element.37), channel_id=1, source_target_pairs={{0,2},{1,3},{2,4},{3,5},{4,6},{5,7},{6,0},{7,1},{8,10},{9,11},{10,... | collective-permute-start | bytes 393224 | tf_op jit(solution)/shard_map/ppermute | solution.py:236
  50.5 9.0 %collective-permute-start.13 = (f32[8,32,128]{2,1,0:T(8,128)S(1)}, f32[8,32,128]{2,1,0:T(8,128)S(1)}, u32[]{:S(2)}, u32[]{:S(2)}) collective-permute-start(f32[8,32,128]{2,1,0:T(8,128)S(1)} %get-tuple-element.39), channel_id=1, source_target_pairs={{0,4},{1,5},{2,6},{3,7},{4,0},{5,1},{6,2},{7,3},{8,12},{9,13},{10,... | collective-permute-start | bytes 393224 | tf_op jit(solution)/shard_map/ppermute | solution.py:236
  51.8 9.4 %collective-permute-start.14 = (f32[8,32,128]{2,1,0:T(8,128)S(1)}, f32[8,32,128]{2,1,0:T(8,128)S(1)}, u32[]{:S(2)}, u32[]{:S(2)}) collective-permute-start(f32[8,32,128]{2,1,0:T(8,128)S(1)} %get-tuple-element.38), channel_id=1, source_target_pairs={{0,6},{1,7},{2,0},{3,1},{4,2},{5,3},{6,4},{7,5},{8,14},{9,15},{10,... | collective-permute-start | bytes 393224 | tf_op jit(solution)/shard_map/ppermute | solution.py:236
  57.5 8.4 %collective-permute-start.19 = (f32[8,32,128]{2,1,0:T(8,128)S(1)}, f32[8,32,128]{2,1,0:T(8,128)S(1)}, u32[]{:S(2)}, u32[]{:S(2)}) collective-permute-start(f32[8,32,128]{2,1,0:T(8,128)S(1)} %fusion.2), channel_id=1, source_target_pairs={{0,8},{8,16},{16,24},{24,32},{32,40},{40,48},{48,56},{56,64},{64,7... | collective-permute-start | bytes 393224 | tf_op jit(solution)/shard_map/ppermute | solution.py:250
  66.0 5.0 %collective-permute-start.20 = (f32[8,32,128]{2,1,0:T(8,128)S(1)}, f32[8,32,128]{2,1,0:T(8,128)S(1)}, u32[]{:S(2)}, u32[]{:S(2)}) collective-permute-start(f32[8,32,128]{2,1,0:T(8,128)S(1)} %get-tuple-element.44), channel_id=1, source_target_pairs={{0,2},{1,3},{2,4},{3,5},{4,6},{5,7},{6,0},{7,1},{8,10},{9,11},{10,... | collective-permute-start | bytes 393224 | tf_op jit(solution)/shard_map/ppermute | solution.py:236
  66.0 7.0 %collective-permute-start.21 = (f32[8,32,128]{2,1,0:T(8,128)S(1)}, f32[8,32,128]{2,1,0:T(8,128)S(1)}, u32[]{:S(2)}, u32[]{:S(2)}) collective-permute-start(f32[8,32,128]{2,1,0:T(8,128)S(1)} %get-tuple-element.43), channel_id=1, source_target_pairs={{0,4},{1,5},{2,6},{3,7},{4,0},{5,1},{6,2},{7,3},{8,12},{9,13},{10,... | collective-permute-start | bytes 393224 | tf_op jit(solution)/shard_map/ppermute | solution.py:236
  67.3 7.0 %collective-permute-start.22 = (f32[8,32,128]{2,1,0:T(8,128)S(1)}, f32[8,32,128]{2,1,0:T(8,128)S(1)}, u32[]{:S(2)}, u32[]{:S(2)}) collective-permute-start(f32[8,32,128]{2,1,0:T(8,128)S(1)} %get-tuple-element.35), channel_id=1, source_target_pairs={{0,6},{1,7},{2,0},{3,1},{4,2},{5,3},{6,4},{7,5},{8,14},{9,15},{10,... | collective-permute-start | bytes 393224 | tf_op jit(solution)/shard_map/ppermute | solution.py:236

commit v8 on v7

--- a/solution.py
+++ b/solution.py
@@ -139,7 +139,7 @@
         out[pl.ds(z + 4, 4)] = upper.reshape(4, width, length)
         return carry
 
-    lax.fori_loop(0, lines // 8, step, 0, unroll=2)
+    lax.fori_loop(0, lines // 8, step, 0, unroll=4)
 
 
 def kinetics(after, states, partly, z_ref, out):
@@ -200,7 +200,7 @@
         return sums
 
     zero = jnp.zeros((8, length), jnp.float32)
-    ss, sh, hh, sw, hw, ww = (total(v) for v in lax.fori_loop(0, width // 16, zz, (zero,) * 6, unroll=2))
+    ss, sh, hh, sw, hw, ww = (total(v) for v in lax.fori_loop(0, width // 16, zz, (zero,) * 6, unroll=4))
     cells = (2 * half * column * length * (1 + double)).astype(jnp.float32)
     first = 1.0 + STEP_LENGTH * sh / (ss + EPSILON)
     tt = first * first * ss - 2.0 * STEP_LENGTH * first * sh + STEP_LENGTH * STEP_LENGTH * hh

time: 75.4 us -> 75.2 us (level)
  no operation moved by 1% of the time
where the time goes in v8:
time: 75.2 us; the launch traced here: 74.8 us
  waiting for transfers between devices  33.3 us (44%)
  starting transfers between devices  26.4 us (35%)
  Pallas kernels  10.2 us (14%)
  local copies, waits for them, and re-layouts  3.22 us (4%)
  between operations  1.48 us (2%)
    ppermute x17, waiting for transfers between devices, to_next_chip(): return lax.ppermute(block, 'band', [(b, (b + 2 * k) % m) for b in range(m)])  20.2 us
    ppermute x17, starting transfers between devices, to_next_chip(): return lax.ppermute(block, 'band', [(b, (b + 2 * k) % m) for b in range(m)])  18.8 us
    ppermute x3, waiting for transfers between devices, to_group(): lax.ppermute(block, 'frag', [(i, (i + distance) % n) for i in range(n)])  8.99 us
    ppermute x3, starting transfers between devices, to_group(): lax.ppermute(block, 'frag', [(i, (i + distance) % n) for i in range(n)])  6.77 us
    pallas_call x1, Pallas kernels, body(): kernel(both_steps, [quarter] * 4, [SMEM] * 2 + [VMEM] * 7, BIG, scratch=[...  5.12 us
    ppermute x3, waiting for transfers between devices, to_other_core(): return lax.ppermute(block, 'band', [(b, b ^ 1) for b in range(2 * CHIPS)])  4.05 us
    unnamed x6, local copies, waits for them, and re-layouts  3.17 us
    pallas_call x1, Pallas kernels, body(): kernel(prepare, [box] * 2 + ops, [SMEM, VMEM, VMEM], MIDDLE)  1.82 us
  transfers between devices with their start and end apart: 23, of which 15 were waited for; matrix products, arithmetic and copies ran while one was open for 0% of the time, Pallas kernels for 5%

profile of v8, /device:TPU:24, one launch (start us, length us, event | category | flops | bytes accessed | tf_op | source)
XLA Modules:
  0.0 74.8 jit_solution(584992602445034688)
XLA Ops:
  0.0 1.0 %copy-done.1 = f32[32,32,128]{2,1,0:T(8,128)S(1)} copy-done((f32[32,32,128]{2,1,0:T(8,128)S(1)}, f32[32,32,128]{2,1,0:T(8,128)}, u32[]{:S(2)}) %copy-start.1) | copy-done | bytes 524312
  1.1 2.0 %collective-permute-start.1 = (f32[8,32,128]{2,1,0:T(8,128)S(1)}, f32[8,32,128]{2,1,0:T(8,128)S(1)}, u32[]{:S(2)}, u32[]{:S(2)}) collective-permute-start(f32[8,32,128]{2,1,0:T(8,128)S(1)} %get-tuple-element.22), channel_id=1, source_target_pairs={{0,2},{1,3},{2,4},{3,5},{4,6},{5,7},{6,0},{7,1},{8,10},{9,11},{10,... | collective-permute-start | bytes 393224 | tf_op jit(solution)/shard_map/ppermute | solution.py:236
  3.1 0.9 %collective-permute-start.2 = (f32[8,32,128]{2,1,0:T(8,128)S(1)}, f32[8,32,128]{2,1,0:T(8,128)S(1)}, u32[]{:S(2)}, u32[]{:S(2)}) collective-permute-start(f32[8,32,128]{2,1,0:T(8,128)S(1)} %get-tuple-element.23), channel_id=1, source_target_pairs={{0,4},{1,5},{2,6},{3,7},{4,0},{5,1},{6,2},{7,3},{8,12},{9,13},{10,... | collective-permute-start | bytes 393224 | tf_op jit(solution)/shard_map/ppermute | solution.py:236
  4.0 0.1 collective-permute-start.3
  4.1 1.4 %collective-permute-start = (s32[1,1]{1,0:T(1,128)}, s32[1,1]{1,0:T(1,128)}, u32[]{:S(2)}, u32[]{:S(2)}) collective-permute-start(s32[1,1]{1,0:T(1,128)} %param.10), channel_id=1, source_target_pairs={{0,8},{8,16},{16,24},{24,32},{32,40},{40,48},{48,56},{56,64},{64,7... | collective-permute-start | bytes 20 | tf_op jit(solution)/shard_map/ppermute | solution.py:250
  6.2 1.2 %copy-done = bf16[1,1,64,64,128]{4,3,2,1,0:T(8,128)(2,1)S(1)} copy-done((bf16[1,1,64,64,128]{4,3,2,1,0:T(8,128)(2,1)S(1)}, bf16[1,1,64,64,128]{4,3,2,1,0:T(8,128)(2,1)}, u32[]{:S(2)}) %copy-start) | copy-done | bytes 1048600
  7.4 0.9 %copy-done.2 = bf16[544,128]{1,0:T(8,128)(2,1)S(1)} copy-done((bf16[544,128]{1,0:T(8,128)(2,1)S(1)}, bf16[544,128]{1,0:T(8,128)(2,1)}, u32[]{:S(2)}) %copy-start.2) | copy-done | bytes 139288
  8.3 1.8 %prepare.1 = (f32[64,64,128]{2,1,0:T(8,128)S(1)}, f32[64,64,128]{2,1,0:T(8,128)S(1)}, bf16[256,256]{1,0:T(8,128)(2,1)S(1)}, bf16[2,256,256]{2,1,0:T(8,128)(2,1)S(1)}, bf16[4,256,256]{2,1,0:T(8,128)(2,1)S(1)}) custom-call(s32[1,1]{1,0:T(1,128)S(6)} %copy.9.code, bf16[64,64,128]{2,1,0:T(8,128)(2,1)S(1)} %bitcast.33, bf16[544,128]{1,0:T(8,128)(2,1)S(1)} %copy-done.2), custom_call_target="tpu_custom_call" | custom-call | tf_op jit(solution)/shard_map/prepare/pallas_call | solution.py:311
  10.1 3.5 %collective-permute-done.code_before = s32[1,1]{1,0:T(1,128)} collective-permute-done((s32[1,1]{1,0:T(1,128)}, s32[1,1]{1,0:T(1,128)}, u32[]{:S(2)}, u32[]{:S(2)}) %collective-permute-start) | collective-permute-done | bytes 36 | tf_op jit(solution)/shard_map/ppermute | solution.py:250
  13.6 0.7 pick.1
  14.3 5.3 %collective-permute-start.4 = (f32[8,32,128]{2,1,0:T(8,128)S(1)}, f32[8,32,128]{2,1,0:T(8,128)S(1)}, u32[]{:S(2)}, u32[]{:S(2)}) collective-permute-start(f32[8,32,128]{2,1,0:T(8,128)S(1)} %get-tuple-element.26), channel_id=1, source_target_pairs={{0,248},{8,0},{16,8},{24,16},{32,24},{40,32},{48,40},{56,48},{64,5... | collective-permute-start | bytes 393224 | tf_op jit(solution)/shard_map/ppermute | solution.py:250
  19.6 1.1 %collective-permute-start.5 = (f32[8,32,128]{2,1,0:T(8,128)S(1)}, f32[8,32,128]{2,1,0:T(8,128)S(1)}, u32[]{:S(2)}, u32[]{:S(2)}) collective-permute-start(f32[8,32,128]{2,1,0:T(8,128)S(1)} %get-tuple-element.25.refs_0_), channel_id=1, source_target_pairs={{0,2},{1,3},{2,4},{3,5},{4,6},{5,7},{6,0},{7,1},{8,10},{9,11},{10,... | collective-permute-start | bytes 393224 | tf_op jit(solution)/shard_map/ppermute | solution.py:236
  20.7 0.9 %collective-permute-start.6 = (f32[8,32,128]{2,1,0:T(8,128)S(1)}, f32[8,32,128]{2,1,0:T(8,128)S(1)}, u32[]{:S(2)}, u32[]{:S(2)}) collective-permute-start(f32[8,32,128]{2,1,0:T(8,128)S(1)} %get-tuple-element.25.refs_0_), channel_id=1, source_target_pairs={{0,6},{1,7},{2,0},{3,1},{4,2},{5,3},{6,4},{7,5},{8,14},{9,15},{10,... | collective-permute-start | bytes 393224 | tf_op jit(solution)/shard_map/ppermute | solution.py:236
  21.6 0.5 collective-permute-done.4.refs_1_.refs_3_
  22.2 1.8 %collective-permute-start.9 = (f32[2,8,32,128]{3,2,1,0:T(8,128)S(1)}, f32[2,8,32,128]{3,2,1,0:T(8,128)S(1)}, u32[]{:S(2)}, u32[]{:S(2)}) collective-permute-start(f32[2,8,32,128]{3,2,1,0:T(8,128)S(1)} %stack.2.after), channel_id=1, source_target_pairs={{0,4},{1,5},{2,6},{3,7},{4,0},{5,1},{6,2},{7,3},{8,12},{9,13},{10,... | collective-permute-start | bytes 786440 | tf_op jit(solution)/shard_map/ppermute | solution.py:236
  24.0 1.9 %collective-permute-start.7 = (f32[8,32,128]{2,1,0:T(8,128)S(1)}, f32[8,32,128]{2,1,0:T(8,128)S(1)}, u32[]{:S(2)}, u32[]{:S(2)}) collective-permute-start(f32[8,32,128]{2,1,0:T(8,128)S(1)} %collective-permute-done.4.refs_1_.refs_3_), channel_id=1, source_target_pairs={{0,2},{1,3},{2,4},{3,5},{4,6},{5,7},{6,0},{7,1},{8,10},{9,11},{10,... | collective-permute-start | bytes 393224 | tf_op jit(solution)/shard_map/ppermute | solution.py:236
  25.9 0.1 collective-permute-start.8
  26.0 1.6 %kinetics.1.after.kinetic = f32[64,64,128]{2,1,0:T(8,128)S(1)} custom-call(f32[2,8,32,128]{3,2,1,0:T(8,128)S(1)} %stack.2.after, f32[64,64,128]{2,1,0:T(8,128)S(1)} %get-tuple-element.20.after.states, f32[64,64,128]{2,1,0:T(8,128)S(1)} %get-tuple-element.27.partly, bf16[4,256,256]{2,1,0:T(8,128)(2,1)S(1)} %get-tuple-element.28.z_ref), custom_call_target="tpu_custom_call" | custom-call | flops 4000000000 | bytes 4000000 | tf_op jit(solution)/shard_map/kinetics/pallas_call | solution.py:327
  27.6 4.6 %collective-permute-done.6.refs_2_ = f32[8,32,128]{2,1,0:T(8,128)S(1)} collective-permute-done((f32[8,32,128]{2,1,0:T(8,128)S(1)}, f32[8,32,128]{2,1,0:T(8,128)S(1)}, u32[]{:S(2)}, u32[]{:S(2)}) %collective-permute-start.6) | collective-permute-done | bytes 131104 | tf_op jit(solution)/shard_map/ppermute | solution.py:236
  32.2 0.8 %collective-permute-done.7.refs_4_ = f32[8,32,128]{2,1,0:T(8,128)S(1)} collective-permute-done((f32[8,32,128]{2,1,0:T(8,128)S(1)}, f32[8,32,128]{2,1,0:T(8,128)S(1)}, u32[]{:S(2)}, u32[]{:S(2)}) %collective-permute-start.7) | collective-permute-done | bytes 131104 | tf_op jit(solution)/shard_map/ppermute | solution.py:236
  33.0 1.8 %collective-permute-done.8.refs_5_ = f32[8,32,128]{2,1,0:T(8,128)S(1)} collective-permute-done((f32[8,32,128]{2,1,0:T(8,128)S(1)}, f32[8,32,128]{2,1,0:T(8,128)S(1)}, u32[]{:S(2)}, u32[]{:S(2)}) %collective-permute-start.8) | collective-permute-done | bytes 131104 | tf_op jit(solution)/shard_map/ppermute | solution.py:236
  34.9 0.3 collective-permute-start.10
  35.2 2.6 %collective-permute-done.10.other = f32[8,8,32,128]{3,2,1,0:T(8,128)S(1)} collective-permute-done((f32[8,8,32,128]{3,2,1,0:T(8,128)S(1)}, f32[8,8,32,128]{3,2,1,0:T(8,128)S(1)}, u32[]{:S(2)}, u32[]{:S(2)}) %collective-permute-start.10) | collective-permute-done | bytes 1048608 | tf_op jit(solution)/shard_map/ppermute | solution.py:245
  37.8 5.1 %both_steps.1 = (f32[4,8,32,128]{3,2,1,0:T(8,128)S(1)}, f32[4,8,32,128]{3,2,1,0:T(8,128)S(1)}, f32[4,8,32,128]{3,2,1,0:T(8,128)S(1)}, f32[4,8,32,128]{3,2,1,0:T(8,128)S(1)}) custom-call(s32[1]{0:T(128)} %bitcast.band, s32[1,1]{1,0:T(1,128)S(6)} %copy.9.code, f32[64,64,128]{2,1,0:T(8,128)S(1)} %get-tuple-element.20.after.states, ...), custom_call_target="tpu_custom_call" | custom-call | tf_op jit(solution)/shard_map/both_steps/pallas_call | solution.py:329
  43.0 0.2 collective-permute-start.15
  43.2 0.4 collective-permute-start.11
  43.6 1.4 %collective-permute-done.15 = f32[4,8,32,128]{3,2,1,0:T(8,128)S(1)} collective-permute-done((f32[4,8,32,128]{3,2,1,0:T(8,128)S(1)}, f32[4,8,32,128]{3,2,1,0:T(8,128)S(1)}, u32[]{:S(2)}, u32[]{:S(2)}) %collective-permute-start.15) | collective-permute-done | bytes 524320 | tf_op jit(solution)/shard_map/ppermute | solution.py:245
  45.0 0.1 add.65
  45.1 0.6 collective-permute-start.16
  45.6 1.4 %collective-permute-start.17 = (f32[8,32,128]{2,1,0:T(8,128)S(1)}, f32[8,32,128]{2,1,0:T(8,128)S(1)}, u32[]{:S(2)}, u32[]{:S(2)}) collective-permute-start(f32[8,32,128]{2,1,0:T(8,128)S(1)} %get-tuple-element.42), channel_id=1, source_target_pairs={{0,4},{1,5},{2,6},{3,7},{4,0},{5,1},{6,2},{7,3},{8,12},{9,13},{10,... | collective-permute-start | bytes 393224 | tf_op jit(solution)/shard_map/ppermute | solution.py:236
  47.0 0.8 %collective-permute-start.18 = (f32[8,32,128]{2,1,0:T(8,128)S(1)}, f32[8,32,128]{2,1,0:T(8,128)S(1)}, u32[]{:S(2)}, u32[]{:S(2)}) collective-permute-start(f32[8,32,128]{2,1,0:T(8,128)S(1)} %get-tuple-element.41), channel_id=1, source_target_pairs={{0,6},{1,7},{2,0},{3,1},{4,2},{5,3},{6,4},{7,5},{8,14},{9,15},{10,... | collective-permute-start | bytes 393224 | tf_op jit(solution)/shard_map/ppermute | solution.py:236
  47.8 0.1 add.59
  47.9 2.5 %collective-permute-start.12 = (f32[8,32,128]{2,1,0:T(8,128)S(1)}, f32[8,32,128]{2,1,0:T(8,128)S(1)}, u32[]{:S(2)}, u32[]{:S(2)}) collective-permute-start(f32[8,32,128]{2,1,0:T(8,128)S(1)} %get-tuple-element.37), channel_id=1, source_target_pairs={{0,2},{1,3},{2,4},{3,5},{4,6},{5,7},{6,0},{7,1},{8,10},{9,11},{10,... | collective-permute-start | bytes 393224 | tf_op jit(solution)/shard_map/ppermute | solution.py:236
  50.5 1.2 %collective-permute-start.13 = (f32[8,32,128]{2,1,0:T(8,128)S(1)}, f32[8,32,128]{2,1,0:T(8,128)S(1)}, u32[]{:S(2)}, u32[]{:S(2)}) collective-permute-start(f32[8,32,128]{2,1,0:T(8,128)S(1)} %get-tuple-element.39), channel_id=1, source_target_pairs={{0,4},{1,5},{2,6},{3,7},{4,0},{5,1},{6,2},{7,3},{8,12},{9,13},{10,... | collective-permute-start | bytes 393224 | tf_op jit(solution)/shard_map/ppermute | solution.py:236
  51.6 1.3 %collective-permute-start.14 = (f32[8,32,128]{2,1,0:T(8,128)S(1)}, f32[8,32,128]{2,1,0:T(8,128)S(1)}, u32[]{:S(2)}, u32[]{:S(2)}) collective-permute-start(f32[8,32,128]{2,1,0:T(8,128)S(1)} %get-tuple-element.38), channel_id=1, source_target_pairs={{0,6},{1,7},{2,0},{3,1},{4,2},{5,3},{6,4},{7,5},{8,14},{9,15},{10,... | collective-permute-start | bytes 393224 | tf_op jit(solution)/shard_map/ppermute | solution.py:236
  52.9 0.4 collective-permute-done.17
  53.4 4.0 %collective-permute-done.18 = f32[8,32,128]{2,1,0:T(8,128)S(1)} collective-permute-done((f32[8,32,128]{2,1,0:T(8,128)S(1)}, f32[8,32,128]{2,1,0:T(8,128)S(1)}, u32[]{:S(2)}, u32[]{:S(2)}) %collective-permute-start.18) | collective-permute-done | bytes 131104 | tf_op jit(solution)/shard_map/ppermute | solution.py:236
  57.4 0.1 collective-permute-start.19
  58.2 0.8 %collective-permute-done.13 = f32[8,32,128]{2,1,0:T(8,128)S(1)} collective-permute-done((f32[8,32,128]{2,1,0:T(8,128)S(1)}, f32[8,32,128]{2,1,0:T(8,128)S(1)}, u32[]{:S(2)}, u32[]{:S(2)}) %collective-permute-start.13) | collective-permute-done | bytes 131104 | tf_op jit(solution)/shard_map/ppermute | solution.py:236
  59.0 1.8 %collective-permute-done.14 = f32[8,32,128]{2,1,0:T(8,128)S(1)} collective-permute-done((f32[8,32,128]{2,1,0:T(8,128)S(1)}, f32[8,32,128]{2,1,0:T(8,128)S(1)}, u32[]{:S(2)}, u32[]{:S(2)}) %collective-permute-start.14) | collective-permute-done | bytes 131104 | tf_op jit(solution)/shard_map/ppermute | solution.py:236
  60.8 5.0 %collective-permute-done.19 = f32[8,32,128]{2,1,0:T(8,128)S(1)} collective-permute-done((f32[8,32,128]{2,1,0:T(8,128)S(1)}, f32[8,32,128]{2,1,0:T(8,128)S(1)}, u32[]{:S(2)}, u32[]{:S(2)}) %collective-permute-start.19) | collective-permute-done | bytes 131104 | tf_op jit(solution)/shard_map/ppermute | solution.py:250
  65.9 0.1 collective-permute-start.20
  66.0 0.9 %collective-permute-start.21 = (f32[8,32,128]{2,1,0:T(8,128)S(1)}, f32[8,32,128]{2,1,0:T(8,128)S(1)}, u32[]{:S(2)}, u32[]{:S(2)}) collective-permute-start(f32[8,32,128]{2,1,0:T(8,128)S(1)} %get-tuple-element.43), channel_id=1, source_target_pairs={{0,4},{1,5},{2,6},{3,7},{4,0},{5,1},{6,2},{7,3},{8,12},{9,13},{10,... | collective-permute-start | bytes 393224 | tf_op jit(solution)/shard_map/ppermute | solution.py:236
  66.9 1.2 %collective-permute-start.22 = (f32[8,32,128]{2,1,0:T(8,128)S(1)}, f32[8,32,128]{2,1,0:T(8,128)S(1)}, u32[]{:S(2)}, u32[]{:S(2)}) collective-permute-start(f32[8,32,128]{2,1,0:T(8,128)S(1)} %get-tuple-element.35), channel_id=1, source_target_pairs={{0,6},{1,7},{2,0},{3,1},{4,2},{5,3},{6,4},{7,5},{8,14},{9,15},{10,... | collective-permute-start | bytes 393224 | tf_op jit(solution)/shard_map/ppermute | solution.py:236
  68.1 2.9 %collective-permute-done.20.refs_1_ = f32[8,32,128]{2,1,0:T(8,128)S(1)} collective-permute-done((f32[8,32,128]{2,1,0:T(8,128)S(1)}, f32[8,32,128]{2,1,0:T(8,128)S(1)}, u32[]{:S(2)}, u32[]{:S(2)}) %collective-permute-start.20) | collective-permute-done | bytes 131104 | tf_op jit(solution)/shard_map/ppermute | solution.py:236
  71.0 1.6 %collective-permute-done.21.refs_2_ = f32[8,32,128]{2,1,0:T(8,128)S(1)} collective-permute-done((f32[8,32,128]{2,1,0:T(8,128)S(1)}, f32[8,32,128]{2,1,0:T(8,128)S(1)}, u32[]{:S(2)}, u32[]{:S(2)}) %collective-permute-start.21) | collective-permute-done | bytes 131104 | tf_op jit(solution)/shard_map/ppermute | solution.py:236
  72.6 1.4 %collective-permute-done.22.refs_3_ = f32[8,32,128]{2,1,0:T(8,128)S(1)} collective-permute-done((f32[8,32,128]{2,1,0:T(8,128)S(1)}, f32[8,32,128]{2,1,0:T(8,128)S(1)}, u32[]{:S(2)}, u32[]{:S(2)}) %collective-permute-start.22) | collective-permute-done | bytes 131104 | tf_op jit(solution)/shard_map/ppermute | solution.py:236
  74.0 0.8 %settle.1 = f32[32,32,128]{2,1,0:T(8,128)} custom-call(s32[1]{0:T(128)} %bitcast.band, f32[8,32,128]{2,1,0:T(8,128)S(1)} %get-tuple-element.45.refs_0_, f32[8,32,128]{2,1,0:T(8,128)S(1)} %collective-permute-done.20.refs_1_, f32[8,32,128]{2,1,0:T(8,128)S(1)} %collective-permute-done.21.refs_2_, f32[8,32,128]{2,1,0:T(8,128)S(1)} %collective-permute-done.22.refs_3_), custom_call_target="tpu_custom_call" | custom-call | tf_op jit(solution)/shard_map/settle/pallas_call | solution.py:346
  (19 shorter events, 0.4 us)
Async XLA Ops:
  0.0 1.0 %copy-start.1 = (f32[32,32,128]{2,1,0:T(8,128)S(1)}, f32[32,32,128]{2,1,0:T(8,128)}, u32[]{:S(2)}) copy-start(f32[32,32,128]{2,1,0:T(8,128)} %potential.1) | copy-start | bytes 1572868
  1.1 12.6 %collective-permute-start.1 = (f32[8,32,128]{2,1,0:T(8,128)S(1)}, f32[8,32,128]{2,1,0:T(8,128)S(1)}, u32[]{:S(2)}, u32[]{:S(2)}) collective-permute-start(f32[8,32,128]{2,1,0:T(8,128)S(1)} %get-tuple-element.22), channel_id=1, source_target_pairs={{0,2},{1,3},{2,4},{3,5},{4,6},{5,7},{6,0},{7,1},{8,10},{9,11},{10,... | collective-permute-start | bytes 393224 | tf_op jit(solution)/shard_map/ppermute | solution.py:236
  3.1 10.5 %collective-permute-start.2 = (f32[8,32,128]{2,1,0:T(8,128)S(1)}, f32[8,32,128]{2,1,0:T(8,128)S(1)}, u32[]{:S(2)}, u32[]{:S(2)}) collective-permute-start(f32[8,32,128]{2,1,0:T(8,128)S(1)} %get-tuple-element.23), channel_id=1, source_target_pairs={{0,4},{1,5},{2,6},{3,7},{4,0},{5,1},{6,2},{7,3},{8,12},{9,13},{10,... | collective-permute-start | bytes 393224 | tf_op jit(solution)/shard_map/ppermute | solution.py:236
  4.0 9.7 %collective-permute-start.3 = (f32[8,32,128]{2,1,0:T(8,128)S(1)}, f32[8,32,128]{2,1,0:T(8,128)S(1)}, u32[]{:S(2)}, u32[]{:S(2)}) collective-permute-start(f32[8,32,128]{2,1,0:T(8,128)S(1)} %get-tuple-element.24), channel_id=1, source_target_pairs={{0,6},{1,7},{2,0},{3,1},{4,2},{5,3},{6,4},{7,5},{8,14},{9,15},{10,... | collective-permute-start | bytes 393224 | tf_op jit(solution)/shard_map/ppermute | solution.py:236
  4.1 9.6 %collective-permute-start = (s32[1,1]{1,0:T(1,128)}, s32[1,1]{1,0:T(1,128)}, u32[]{:S(2)}, u32[]{:S(2)}) collective-permute-start(s32[1,1]{1,0:T(1,128)} %param.10), channel_id=1, source_target_pairs={{0,8},{8,16},{16,24},{24,32},{32,40},{40,48},{48,56},{56,64},{64,7... | collective-permute-start | bytes 20 | tf_op jit(solution)/shard_map/ppermute | solution.py:250
  6.2 1.2 %copy-start = (bf16[1,1,64,64,128]{4,3,2,1,0:T(8,128)(2,1)S(1)}, bf16[1,1,64,64,128]{4,3,2,1,0:T(8,128)(2,1)}, u32[]{:S(2)}) copy-start(bf16[1,1,64,64,128]{4,3,2,1,0:T(8,128)(2,1)} %param.8) | copy-start | bytes 3145732
  7.4 0.9 %copy-start.2 = (bf16[544,128]{1,0:T(8,128)(2,1)S(1)}, bf16[544,128]{1,0:T(8,128)(2,1)}, u32[]{:S(2)}) copy-start(bf16[544,128]{1,0:T(8,128)(2,1)} %constant.59.consts) | copy-start | bytes 417796
  14.3 7.8 %collective-permute-start.4 = (f32[8,32,128]{2,1,0:T(8,128)S(1)}, f32[8,32,128]{2,1,0:T(8,128)S(1)}, u32[]{:S(2)}, u32[]{:S(2)}) collective-permute-start(f32[8,32,128]{2,1,0:T(8,128)S(1)} %get-tuple-element.26), channel_id=1, source_target_pairs={{0,248},{8,0},{16,8},{24,16},{32,24},{40,32},{48,40},{56,48},{64,5... | collective-permute-start | bytes 393224 | tf_op jit(solution)/shard_map/ppermute | solution.py:250
  19.6 8.0 %collective-permute-start.5 = (f32[8,32,128]{2,1,0:T(8,128)S(1)}, f32[8,32,128]{2,1,0:T(8,128)S(1)}, u32[]{:S(2)}, u32[]{:S(2)}) collective-permute-start(f32[8,32,128]{2,1,0:T(8,128)S(1)} %get-tuple-element.25.refs_0_), channel_id=1, source_target_pairs={{0,2},{1,3},{2,4},{3,5},{4,6},{5,7},{6,0},{7,1},{8,10},{9,11},{10,... | collective-permute-start | bytes 393224 | tf_op jit(solution)/shard_map/ppermute | solution.py:236
  20.7 11.5 %collective-permute-start.6 = (f32[8,32,128]{2,1,0:T(8,128)S(1)}, f32[8,32,128]{2,1,0:T(8,128)S(1)}, u32[]{:S(2)}, u32[]{:S(2)}) collective-permute-start(f32[8,32,128]{2,1,0:T(8,128)S(1)} %get-tuple-element.25.refs_0_), channel_id=1, source_target_pairs={{0,6},{1,7},{2,0},{3,1},{4,2},{5,3},{6,4},{7,5},{8,14},{9,15},{10,... | collective-permute-start | bytes 393224 | tf_op jit(solution)/shard_map/ppermute | solution.py:236
  22.2 12.7 %collective-permute-start.9 = (f32[2,8,32,128]{3,2,1,0:T(8,128)S(1)}, f32[2,8,32,128]{3,2,1,0:T(8,128)S(1)}, u32[]{:S(2)}, u32[]{:S(2)}) collective-permute-start(f32[2,8,32,128]{3,2,1,0:T(8,128)S(1)} %stack.2.after), channel_id=1, source_target_pairs={{0,4},{1,5},{2,6},{3,7},{4,0},{5,1},{6,2},{7,3},{8,12},{9,13},{10,... | collective-permute-start | bytes 786440 | tf_op jit(solution)/shard_map/ppermute | solution.py:236
  24.0 9.0 %collective-permute-start.7 = (f32[8,32,128]{2,1,0:T(8,128)S(1)}, f32[8,32,128]{2,1,0:T(8,128)S(1)}, u32[]{:S(2)}, u32[]{:S(2)}) collective-permute-start(f32[8,32,128]{2,1,0:T(8,128)S(1)} %collective-permute-done.4.refs_1_.refs_3_), channel_id=1, source_target_pairs={{0,2},{1,3},{2,4},{3,5},{4,6},{5,7},{6,0},{7,1},{8,10},{9,11},{10,... | collective-permute-start | bytes 393224 | tf_op jit(solution)/shard_map/ppermute | solution.py:236
  25.9 8.9 %collective-permute-start.8 = (f32[8,32,128]{2,1,0:T(8,128)S(1)}, f32[8,32,128]{2,1,0:T(8,128)S(1)}, u32[]{:S(2)}, u32[]{:S(2)}) collective-permute-start(f32[8,32,128]{2,1,0:T(8,128)S(1)} %collective-permute-done.4.refs_1_.refs_3_), channel_id=1, source_target_pairs={{0,6},{1,7},{2,0},{3,1},{4,2},{5,3},{6,4},{7,5},{8,14},{9,15},{10,... | collective-permute-start | bytes 393224 | tf_op jit(solution)/shard_map/ppermute | solution.py:236
  34.9 2.9 %collective-permute-start.10 = (f32[8,8,32,128]{3,2,1,0:T(8,128)S(1)}, f32[8,8,32,128]{3,2,1,0:T(8,128)S(1)}, u32[]{:S(2)}, u32[]{:S(2)}) collective-permute-start(f32[8,8,32,128]{3,2,1,0:T(8,128)S(1)} %stack.3.own), channel_id=1, source_target_pairs={{0,1},{1,0},{2,3},{3,2},{4,5},{5,4},{6,7},{7,6},{8,9},{9,8},{10,11... | collective-permute-start | bytes 3145736 | tf_op jit(solution)/shard_map/ppermute | solution.py:245
  43.0 2.0 %collective-permute-start.15 = (f32[4,8,32,128]{3,2,1,0:T(8,128)S(1)}, f32[4,8,32,128]{3,2,1,0:T(8,128)S(1)}, u32[]{:S(2)}, u32[]{:S(2)}) collective-permute-start(f32[4,8,32,128]{3,2,1,0:T(8,128)S(1)} %get-tuple-element.34), channel_id=1, source_target_pairs={{0,1},{1,0},{2,3},{3,2},{4,5},{5,4},{6,7},{7,6},{8,9},{9,8},{10,11... | collective-permute-start | bytes 1572872 | tf_op jit(solution)/shard_map/ppermute | solution.py:245
  43.2 4.6 %collective-permute-start.11 = (f32[4,8,32,128]{3,2,1,0:T(8,128)S(1)}, f32[4,8,32,128]{3,2,1,0:T(8,128)S(1)}, u32[]{:S(2)}, u32[]{:S(2)}) collective-permute-start(f32[4,8,32,128]{3,2,1,0:T(8,128)S(1)} %get-tuple-element.32), channel_id=1, source_target_pairs={{0,1},{1,0},{2,3},{3,2},{4,5},{5,4},{6,7},{7,6},{8,9},{9,8},{10,11... | collective-permute-start | bytes 1572872 | tf_op jit(solution)/shard_map/ppermute | solution.py:245
  45.1 6.5 %collective-permute-start.16 = (f32[8,32,128]{2,1,0:T(8,128)S(1)}, f32[8,32,128]{2,1,0:T(8,128)S(1)}, u32[]{:S(2)}, u32[]{:S(2)}) collective-permute-start(f32[8,32,128]{2,1,0:T(8,128)S(1)} %get-tuple-element.40), channel_id=1, source_target_pairs={{0,2},{1,3},{2,4},{3,5},{4,6},{5,7},{6,0},{7,1},{8,10},{9,11},{10,... | collective-permute-start | bytes 393224 | tf_op jit(solution)/shard_map/ppermute | solution.py:236
  45.6 7.7 %collective-permute-start.17 = (f32[8,32,128]{2,1,0:T(8,128)S(1)}, f32[8,32,128]{2,1,0:T(8,128)S(1)}, u32[]{:S(2)}, u32[]{:S(2)}) collective-permute-start(f32[8,32,128]{2,1,0:T(8,128)S(1)} %get-tuple-element.42), channel_id=1, source_target_pairs={{0,4},{1,5},{2,6},{3,7},{4,0},{5,1},{6,2},{7,3},{8,12},{9,13},{10,... | collective-permute-start | bytes 393224 | tf_op jit(solution)/shard_map/ppermute | solution.py:236
  47.0 10.4 %collective-permute-start.18 = (f32[8,32,128]{2,1,0:T(8,128)S(1)}, f32[8,32,128]{2,1,0:T(8,128)S(1)}, u32[]{:S(2)}, u32[]{:S(2)}) collective-permute-start(f32[8,32,128]{2,1,0:T(8,128)S(1)} %get-tuple-element.41), channel_id=1, source_target_pairs={{0,6},{1,7},{2,0},{3,1},{4,2},{5,3},{6,4},{7,5},{8,14},{9,15},{10,... | collective-permute-start | bytes 393224 | tf_op jit(solution)/shard_map/ppermute | solution.py:236
  47.9 10.3 %collective-permute-start.12 = (f32[8,32,128]{2,1,0:T(8,128)S(1)}, f32[8,32,128]{2,1,0:T(8,128)S(1)}, u32[]{:S(2)}, u32[]{:S(2)}) collective-permute-start(f32[8,32,128]{2,1,0:T(8,128)S(1)} %get-tuple-element.37), channel_id=1, source_target_pairs={{0,2},{1,3},{2,4},{3,5},{4,6},{5,7},{6,0},{7,1},{8,10},{9,11},{10,... | collective-permute-start | bytes 393224 | tf_op jit(solution)/shard_map/ppermute | solution.py:236
  50.5 8.5 %collective-permute-start.13 = (f32[8,32,128]{2,1,0:T(8,128)S(1)}, f32[8,32,128]{2,1,0:T(8,128)S(1)}, u32[]{:S(2)}, u32[]{:S(2)}) collective-permute-start(f32[8,32,128]{2,1,0:T(8,128)S(1)} %get-tuple-element.39), channel_id=1, source_target_pairs={{0,4},{1,5},{2,6},{3,7},{4,0},{5,1},{6,2},{7,3},{8,12},{9,13},{10,... | collective-permute-start | bytes 393224 | tf_op jit(solution)/shard_map/ppermute | solution.py:236
  51.6 9.2 %collective-permute-start.14 = (f32[8,32,128]{2,1,0:T(8,128)S(1)}, f32[8,32,128]{2,1,0:T(8,128)S(1)}, u32[]{:S(2)}, u32[]{:S(2)}) collective-permute-start(f32[8,32,128]{2,1,0:T(8,128)S(1)} %get-tuple-element.38), channel_id=1, source_target_pairs={{0,6},{1,7},{2,0},{3,1},{4,2},{5,3},{6,4},{7,5},{8,14},{9,15},{10,... | collective-permute-start | bytes 393224 | tf_op jit(solution)/shard_map/ppermute | solution.py:236
  57.4 8.4 %collective-permute-start.19 = (f32[8,32,128]{2,1,0:T(8,128)S(1)}, f32[8,32,128]{2,1,0:T(8,128)S(1)}, u32[]{:S(2)}, u32[]{:S(2)}) collective-permute-start(f32[8,32,128]{2,1,0:T(8,128)S(1)} %fusion.2), channel_id=1, source_target_pairs={{0,8},{8,16},{16,24},{24,32},{32,40},{40,48},{48,56},{56,64},{64,7... | collective-permute-start | bytes 393224 | tf_op jit(solution)/shard_map/ppermute | solution.py:250
  65.9 5.0 %collective-permute-start.20 = (f32[8,32,128]{2,1,0:T(8,128)S(1)}, f32[8,32,128]{2,1,0:T(8,128)S(1)}, u32[]{:S(2)}, u32[]{:S(2)}) collective-permute-start(f32[8,32,128]{2,1,0:T(8,128)S(1)} %get-tuple-element.44), channel_id=1, source_target_pairs={{0,2},{1,3},{2,4},{3,5},{4,6},{5,7},{6,0},{7,1},{8,10},{9,11},{10,... | collective-permute-start | bytes 393224 | tf_op jit(solution)/shard_map/ppermute | solution.py:236
  66.0 6.6 %collective-permute-start.21 = (f32[8,32,128]{2,1,0:T(8,128)S(1)}, f32[8,32,128]{2,1,0:T(8,128)S(1)}, u32[]{:S(2)}, u32[]{:S(2)}) collective-permute-start(f32[8,32,128]{2,1,0:T(8,128)S(1)} %get-tuple-element.43), channel_id=1, source_target_pairs={{0,4},{1,5},{2,6},{3,7},{4,0},{5,1},{6,2},{7,3},{8,12},{9,13},{10,... | collective-permute-start | bytes 393224 | tf_op jit(solution)/shard_map/ppermute | solution.py:236
  66.9 7.1 %collective-permute-start.22 = (f32[8,32,128]{2,1,0:T(8,128)S(1)}, f32[8,32,128]{2,1,0:T(8,128)S(1)}, u32[]{:S(2)}, u32[]{:S(2)}) collective-permute-start(f32[8,32,128]{2,1,0:T(8,128)S(1)} %get-tuple-element.35), channel_id=1, source_target_pairs={{0,6},{1,7},{2,0},{3,1},{4,2},{5,3},{6,4},{7,5},{8,14},{9,15},{10,... | collective-permute-start | bytes 393224 | tf_op jit(solution)/shard_map/ppermute | solution.py:236
